TPU v7x, 32 devices: a whole 2x2x4 slice. The times are simulated.
32 devices in a mesh: grp: 4 (over y, x), shard: 8 (over z, core).
Axes of the slice: x: 2, y: 2, z: 4, core: 2. Of those that a mesh axis runs over, the one named last changes fastest.
Arguments:
- cells: bfloat16 [128, 64, 768], P('shard'), may hold values from -8 to 8
- w_cell: bfloat16 [768, 768], replicated, may hold values from -0.21875 to 0.21875
- w_mix: bfloat16 [768, 768], replicated, may hold values from -0.21875 to 0.21875
- w_pool: bfloat16 [768, 768], replicated, may hold values from -0.21875 to 0.21875
- pairs: int32 [2048, 2], P(('grp', 'shard')), may hold values from 0 to 127, as said below
- counts: int32 [32], P(('grp', 'shard')), may hold values from 1 to 64, 1536 in all
Outputs:
- scores: float32 [2048], P(('grp', 'shard'))
Inputs may be any that keep to these rules, and one draw needn't show every extreme that they name: Column c lies on shard index c // 16. The first column of each pair of reader r lies on shard index r % 8. Among the 64 pairs of one reader at most 16 have their second column on one shard index, and on some shard index exactly 16. The two columns of a pair differ.
All inputs are finite; a program needn't handle non-finite values. No bound on the sum of `counts` on one device may be relied on, other than what follows from the above.
Results may differ from a plain program's by a relative error of at most 0.0014.
Values may be sent and summed in bfloat16 or wider, within the bound.
No kernel may reach another device: no remote copies, remote signals or barrier semaphores. Data moves between devices by JAX's collectives and lax.ppermute only.
A program may use at most 192 MiB of HBM per device.

v0:
```python
import math

import jax
import jax.numpy as jnp
from jax import lax
from jax.sharding import PartitionSpec as P

SOFTMAX_WARMTH = 0.07
EPSILON = 1e-06


def pair_scores(left_block, right_block, w_mix, w_pool):
    score_scale = 1.0 / math.sqrt(left_block.shape[2])
    forward = (
        jnp.einsum("psd,ptd->pst", left_block, right_block, preferred_element_type=jnp.float32)
        * score_scale
    )
    backward = (
        jnp.einsum("ptd,psd->pts", right_block, left_block, preferred_element_type=jnp.float32)
        * score_scale
    )
    attend_left_side = jax.nn.softmax(forward, axis=-1).astype(jnp.bfloat16)
    attend_right = jax.nn.softmax(backward, axis=-1).astype(jnp.bfloat16)
    context_left = jnp.einsum(
        "pst,ptd->psd", attend_left_side, right_block, preferred_element_type=jnp.float32
    )
    context_right = jnp.einsum(
        "pts,psd->ptd", attend_right, left_block, preferred_element_type=jnp.float32
    )
    mixed_left = (left_block.astype(jnp.float32) + context_left).astype(jnp.bfloat16)
    mixed_right = (right_block.astype(jnp.float32) + context_right).astype(jnp.bfloat16)
    pooled_left = jnp.mean(
        jnp.tanh(jnp.einsum("psd,de->pse", mixed_left, w_mix, preferred_element_type=jnp.float32)),
        axis=1,
    ).astype(jnp.bfloat16)
    pooled_right = jnp.mean(
        jnp.tanh(jnp.einsum("psd,de->pse", mixed_right, w_mix, preferred_element_type=jnp.float32)),
        axis=1,
    ).astype(jnp.bfloat16)
    z_left = jnp.dot(pooled_left, w_pool, preferred_element_type=jnp.float32)
    z_right = jnp.dot(pooled_right, w_pool, preferred_element_type=jnp.float32)
    inner_product = jnp.mean(z_left * z_right, axis=-1)
    vector_norms = (jnp.mean(z_left * z_left, axis=-1) + EPSILON) * (
        jnp.mean(z_right * z_right, axis=-1) + EPSILON
    )
    return inner_product / jnp.sqrt(vector_norms) / SOFTMAX_WARMTH


def local(cells, w_cell, w_mix, w_pool, pairs, counts):
    col_dev, samples, features = cells.shape
    pair_dev = pairs.shape[0]
    projected = jnp.dot(
        cells.reshape(col_dev * samples, features), w_cell, preferred_element_type=jnp.float32
    )
    projected = projected.astype(jnp.bfloat16).reshape(col_dev, samples, features)
    left_local = pairs[:, 0] % col_dev
    right_ids = pairs[:, 1]
    position_index = jnp.arange(pair_dev, dtype=jnp.int32)
    live_count = counts[0]
    empty = jnp.zeros((pair_dev, samples, features), jnp.bfloat16)
    piece = lax.all_gather(projected, "shard", axis=0, tiled=True)
    inside = (right_ids >= 0) & (right_ids < piece.shape[0])
    picked = jnp.take(piece, jnp.clip(right_ids, 0, piece.shape[0] - 1), axis=0)
    right_blocks = jnp.where(inside[:, None, None], picked, empty)

    def score_block(block_index, totals):
        first = block_index * 8
        left_sel = lax.dynamic_slice_in_dim(left_local, first, 8, 0)
        left_block = jnp.take(projected, left_sel, axis=0)
        right_block = lax.dynamic_slice_in_dim(right_blocks, first, 8, 0)
        value_rows = pair_scores(left_block, right_block, w_mix, w_pool)
        return lax.dynamic_update_slice_in_dim(totals, value_rows, first, 0)

    block_total = (live_count + 7) // 8
    value_rows = lax.fori_loop(0, block_total, score_block, jnp.zeros((pair_dev,), jnp.float32))
    return jnp.where(position_index < live_count, value_rows, jnp.zeros_like(value_rows))


def solution(mesh):
    placed = (P("shard", None, None), P(), P(), P(), P(("grp", "shard"), None), P(("grp", "shard")))
    return jax.shard_map(
        local, mesh=mesh, in_specs=placed, out_specs=P(("grp", "shard")), check_vma=False
    )
```

profile of v0, /device:TPU:0, one launch (start us, length us, event | category | flops | bytes accessed | tf_op | source)
XLA Modules:
  0.0 280.1 jit_solution(4503959859544326556)
XLA Ops:
  6.5 1.4 copy-done
  7.9 3.8 %convolution_convert_fusion = bf16[1024,768]{1,0:T(8,128)(2,1)} fusion(bf16[1024,768]{1,0:T(8,128)(2,1)S(1)} %bitcast.42, bf16[768,768]{1,0:T(8,128)(2,1)} %param.9), kind=kOutput, calls=%fused_computation.47 | convolution fusion | flops 1208745984 | bytes 4325376 | tf_op jit(solution)/shard_map/dot_general | solution.py:52
  12.5 118.8 %all-gather.2.cloned.1.call-done = bf16[128,64,768]{2,1,0:T(8,128)(2,1)} async-done(((bf16[16,64,768]{2,1,0:T(8,128)(2,1)}), bf16[128,64,768]{2,1,0:T(8,128)(2,1)}) %all-gather.2.cloned.1.call-update) | async-done | bytes 12582928 | tf_op jit(solution)/shard_map/all_gather | solution.py:61
  131.4 8.1 %gather_fusion.1 = bf16[64,64,768]{2,1,0:T(8,128)(2,1)} fusion(bf16[128,64,768]{2,1,0:T(8,128)(2,1)} %all-gather.2.cloned.1.call-done, s32[1024]{0:T(1024)S(1)} %pad_clamp_fusion.1), kind=kCustom, calls=%fused_computation.1 | custom fusion | bytes 12583168 | tf_op jit(solution)/shard_map/jit(_take)/gather | solution.py:63
  139.5 6.3 %select_select_fusion = bf16[64,64,768]{2,1,0:T(8,128)(2,1)} fusion(bf16[64,64,768]{2,1,0:T(8,128)(2,1)} %gather_fusion.1, pred[64]{0:T(512)(128)(4,1)S(1)} %get-tuple-element.71, pred[64]{0:T(512)(128)(4,1)S(1)} %get-tuple-element.70), kind=kLoop, calls=%fused_computation.46 | loop fusion | flops 6291456 | bytes 12583040 | tf_op jit(solution)/shard_map/jit(_where)/select_n | solution.py:64
  145.8 127.0 %while.10 = (s32[]{:T(128)}, f32[64]{0:T(128)S(1)}, s32[]{:T(128)}, s32[64]{0:T(128)S(1)}, bf16[16,64,768]{2,1,0:T(8,128)(2,1)}, /*index=5*/bf16[64,64,768]{2,1,...) while((s32[]{:T(128)}, f32[64]{0:T(128)S(1)}, s32[]{:T(128)}, ...), condition=%wide.region_10.11_spmd, body=%wide.region_0.10_spmd.sunk | while | flops 1433323776 | bytes 15366395 | solution.py:75
  145.9 2.0 gather_fusion
  147.9 1.6 convolution_multiply_fusion.5
  150.3 3.4 %tanh_reduce_fusion.5 = f32[8,768]{1,0:T(8,128)} fusion(bf16[768,768]{1,0:T(8,128)(2,1)} %get-tuple-element.162, bf16[64,64,768]{2,1,0:T(8,128)(2,1)} %get-tuple-element.161, s32[]{:T(128)S(6)} %select_n.78, f32[8,64]{1,0:T(8,128)S(1)} %fusion.71, f32[8,64,64]{1,2,0:T(8,128)} %copy-done.4, bf16[8,64,768]{2,1,0:T(8,128)(2,1)S(1)} %gather_fusion, ...), kind=kOutput, calls=%fused_computation.6.clone.1 | convolution fusion | flops 656370240 | bytes 3303436 | tf_op jit(solution)/shard_map/while/body/psd,de->pse/dot_general | solution.py:33
  153.7 1.5 convolution_multiply_fusion.4
  155.2 0.7 copy-done.3
  156.0 3.4 %tanh_reduce_fusion.4 = f32[8,768]{1,0:T(8,128)} fusion(bf16[768,768]{1,0:T(8,128)(2,1)} %get-tuple-element.162, bf16[64,64,768]{2,1,0:T(8,128)(2,1)} %get-tuple-element.161, s32[]{:T(128)S(6)} %select_n.78, f32[8,64]{1,0:T(8,128)S(1)} %fusion.69, f32[8,64,64]{1,2,0:T(8,128)} %copy-done.3, bf16[8,64,768]{2,1,0:T(8,128)(2,1)S(1)} %gather_fusion, ...), kind=kOutput, calls=%fused_computation.4.clone.1 | convolution fusion | flops 656370240 | bytes 3303436 | tf_op jit(solution)/shard_map/while/body/psd,de->pse/dot_general | solution.py:37
  159.4 1.0 fusion.70
  160.4 1.2 multiply_reduce_fusion.4
  161.8 2.0 gather_fusion
  163.8 1.6 convolution_multiply_fusion.5
  165.4 0.7 copy-done.4
  166.1 3.4 %tanh_reduce_fusion.5 = f32[8,768]{1,0:T(8,128)} fusion(bf16[768,768]{1,0:T(8,128)(2,1)} %get-tuple-element.162, bf16[64,64,768]{2,1,0:T(8,128)(2,1)} %get-tuple-element.161, s32[]{:T(128)S(6)} %select_n.78, f32[8,64]{1,0:T(8,128)S(1)} %fusion.71, f32[8,64,64]{1,2,0:T(8,128)} %copy-done.4, bf16[8,64,768]{2,1,0:T(8,128)(2,1)S(1)} %gather_fusion, ...), kind=kOutput, calls=%fused_computation.6.clone.1 | convolution fusion | flops 656370240 | bytes 3303436 | tf_op jit(solution)/shard_map/while/body/psd,de->pse/dot_general | solution.py:33
  169.5 1.5 convolution_multiply_fusion.4
  171.8 3.4 %tanh_reduce_fusion.4 = f32[8,768]{1,0:T(8,128)} fusion(bf16[768,768]{1,0:T(8,128)(2,1)} %get-tuple-element.162, bf16[64,64,768]{2,1,0:T(8,128)(2,1)} %get-tuple-element.161, s32[]{:T(128)S(6)} %select_n.78, f32[8,64]{1,0:T(8,128)S(1)} %fusion.69, f32[8,64,64]{1,2,0:T(8,128)} %copy-done.3, bf16[8,64,768]{2,1,0:T(8,128)(2,1)S(1)} %gather_fusion, ...), kind=kOutput, calls=%fused_computation.4.clone.1 | convolution fusion | flops 656370240 | bytes 3303436 | tf_op jit(solution)/shard_map/while/body/psd,de->pse/dot_general | solution.py:37
  175.2 1.0 fusion.70
  176.2 1.2 multiply_reduce_fusion.4
  177.6 2.0 gather_fusion
  179.6 1.6 convolution_multiply_fusion.5
  182.0 3.4 %tanh_reduce_fusion.5 = f32[8,768]{1,0:T(8,128)} fusion(bf16[768,768]{1,0:T(8,128)(2,1)} %get-tuple-element.162, bf16[64,64,768]{2,1,0:T(8,128)(2,1)} %get-tuple-element.161, s32[]{:T(128)S(6)} %select_n.78, f32[8,64]{1,0:T(8,128)S(1)} %fusion.71, f32[8,64,64]{1,2,0:T(8,128)} %copy-done.4, bf16[8,64,768]{2,1,0:T(8,128)(2,1)S(1)} %gather_fusion, ...), kind=kOutput, calls=%fused_computation.6.clone.1 | convolution fusion | flops 656370240 | bytes 3303436 | tf_op jit(solution)/shard_map/while/body/psd,de->pse/dot_general | solution.py:33
  185.4 1.5 convolution_multiply_fusion.4
  187.7 3.4 %tanh_reduce_fusion.4 = f32[8,768]{1,0:T(8,128)} fusion(bf16[768,768]{1,0:T(8,128)(2,1)} %get-tuple-element.162, bf16[64,64,768]{2,1,0:T(8,128)(2,1)} %get-tuple-element.161, s32[]{:T(128)S(6)} %select_n.78, f32[8,64]{1,0:T(8,128)S(1)} %fusion.69, f32[8,64,64]{1,2,0:T(8,128)} %copy-done.3, bf16[8,64,768]{2,1,0:T(8,128)(2,1)S(1)} %gather_fusion, ...), kind=kOutput, calls=%fused_computation.4.clone.1 | convolution fusion | flops 656370240 | bytes 3303436 | tf_op jit(solution)/shard_map/while/body/psd,de->pse/dot_general | solution.py:37
  191.1 1.0 fusion.70
  192.1 1.2 multiply_reduce_fusion.4
  193.5 2.0 gather_fusion
  195.5 1.6 convolution_multiply_fusion.5
  197.9 3.4 %tanh_reduce_fusion.5 = f32[8,768]{1,0:T(8,128)} fusion(bf16[768,768]{1,0:T(8,128)(2,1)} %get-tuple-element.162, bf16[64,64,768]{2,1,0:T(8,128)(2,1)} %get-tuple-element.161, s32[]{:T(128)S(6)} %select_n.78, f32[8,64]{1,0:T(8,128)S(1)} %fusion.71, f32[8,64,64]{1,2,0:T(8,128)} %copy-done.4, bf16[8,64,768]{2,1,0:T(8,128)(2,1)S(1)} %gather_fusion, ...), kind=kOutput, calls=%fused_computation.6.clone.1 | convolution fusion | flops 656370240 | bytes 3303436 | tf_op jit(solution)/shard_map/while/body/psd,de->pse/dot_general | solution.py:33
  201.3 1.5 convolution_multiply_fusion.4
  203.6 3.4 %tanh_reduce_fusion.4 = f32[8,768]{1,0:T(8,128)} fusion(bf16[768,768]{1,0:T(8,128)(2,1)} %get-tuple-element.162, bf16[64,64,768]{2,1,0:T(8,128)(2,1)} %get-tuple-element.161, s32[]{:T(128)S(6)} %select_n.78, f32[8,64]{1,0:T(8,128)S(1)} %fusion.69, f32[8,64,64]{1,2,0:T(8,128)} %copy-done.3, bf16[8,64,768]{2,1,0:T(8,128)(2,1)S(1)} %gather_fusion, ...), kind=kOutput, calls=%fused_computation.4.clone.1 | convolution fusion | flops 656370240 | bytes 3303436 | tf_op jit(solution)/shard_map/while/body/psd,de->pse/dot_general | solution.py:37
  207.0 1.0 fusion.70
  208.0 1.2 multiply_reduce_fusion.4
  209.4 2.0 gather_fusion
  211.4 1.6 convolution_multiply_fusion.5
  213.7 3.4 %tanh_reduce_fusion.5 = f32[8,768]{1,0:T(8,128)} fusion(bf16[768,768]{1,0:T(8,128)(2,1)} %get-tuple-element.162, bf16[64,64,768]{2,1,0:T(8,128)(2,1)} %get-tuple-element.161, s32[]{:T(128)S(6)} %select_n.78, f32[8,64]{1,0:T(8,128)S(1)} %fusion.71, f32[8,64,64]{1,2,0:T(8,128)} %copy-done.4, bf16[8,64,768]{2,1,0:T(8,128)(2,1)S(1)} %gather_fusion, ...), kind=kOutput, calls=%fused_computation.6.clone.1 | convolution fusion | flops 656370240 | bytes 3303436 | tf_op jit(solution)/shard_map/while/body/psd,de->pse/dot_general | solution.py:33
  217.1 1.5 convolution_multiply_fusion.4
  219.5 3.4 %tanh_reduce_fusion.4 = f32[8,768]{1,0:T(8,128)} fusion(bf16[768,768]{1,0:T(8,128)(2,1)} %get-tuple-element.162, bf16[64,64,768]{2,1,0:T(8,128)(2,1)} %get-tuple-element.161, s32[]{:T(128)S(6)} %select_n.78, f32[8,64]{1,0:T(8,128)S(1)} %fusion.69, f32[8,64,64]{1,2,0:T(8,128)} %copy-done.3, bf16[8,64,768]{2,1,0:T(8,128)(2,1)S(1)} %gather_fusion, ...), kind=kOutput, calls=%fused_computation.4.clone.1 | convolution fusion | flops 656370240 | bytes 3303436 | tf_op jit(solution)/shard_map/while/body/psd,de->pse/dot_general | solution.py:37
  222.9 1.0 fusion.70
  223.9 1.2 multiply_reduce_fusion.4
  225.2 2.0 gather_fusion
  227.3 1.6 convolution_multiply_fusion.5
  229.6 3.4 %tanh_reduce_fusion.5 = f32[8,768]{1,0:T(8,128)} fusion(bf16[768,768]{1,0:T(8,128)(2,1)} %get-tuple-element.162, bf16[64,64,768]{2,1,0:T(8,128)(2,1)} %get-tuple-element.161, s32[]{:T(128)S(6)} %select_n.78, f32[8,64]{1,0:T(8,128)S(1)} %fusion.71, f32[8,64,64]{1,2,0:T(8,128)} %copy-done.4, bf16[8,64,768]{2,1,0:T(8,128)(2,1)S(1)} %gather_fusion, ...), kind=kOutput, calls=%fused_computation.6.clone.1 | convolution fusion | flops 656370240 | bytes 3303436 | tf_op jit(solution)/shard_map/while/body/psd,de->pse/dot_general | solution.py:33
  233.0 1.5 convolution_multiply_fusion.4
  235.3 3.4 %tanh_reduce_fusion.4 = f32[8,768]{1,0:T(8,128)} fusion(bf16[768,768]{1,0:T(8,128)(2,1)} %get-tuple-element.162, bf16[64,64,768]{2,1,0:T(8,128)(2,1)} %get-tuple-element.161, s32[]{:T(128)S(6)} %select_n.78, f32[8,64]{1,0:T(8,128)S(1)} %fusion.69, f32[8,64,64]{1,2,0:T(8,128)} %copy-done.3, bf16[8,64,768]{2,1,0:T(8,128)(2,1)S(1)} %gather_fusion, ...), kind=kOutput, calls=%fused_computation.4.clone.1 | convolution fusion | flops 656370240 | bytes 3303436 | tf_op jit(solution)/shard_map/while/body/psd,de->pse/dot_general | solution.py:37
  238.7 1.0 fusion.70
  239.7 1.2 multiply_reduce_fusion.4
  241.1 2.0 gather_fusion
  243.1 1.6 convolution_multiply_fusion.5
  245.5 3.4 %tanh_reduce_fusion.5 = f32[8,768]{1,0:T(8,128)} fusion(bf16[768,768]{1,0:T(8,128)(2,1)} %get-tuple-element.162, bf16[64,64,768]{2,1,0:T(8,128)(2,1)} %get-tuple-element.161, s32[]{:T(128)S(6)} %select_n.78, f32[8,64]{1,0:T(8,128)S(1)} %fusion.71, f32[8,64,64]{1,2,0:T(8,128)} %copy-done.4, bf16[8,64,768]{2,1,0:T(8,128)(2,1)S(1)} %gather_fusion, ...), kind=kOutput, calls=%fused_computation.6.clone.1 | convolution fusion | flops 656370240 | bytes 3303436 | tf_op jit(solution)/shard_map/while/body/psd,de->pse/dot_general | solution.py:33
  248.9 1.5 convolution_multiply_fusion.4
  251.2 3.4 %tanh_reduce_fusion.4 = f32[8,768]{1,0:T(8,128)} fusion(bf16[768,768]{1,0:T(8,128)(2,1)} %get-tuple-element.162, bf16[64,64,768]{2,1,0:T(8,128)(2,1)} %get-tuple-element.161, s32[]{:T(128)S(6)} %select_n.78, f32[8,64]{1,0:T(8,128)S(1)} %fusion.69, f32[8,64,64]{1,2,0:T(8,128)} %copy-done.3, bf16[8,64,768]{2,1,0:T(8,128)(2,1)S(1)} %gather_fusion, ...), kind=kOutput, calls=%fused_computation.4.clone.1 | convolution fusion | flops 656370240 | bytes 3303436 | tf_op jit(solution)/shard_map/while/body/psd,de->pse/dot_general | solution.py:37
  254.6 1.0 fusion.70
  255.6 1.2 multiply_reduce_fusion.4
  257.0 2.0 gather_fusion
  259.0 1.6 convolution_multiply_fusion.5
  261.4 3.4 %tanh_reduce_fusion.5 = f32[8,768]{1,0:T(8,128)} fusion(bf16[768,768]{1,0:T(8,128)(2,1)} %get-tuple-element.162, bf16[64,64,768]{2,1,0:T(8,128)(2,1)} %get-tuple-element.161, s32[]{:T(128)S(6)} %select_n.78, f32[8,64]{1,0:T(8,128)S(1)} %fusion.71, f32[8,64,64]{1,2,0:T(8,128)} %copy-done.4, bf16[8,64,768]{2,1,0:T(8,128)(2,1)S(1)} %gather_fusion, ...), kind=kOutput, calls=%fused_computation.6.clone.1 | convolution fusion | flops 656370240 | bytes 3303436 | tf_op jit(solution)/shard_map/while/body/psd,de->pse/dot_general | solution.py:33
  264.8 1.5 convolution_multiply_fusion.4
  267.1 3.4 %tanh_reduce_fusion.4 = f32[8,768]{1,0:T(8,128)} fusion(bf16[768,768]{1,0:T(8,128)(2,1)} %get-tuple-element.162, bf16[64,64,768]{2,1,0:T(8,128)(2,1)} %get-tuple-element.161, s32[]{:T(128)S(6)} %select_n.78, f32[8,64]{1,0:T(8,128)S(1)} %fusion.69, f32[8,64,64]{1,2,0:T(8,128)} %copy-done.3, bf16[8,64,768]{2,1,0:T(8,128)(2,1)S(1)} %gather_fusion, ...), kind=kOutput, calls=%fused_computation.4.clone.1 | convolution fusion | flops 656370240 | bytes 3303436 | tf_op jit(solution)/shard_map/while/body/psd,de->pse/dot_general | solution.py:37
  270.5 1.0 fusion.70
  271.5 1.2 multiply_reduce_fusion.4
  (83 shorter events, 13.0 us)
Async XLA Ops:
  6.5 1.4 copy-start
  6.5 124.8 %all-gather.2.cloned.1.call-start = ((), (), s32[]{:S(2)}) async-start(), calls=%async_computation | async-start | bytes 14155776 | tf_op jit(solution)/shard_map/all_gather | solution.py:61
  11.8 0.7 copy-start.2
  139.5 6.3 %copy-start.1 = (bf16[768,768]{1,0:T(8,128)(2,1)S(1)}, bf16[768,768]{1,0:T(8,128)(2,1)}, u32[]{:S(2)}) copy-start(bf16[768,768]{1,0:T(8,128)(2,1)} %param.11) | copy-start | bytes 3538948
  149.5 0.7 copy-start.4
  155.2 0.7 copy-start.3
  165.3 0.7 copy-start.4
  171.1 0.7 copy-start.3
  181.2 0.7 copy-start.4
  186.9 0.7 copy-start.3
  197.1 0.7 copy-start.4
  202.8 0.7 copy-start.3
  213.0 0.7 copy-start.4
  218.7 0.7 copy-start.3
  228.8 0.7 copy-start.4
  234.6 0.7 copy-start.3
  244.7 0.7 copy-start.4
  250.4 0.7 copy-start.3
  260.6 0.7 copy-start.4
  266.3 0.7 copy-start.3
Sparse Core Ops, SparseCore 0:
  11.9 119.4 all-gather.1
where the time goes:
time: 283 us; the launch traced here: 280 us
  waiting for transfers between devices  119 us (42%)
  matrix products  101 us (36%)
  local copies, waits for them, and re-layouts  36.5 us (13%)
  between operations  14.1 us (5%)
  other arithmetic  9.66 us (3%)
    all_gather x1, waiting for transfers between devices, local(): piece = lax.all_gather(projected, 'shard', axis=0, tiled=True)  119 us
    dot_general x8, matrix products, pair_scores(): jnp.einsum('psd,de->pse', mixed_left, w_mix, preferred_element_type=jnp.f...  27.3 us
    dot_general x8, matrix products, pair_scores(): jnp.einsum('psd,de->pse', mixed_right, w_mix, preferred_element_type=jnp....  27.1 us
    gather x8, local copies, waits for them, and re-layouts, score_block(): left_block = jnp.take(projected, left_sel, axis=0)  16 us
    dot_general x8, matrix products, pair_scores(): jnp.einsum('psd,ptd->pst', left_block, right_block, preferred_element_typ...  12.6 us
    dot_general x8, matrix products, pair_scores(): jnp.einsum('ptd,psd->pts', right_block, left_block, preferred_element_typ...  12.4 us
    while x32, local copies, waits for them, and re-layouts  11 us
    dot_general x8, matrix products, pair_scores(): z_left = jnp.dot(pooled_left, w_pool, preferred_element_type=jnp.float32)  9.41 us
  transfers between devices with their start and end apart: 1, of which 1 were waited for; matrix products, arithmetic and copies ran while one was open for 0% of the time, Pallas kernels for 0%

commit v1 on v0

v1 whole, which is shorter than its diff:
```python
import functools
import math

import jax
import jax.numpy as jnp
from jax import lax
from jax.experimental import pallas as pl
from jax.experimental.pallas import tpu as pltpu
from jax.sharding import PartitionSpec as P

SOFTMAX_WARMTH = 0.07
EPSILON = 1e-06
LANES = 128
UNROLL = 2
F32 = jnp.float32
BF16 = jnp.bfloat16
NT = (((1,), (1,)), ((), ()))
IX, IY, READER, SLOT, VALID, TOTAL = range(6)


def vmem():
    return pl.BlockSpec(memory_space=pltpu.VMEM)


def smem():
    return pl.BlockSpec(memory_space=pltpu.SMEM)


def dot(a, b):
    return jnp.dot(a, b, preferred_element_type=F32)


def dot_nt(a, b):
    return lax.dot_general(a, b, NT, preferred_element_type=F32)


def project_into(rows, w_cell, w_mix, cells_ref, proj_ref, mixed_ref, base):
    columns, samples, width = cells_ref.shape

    def step(i, carry):
        block = cells_ref[pl.ds(i * rows, rows)].reshape(rows * samples, width)
        proj = dot(block, w_cell[...]).astype(BF16)
        proj_ref[pl.ds(base + i * rows, rows)] = proj.reshape(rows, samples, width)
        mixed = dot(proj, w_mix[...]).astype(BF16)
        mixed_ref[pl.ds(base + i * rows, rows)] = mixed.reshape(rows, samples, width)
        return carry

    lax.fori_loop(0, columns // rows, step, 0)


def project_kernel(own_ref, partner_ref, w_cell, w_mix, proj_ref, mixed_ref):
    columns = own_ref.shape[0]
    rows = 4 if columns % 4 == 0 else 1
    project_into(rows, w_cell, w_mix, own_ref, proj_ref, mixed_ref, 0)
    project_into(rows, w_cell, w_mix, partner_ref, proj_ref, mixed_ref, columns)


def attend_pair(left, right, left_mix, right_mix, score_scale):
    samples = left.shape[0]
    both = jnp.concatenate([dot_nt(right, left), dot_nt(left, right)], axis=1) * score_scale
    weights = jnp.exp(both - jnp.max(both, axis=0, keepdims=True))
    weights = weights * (1.0 / jnp.sum(weights, axis=0, keepdims=True))
    attend = jnp.transpose(weights).astype(BF16)
    mixed_left = left_mix.astype(F32) + dot(attend[:samples], right_mix)
    mixed_right = right_mix.astype(F32) + dot(attend[samples:], left_mix)
    inverse = 1.0 / samples
    return (
        jnp.sum(jnp.tanh(mixed_left), axis=0, keepdims=True) * inverse,
        jnp.sum(jnp.tanh(mixed_right), axis=0, keepdims=True) * inverse,
    )


def score_list(index, rows, x, y, pooled, w_pool, score_scale, out_ref):
    x_proj, x_mix = x
    y_proj, y_mix = y
    pool_x, pool_y = pooled
    total = index[TOTAL, 0]
    capacity = index.shape[1]
    block = min(64, capacity)

    def step(i, carry):
        for u in range(UNROLL):
            at = i * UNROLL + u
            ix, iy = index[IX, at], index[IY, at]
            row_x, row_y = attend_pair(x_proj[ix], y_proj[iy], x_mix[ix], y_mix[iy], score_scale)
            pool_x[pl.ds(at, 1)] = row_x
            pool_y[pl.ds(at, 1)] = row_y
        return carry

    lax.fori_loop(0, (total + UNROLL - 1) // UNROLL, step, 0)

    for start in range(0, capacity, block):

        @pl.when(total > start)
        def _():
            both = jnp.concatenate(
                [pool_x[start : start + block], pool_y[start : start + block]], axis=0
            ).astype(BF16)
            z = dot(both, w_pool[...])
            zx, zy = z[:block], z[block:]
            inner = jnp.mean(zx * zy, axis=1, keepdims=True)
            norms = (jnp.mean(zx * zx, axis=1, keepdims=True) + EPSILON) * (
                jnp.mean(zy * zy, axis=1, keepdims=True) + EPSILON
            )
            score = inner / jnp.sqrt(norms) / SOFTMAX_WARMTH
            score = jnp.transpose(jnp.broadcast_to(score, (block, LANES)))[:1]
            here = rows[:, start : start + block]
            live = here[VALID : VALID + 1] > 0
            score = jnp.where(live, score, 0.0)
            readers, slots = out_ref.shape
            of_reader = here[READER : READER + 1] == lax.broadcasted_iota(
                jnp.int32, (readers, block), 0
            )
            of_slot = here[SLOT : SLOT + 1] == lax.broadcasted_iota(jnp.int32, (slots, block), 0)
            out_ref[...] += lax.dot_general(
                jnp.where(of_reader, score, 0.0),
                of_slot.astype(F32),
                NT,
                preferred_element_type=F32,
                precision=lax.Precision.HIGHEST,
            )


def round_kernel(kinds, score_scale, *refs):
    count = len(kinds)
    index, rows = refs[:count], refs[count : 2 * count]
    (remote, w_cell, w_mix, w_pool, proj, mixed, before, out, r_proj, r_mix, pool_x, pool_y) = refs[
        2 * count :
    ]
    out[...] = before[...]
    columns = remote.shape[0]
    project_into(columns if columns <= 4 else 1, w_cell, w_mix, remote, r_proj, r_mix, 0)
    own, far = (proj, mixed), (r_proj, r_mix)
    for kind, index_ref, rows_ref in zip(kinds, index, rows):
        score_list(
            index_ref,
            rows_ref,
            own,
            far if kind == "far" else own,
            (pool_x, pool_y),
            w_pool,
            score_scale,
            out,
        )


def route_kernel(sizes, whose, ids_ref, out_ref):
    lines, shards, per_shard, pair_dev = sizes
    total_columns = shards * per_shard
    chip_columns = 2 * per_shard
    chips = shards // 2
    quarter = per_shard // lines
    line = lax.axis_index("grp")
    shard = lax.axis_index("shard")
    chip, core = shard // 2, lax.rem(shard, 2)
    readers = ids_ref.shape[0]
    ids = ids_ref[...]
    live = ids >= 0
    kept = jnp.maximum(ids, 0)
    a = kept // total_columns
    b = kept - a * total_columns
    b_chip = b // chip_columns
    b_shard = b // per_shard
    a_local = lax.rem(a, per_shard)
    b_local = lax.rem(b, per_shard)
    reader_row = lax.broadcasted_iota(jnp.int32, ids.shape, 0)
    reader_core = lax.rem(reader_row, 2)
    reader_line = lax.rem(line + reader_row // 2, lines)
    reader_shard = chip * 2 + lax.rem(core + reader_core, 2)
    reader_id = reader_line * shards + reader_shard
    slot = lax.broadcasted_iota(jnp.int32, ids.shape, 1)
    a_own = a_local + per_shard * reader_core
    b_own = b_local + per_shard * lax.rem(b_shard + core, 2)
    upper = (
        lax.broadcasted_iota(jnp.int32, (pair_dev, pair_dev), 0)
        < lax.broadcasted_iota(jnp.int32, (pair_dev, pair_dev), 1)
    ).astype(BF16)
    earlier = (
        lax.broadcasted_iota(jnp.int32, (readers, readers), 1)
        < lax.broadcasted_iota(jnp.int32, (readers, readers), 0)
    ).astype(BF16)
    lanes = out_ref.shape[2]
    place = lax.broadcasted_iota(jnp.int32, (lanes, pair_dev), 0)
    field = lax.broadcasted_iota(jnp.int32, (8, pair_dev), 0)
    for number, (kind, offset) in enumerate(whose):
        if kind == "own":
            mine = live & (reader_row == 0) & (b_chip == chip)
            ix, iy = a_own, b_own
        elif kind == "receive":
            source = ring_place(chip, chips, offset)
            mine = live & (b_shard == source * 2 + core) & (b_local // quarter == line)
            ix, iy = a_own, b_local - line * quarter
        else:
            target = ring_place(chip, chips, -offset)
            mine = live & (reader_core == 0) & (b_chip == target) & (a_local // quarter == line)
            ix, iy = b_own, a_local - line * quarter
        taken = mine.astype(BF16)
        before = dot(taken, upper)
        row_total = jnp.sum(mine.astype(F32), axis=1, keepdims=True)
        offsets = dot(earlier, row_total.astype(BF16))
        position = (before + offsets).astype(jnp.int32)
        position = jnp.where(mine, position, -1)
        total = jnp.sum(row_total, axis=0, keepdims=True)
        packed = jnp.zeros((8, lanes), F32)
        for r in range(readers):
            chosen = (place == position[r : r + 1]).astype(BF16)
            fields = jnp.where(field == VALID, 1, 0)
            for which, value in ((IX, ix), (IY, iy), (READER, reader_id), (SLOT, slot)):
                fields = jnp.where(field == which, value[r : r + 1], fields)
            packed = packed + dot_nt(fields.astype(BF16), chosen)
        row = lax.broadcasted_iota(jnp.int32, (8, lanes), 0)
        packed = jnp.where(row == TOTAL, total, packed)
        out_ref[number] = packed.astype(jnp.int32)


def ring_place(chip, chips, offset):
    half = chips // 2
    place = jnp.where(chip < half, 2 * chip, 2 * (chip - half) + 1)
    other = lax.rem(place + offset + 2 * chips, chips)
    return other // 2 + half * lax.rem(other, 2)


def ring_of(chips):
    half = chips // 2
    return [p // 2 + half * (p % 2) for p in range(chips)]


def local(mesh_shape, cells, w_cell, w_mix, w_pool, pairs, counts):
    lines, shards = mesh_shape["grp"], mesh_shape["shard"]
    chips = shards // 2
    per_shard, samples, width = cells.shape
    pair_dev = pairs.shape[0]
    quarter = per_shard // lines
    line = lax.axis_index("grp")
    score_scale = 1.0 / math.sqrt(width)
    ring = ring_of(chips)

    def from_ahead(offset):
        return [
            (2 * ring[(p + offset) % chips] + c, 2 * ring[p] + c) for p in range(chips) for c in (0, 1)
        ]

    offsets = range(1, chips // 2 + 1)
    swap = [(s, s ^ 1) for s in range(shards)]
    partner = lax.ppermute(cells, "shard", swap)
    share = lax.dynamic_slice_in_dim(cells, line * quarter, quarter, 0)
    remote = [lax.ppermute(share, "shard", from_ahead(d)) for d in offsets]

    slot = jnp.arange(pair_dev, dtype=jnp.int32)
    ids = jnp.where(slot < counts[0], pairs[:, 0] * (shards * per_shard) + pairs[:, 1], -1)
    ids = jnp.stack([ids, lax.ppermute(ids, "shard", swap)])
    ids = jnp.concatenate(
        [ids]
        + [
            lax.ppermute(ids, "grp", [((g + k) % lines, g) for g in range(lines)])
            for k in range(1, lines)
        ]
    )

    two_sided = [d for d in offsets if 2 * d != chips]
    whose = (
        [("own", 0)]
        + [("receive", d) for d in offsets]
        + [("send", d) for d in two_sided]
    )
    most = 2 * lines * min(pair_dev, 2 * pair_dev // shards)
    lanes = -(-max(most, pair_dev) // LANES) * LANES
    lists = pl.pallas_call(
        functools.partial(route_kernel, (lines, shards, per_shard, pair_dev), whose),
        out_shape=jax.ShapeDtypeStruct((len(whose), 8, lanes), jnp.int32),
        in_specs=[vmem()],
        out_specs=vmem(),
        name="route",
    )(ids)
    received = {
        d: lax.ppermute(lists[1 + len(offsets) + i], "shard", from_ahead(d))
        for i, d in enumerate(two_sided)
    }

    block = jax.ShapeDtypeStruct((2 * per_shard, samples, width), BF16)
    proj, mixed = pl.pallas_call(
        project_kernel,
        out_shape=(block, block),
        in_specs=[vmem()] * 4,
        out_specs=(vmem(), vmem()),
        compiler_params=pltpu.CompilerParams(vmem_limit_bytes=32 * 2**20),
        name="project",
    )(cells, partner, w_cell, w_mix)

    out = jnp.zeros((lines * shards, pair_dev), F32)
    order = sorted(offsets, reverse=True)
    for d in order:
        use = [lists[d]]
        kinds = ["far"]
        if d in received:
            use.append(received[d])
            kinds.append("far")
        if d == order[0]:
            use.append(lists[0])
            kinds.append("own")
        out = pl.pallas_call(
            functools.partial(round_kernel, tuple(kinds), score_scale),
            out_shape=jax.ShapeDtypeStruct(out.shape, F32),
            in_specs=[smem()] * len(use) + [vmem()] * (len(use) + 7),
            out_specs=vmem(),
            scratch_shapes=[
                pltpu.VMEM((quarter, samples, width), BF16),
                pltpu.VMEM((quarter, samples, width), BF16),
                pltpu.VMEM((lanes, width), F32),
                pltpu.VMEM((lanes, width), F32),
            ],
            compiler_params=pltpu.CompilerParams(vmem_limit_bytes=40 * 2**20),
            name=f"round{d}",
        )(*use, *use, remote[d - 1], w_cell, w_mix, w_pool, proj, mixed, out)

    back = lax.all_to_all(out, ("grp", "shard"), 0, 0, tiled=True)
    return jnp.sum(back, axis=0)


def solution(mesh):
    placed = (P("shard", None, None), P(), P(), P(), P(("grp", "shard"), None), P(("grp", "shard")))
    return jax.shard_map(
        functools.partial(local, dict(mesh.shape)),
        mesh=mesh,
        in_specs=placed,
        out_specs=P(("grp", "shard")),
        check_vma=False,
    )
```

time: 283 us -> 88.3 us (0.31); the launches traced: 280 us -> 89.9 us
  waiting for transfers between devices: 119 us -> 3.68 us
  matrix products: 101 us -> 0 us
  Pallas kernels: 0 us -> 39.6 us
  local copies, waits for them, and re-layouts: 36.5 us -> 6.28 us
  blocking collectives: 0 us -> 26.4 us
  between operations: 14.1 us -> 0.72 us
  starting transfers between devices: 0.01 us -> 11.1 us
  other arithmetic: 9.66 us -> 2.09 us
    all_gather x1 -> x0, waiting for transfers between devices: 119 us -> none  [local(): piece = lax.all_gather(projected, 'shard', axis=0, tiled=True)]
    dot_general x49 -> x0, matrix products: 101 us -> none  [the longest x8 27.3 us: pair_scores(): jnp.einsum('psd,de->pse', mixed_left, w_mix, preferred_element_type=jnp.f...]
    pallas_call x0 -> x4, Pallas kernels: none -> 39.6 us  [the longest x2 29.9 us: local(): pl.pallas_call(functools.partial(round_kernel, tuple(kinds), score_scale)...]
    all_to_all x0 -> x1, blocking collectives: none -> 26.4 us  [local(): back = lax.all_to_all(out, ('grp', 'shard'), 0, 0, tiled=True)]
    gather x9 -> x0, local copies, waits for them, and re-layouts: 24.2 us -> none  [the longest x8 16 us: score_block(): left_block = jnp.take(projected, left_sel, axis=0)]
    ppermute x0 -> x8, starting transfers between devices: none -> 11.1 us  [the longest x3 5.21 us: local(): lax.ppermute(ids, 'grp', [((g + k) % lines, g) for g in range(lines)])]
    while x32 -> x0, local copies, waits for them, and re-layouts: 11 us -> none
    select_n x4 -> x2, other arithmetic: 6.82 us -> 1.52 us  [local(): jnp.where(slot < counts[0], pairs[:, 0] * (shards * per_shard) + pairs[:,...]
  transfers between devices with their start and end apart: 1 -> 8, of which waited for: 1 -> 4; matrix products, arithmetic and copies ran while one was open for 0% -> 4% of each run, Pallas kernels for 0% -> 29%
where the time goes in v1:
time: 88.3 us; the launch traced here: 89.9 us
  Pallas kernels  39.6 us (45%)
  blocking collectives  26.4 us (30%)
  starting transfers between devices  11.1 us (13%)
  local copies, waits for them, and re-layouts  6.28 us (7%)
  waiting for transfers between devices  3.68 us (4%)
  other arithmetic  2.09 us (2%)
    pallas_call x2, Pallas kernels, local(): pl.pallas_call(functools.partial(round_kernel, tuple(kinds), score_scale)...  29.9 us
    all_to_all x1, blocking collectives, local(): back = lax.all_to_all(out, ('grp', 'shard'), 0, 0, tiled=True)  26.4 us
    pallas_call x1, Pallas kernels, local(): pl.pallas_call(project_kernel, out_shape=(block, block), in_specs=[vmem()...  7.27 us
    ppermute x3, starting transfers between devices, local(): lax.ppermute(ids, 'grp', [((g + k) % lines, g) for g in range(lines)])  5.21 us
    ppermute x2, starting transfers between devices, local(): remote = [lax.ppermute(share, 'shard', from_ahead(d)) for d in offsets]  5.11 us
    unnamed x10, local copies, waits for them, and re-layouts  3.96 us
    ppermute x3, waiting for transfers between devices, local(): lax.ppermute(ids, 'grp', [((g + k) % lines, g) for g in range(lines)])  3.29 us
    pallas_call x1, Pallas kernels, local(): pl.pallas_call(functools.partial(route_kernel, (lines, shards, per_shard,...  2.41 us
  transfers between devices with their start and end apart: 8, of which 4 were waited for; matrix products, arithmetic and copies ran while one was open for 4% of the time, Pallas kernels for 29%

profile of v1, /device:TPU:0, one launch (start us, length us, event | category | flops | bytes accessed | tf_op | source)
XLA Modules:
  0.0 89.9 jit_solution(15392475909298605894)
XLA Ops:
  0.0 0.5 collective-permute-start.6
  0.5 1.0 %constant_dynamic-slice_fusion = bf16[4,64,768]{2,1,0:T(8,128)(2,1)S(1)} fusion(bf16[16,64,768]{2,1,0:T(8,128)(2,1)} %own_ref.1, s32[]{:T(128)S(6)} %select_n.18), kind=kLoop, calls=%fused_computation.8 | loop fusion | bytes 786436 | tf_op jit(solution)/shard_map/dynamic_slice | solution.py:246
  1.5 2.6 %collective-permute-start.7 = (bf16[4,64,768]{2,1,0:T(8,128)(2,1)S(1)}, bf16[4,64,768]{2,1,0:T(8,128)(2,1)S(1)}, u32[]{:S(2)}, u32[]{:S(2)}) collective-permute-start(bf16[4,64,768]{2,1,0:T(8,128)(2,1)S(1)} %constant_dynamic-slice_fusion), channel_id=1, source_target_pairs={{2,0},{3,1},{6,4},{7,5},{0,2},{1,3},{4,6},{5,7},{10,8},{11,9},{14,... | collective-permute-start | bytes 1179656 | tf_op jit(solution)/shard_map/ppermute | solution.py:247
  4.1 2.5 %collective-permute-start.5 = (bf16[4,64,768]{2,1,0:T(8,128)(2,1)S(1)}, bf16[4,64,768]{2,1,0:T(8,128)(2,1)S(1)}, u32[]{:S(2)}, u32[]{:S(2)}) collective-permute-start(bf16[4,64,768]{2,1,0:T(8,128)(2,1)S(1)} %constant_dynamic-slice_fusion), channel_id=1, source_target_pairs={{4,0},{5,1},{2,4},{3,5},{6,2},{7,3},{0,6},{1,7},{12,8},{13,9},{10,... | collective-permute-start | bytes 1179656 | tf_op jit(solution)/shard_map/ppermute | solution.py:247
  7.2 0.8 compare_select_fusion
  8.0 0.0 collective-permute-start
  8.0 0.8 compare_select_fusion.1
  8.8 0.4 collective-permute-done
  9.1 2.5 %collective-permute-start.1 = (s32[2,64]{1,0:T(2,128)S(1)}, s32[2,64]{1,0:T(2,128)S(1)}, u32[]{:S(2)}, u32[]{:S(2)}) collective-permute-start(s32[2,64]{1,0:T(2,128)S(1)} %pad_add_fusion), channel_id=1, source_target_pairs={{8,0},{16,8},{24,16},{0,24},{9,1},{17,9},{25,17},{1,25},{10,2},{18... | collective-permute-start | bytes 1544 | tf_op jit(solution)/shard_map/ppermute | solution.py:255
  11.6 0.5 collective-permute-start.2
  12.1 0.8 collective-permute-done.1
  12.9 2.2 %collective-permute-start.3 = (s32[2,64]{1,0:T(2,128)S(1)}, s32[2,64]{1,0:T(2,128)S(1)}, u32[]{:S(2)}, u32[]{:S(2)}) collective-permute-start(s32[2,64]{1,0:T(2,128)S(1)} %pad_add_fusion), channel_id=1, source_target_pairs={{24,0},{0,8},{8,16},{16,24},{25,1},{1,9},{9,17},{17,25},{26,2},{2,... | collective-permute-start | bytes 1544 | tf_op jit(solution)/shard_map/ppermute | solution.py:255
  15.1 0.1 collective-permute-done.2
  15.2 2.4 %collective-permute-done.3 = s32[2,64]{1,0:T(2,128)S(1)} collective-permute-done((s32[2,64]{1,0:T(2,128)S(1)}, s32[2,64]{1,0:T(2,128)S(1)}, u32[]{:S(2)}, u32[]{:S(2)}) %collective-permute-start.3) | collective-permute-done | bytes 544 | tf_op jit(solution)/shard_map/ppermute | solution.py:255
  17.6 0.6 concatenate.4.ids_ref
  18.2 2.4 %route.1 = s32[4,8,128]{2,1,0:T(8,128)} custom-call(s32[8,64]{1,0:T(8,128)} %concatenate.4.ids_ref), custom_call_target="tpu_custom_call" | custom-call | tf_op jit(solution)/shard_map/route/pallas_call | solution.py:268
  20.7 0.7 slice_bitcast_fusion
  21.4 0.3 collective-permute-start.4
  21.7 0.0 collective-permute-done.6.partner_ref
  21.7 0.0 copy-start
  21.7 1.3 %copy-done = bf16[768,768]{1,0:T(8,128)(2,1)S(1)} copy-done((bf16[768,768]{1,0:T(8,128)(2,1)S(1)}, bf16[768,768]{1,0:T(8,128)(2,1)}, u32[]{:S(2)}) %copy-start) | copy-done | bytes 1179672
  23.0 0.0 copy-start.2
  23.0 1.3 %copy-done.2 = bf16[768,768]{1,0:T(8,128)(2,1)S(1)} copy-done((bf16[768,768]{1,0:T(8,128)(2,1)S(1)}, bf16[768,768]{1,0:T(8,128)(2,1)}, u32[]{:S(2)}) %copy-start.2) | copy-done | bytes 1179672
  24.2 0.0 copy-start.4
  24.2 1.4 %copy-done.4 = bf16[16,64,768]{2,1,0:T(8,128)(2,1)S(1)} copy-done((bf16[16,64,768]{2,1,0:T(8,128)(2,1)S(1)}, bf16[16,64,768]{2,1,0:T(8,128)(2,1)}, u32[]{:S(2)}) %copy-start.4) | copy-done | bytes 1572888
  25.6 0.0 copy-start.1
  25.7 0.0 copy-start.3
  25.7 7.3 %project.1 = (bf16[32,64,768]{2,1,0:T(8,128)(2,1)S(1)}, bf16[32,64,768]{2,1,0:T(8,128)(2,1)S(1)}) custom-call(bf16[16,64,768]{2,1,0:T(8,128)(2,1)S(1)} %copy-done.4, bf16[16,64,768]{2,1,0:T(8,128)(2,1)S(1)} %collective-permute-done.6.partner_ref, bf16[768,768]{1,0:T(8,128)(2,1)S(1)} %copy-done, bf16[768,768]{1,0:T(8,128)(2,1)S(1)} %copy-done.2), custom_call_target="tpu_custom_call" | custom-call | tf_op jit(solution)/shard_map/project/pallas_call | solution.py:281
  32.9 0.0 collective-permute-done.7.refs_4_
  32.9 0.0 copy-done.1
  33.0 0.0 copy-done.3
  33.0 15.9 %round2.1.refs_10_ = f32[32,64]{1,0:T(8,128)S(1)} custom-call(s32[8,128]{1,0:T(8,128)S(1)} %get-tuple-element.10.refs_0_.refs_2_, s32[8,128]{1,0:T(8,128)S(1)} %get-tuple-element.9.refs_1_.refs_3_, s32[8,128]{1,0:T(8,128)S(1)} %get-tuple-element.10.refs_0_.refs_2_, s32[8,128]{1,0:T(8,128)S(1)} %get-tuple-element.9.refs_1_.refs_3_, ...), custom_call_target="tpu_custom_call" | custom-call | tf_op jit(solution)/shard_map/round2/pallas_call | solution.py:301
  48.9 0.0 collective-permute-done.4.refs_1_.refs_3_
  48.9 0.0 collective-permute-done.5.refs_4_
  49.0 14.0 %round1.1 = f32[32,64]{1,0:T(8,128)S(1)} custom-call(s32[8,128]{1,0:T(8,128)S(1)} %get-tuple-element.12.refs_0_.refs_2_, s32[8,128]{1,0:T(8,128)S(1)} %collective-permute-done.4.refs_1_.refs_3_, s32[8,128]{1,0:T(8,128)S(1)} %get-tuple-element.12.refs_0_.refs_2_, s32[8,128]{1,0:T(8,128)S(1)} %collective-permute-done.4.refs_1_.refs_3_, ...), custom_call_target="tpu_custom_call" | custom-call | tf_op jit(solution)/shard_map/round1/pallas_call | solution.py:301
  62.9 26.4 %all_to_all.9 = f32[32,1,64]{2,1,0:T(1,128)S(1)} all-to-all(f32[32,1,64]{2,1,0:T(1,128)S(1)} %bitcast.19), channel_id=1, replica_groups=mesh['grp'=4,'shard'=8] {'grp','shard'}, dimensions={0} | all-to-all | bytes 16384 | tf_op jit(solution)/shard_map/all_to_all | solution.py:316
  89.3 0.6 reduce_sum.9
  (2 shorter events, 0.0 us)
Async XLA Ops:
  0.0 21.7 %collective-permute-start.6 = (bf16[16,64,768]{2,1,0:T(8,128)(2,1)}, bf16[16,64,768]{2,1,0:T(8,128)(2,1)S(1)}, u32[]{:S(2)}, u32[]{:S(2)}) collective-permute-start(bf16[16,64,768]{2,1,0:T(8,128)(2,1)} %own_ref.1), channel_id=1, source_target_pairs={{0,1},{1,0},{2,3},{3,2},{4,5},{5,4},{6,7},{7,6},{8,9},{9,8},{10,11... | collective-permute-start | bytes 4718600 | tf_op jit(solution)/shard_map/ppermute | solution.py:245
  1.5 31.5 %collective-permute-start.7 = (bf16[4,64,768]{2,1,0:T(8,128)(2,1)S(1)}, bf16[4,64,768]{2,1,0:T(8,128)(2,1)S(1)}, u32[]{:S(2)}, u32[]{:S(2)}) collective-permute-start(bf16[4,64,768]{2,1,0:T(8,128)(2,1)S(1)} %constant_dynamic-slice_fusion), channel_id=1, source_target_pairs={{2,0},{3,1},{6,4},{7,5},{0,2},{1,3},{4,6},{5,7},{10,8},{11,9},{14,... | collective-permute-start | bytes 1179656 | tf_op jit(solution)/shard_map/ppermute | solution.py:247
  4.1 44.8 %collective-permute-start.5 = (bf16[4,64,768]{2,1,0:T(8,128)(2,1)S(1)}, bf16[4,64,768]{2,1,0:T(8,128)(2,1)S(1)}, u32[]{:S(2)}, u32[]{:S(2)}) collective-permute-start(bf16[4,64,768]{2,1,0:T(8,128)(2,1)S(1)} %constant_dynamic-slice_fusion), channel_id=1, source_target_pairs={{4,0},{5,1},{2,4},{3,5},{6,2},{7,3},{0,6},{1,7},{12,8},{13,9},{10,... | collective-permute-start | bytes 1179656 | tf_op jit(solution)/shard_map/ppermute | solution.py:247
  8.0 1.1 %collective-permute-start = (s32[64]{0:T(128)S(1)}, s32[64]{0:T(128)S(1)}, u32[]{:S(2)}, u32[]{:S(2)}) collective-permute-start(s32[64]{0:T(128)S(1)} %compare_select_fusion), channel_id=1, source_target_pairs={{0,1},{1,0},{2,3},{3,2},{4,5},{5,4},{6,7},{7,6},{8,9},{9,8},{10,11... | collective-permute-start | bytes 776 | tf_op jit(solution)/shard_map/ppermute | solution.py:251
  9.1 3.8 %collective-permute-start.1 = (s32[2,64]{1,0:T(2,128)S(1)}, s32[2,64]{1,0:T(2,128)S(1)}, u32[]{:S(2)}, u32[]{:S(2)}) collective-permute-start(s32[2,64]{1,0:T(2,128)S(1)} %pad_add_fusion), channel_id=1, source_target_pairs={{8,0},{16,8},{24,16},{0,24},{9,1},{17,9},{25,17},{1,25},{10,2},{18... | collective-permute-start | bytes 1544 | tf_op jit(solution)/shard_map/ppermute | solution.py:255
  11.6 3.6 %collective-permute-start.2 = (s32[2,64]{1,0:T(2,128)S(1)}, s32[2,64]{1,0:T(2,128)S(1)}, u32[]{:S(2)}, u32[]{:S(2)}) collective-permute-start(s32[2,64]{1,0:T(2,128)S(1)} %pad_add_fusion), channel_id=1, source_target_pairs={{16,0},{24,8},{0,16},{8,24},{17,1},{25,9},{1,17},{9,25},{18,2},{26... | collective-permute-start | bytes 1544 | tf_op jit(solution)/shard_map/ppermute | solution.py:255
  12.9 4.7 %collective-permute-start.3 = (s32[2,64]{1,0:T(2,128)S(1)}, s32[2,64]{1,0:T(2,128)S(1)}, u32[]{:S(2)}, u32[]{:S(2)}) collective-permute-start(s32[2,64]{1,0:T(2,128)S(1)} %pad_add_fusion), channel_id=1, source_target_pairs={{24,0},{0,8},{8,16},{16,24},{25,1},{1,9},{9,17},{17,25},{26,2},{2,... | collective-permute-start | bytes 1544 | tf_op jit(solution)/shard_map/ppermute | solution.py:255
  21.4 27.6 %collective-permute-start.4 = (s32[8,128]{1,0:T(8,128)S(1)}, s32[8,128]{1,0:T(8,128)S(1)}, u32[]{:S(2)}, u32[]{:S(2)}) collective-permute-start(s32[8,128]{1,0:T(8,128)S(1)} %get-tuple-element.11), channel_id=1, source_target_pairs={{4,0},{5,1},{2,4},{3,5},{6,2},{7,3},{0,6},{1,7},{12,8},{13,9},{10,... | collective-permute-start | bytes 12296 | tf_op jit(solution)/shard_map/ppermute | solution.py:276
  21.7 1.3 %copy-start = (bf16[768,768]{1,0:T(8,128)(2,1)S(1)}, bf16[768,768]{1,0:T(8,128)(2,1)}, u32[]{:S(2)}) copy-start(bf16[768,768]{1,0:T(8,128)(2,1)} %refs_5_.3) | copy-start | bytes 3538948
  23.0 1.3 %copy-start.2 = (bf16[768,768]{1,0:T(8,128)(2,1)S(1)}, bf16[768,768]{1,0:T(8,128)(2,1)}, u32[]{:S(2)}) copy-start(bf16[768,768]{1,0:T(8,128)(2,1)} %refs_6_.3) | copy-start | bytes 3538948
  24.2 1.4 %copy-start.4 = (bf16[16,64,768]{2,1,0:T(8,128)(2,1)S(1)}, bf16[16,64,768]{2,1,0:T(8,128)(2,1)}, u32[]{:S(2)}) copy-start(bf16[16,64,768]{2,1,0:T(8,128)(2,1)} %own_ref.1) | copy-start | bytes 4718596
  25.6 7.3 %copy-start.1 = (bf16[768,768]{1,0:T(8,128)(2,1)S(1)}, bf16[768,768]{1,0:T(8,128)(2,1)}, u32[]{:S(2)}) copy-start(bf16[768,768]{1,0:T(8,128)(2,1)} %refs_5_.3) | copy-start | bytes 3538948
  25.7 7.3 %copy-start.3 = (bf16[768,768]{1,0:T(8,128)(2,1)S(1)}, bf16[768,768]{1,0:T(8,128)(2,1)}, u32[]{:S(2)}) copy-start(bf16[768,768]{1,0:T(8,128)(2,1)} %refs_7_.3) | copy-start | bytes 3538948

commit v2 on v1

v2 whole, which is shorter than its diff:
```python
import functools
import math

import jax
import jax.numpy as jnp
from jax import lax
from jax.experimental import pallas as pl
from jax.experimental.pallas import tpu as pltpu
from jax.sharding import PartitionSpec as P

SOFTMAX_WARMTH = 0.07
EPSILON = 1e-06
LANES = 128
UNROLL = 8
F32 = jnp.float32
BF16 = jnp.bfloat16
NT = (((1,), (1,)), ((), ()))
IX, IY, READER, SLOT, VALID, TOTAL = range(6)


def vmem():
    return pl.BlockSpec(memory_space=pltpu.VMEM)


def hbm():
    return pl.BlockSpec(memory_space=pltpu.HBM)


def in_hbm(x):
    return pltpu.with_memory_space_constraint(x, pltpu.HBM)


def smem():
    return pl.BlockSpec(memory_space=pltpu.SMEM)


def dot(a, b):
    return jnp.dot(a, b, preferred_element_type=F32)


def dot_nt(a, b):
    return lax.dot_general(a, b, NT, preferred_element_type=F32)


def project_columns(block, w_cell, w_mix, proj_ref, mixed_ref, at):
    columns, samples, width = block.shape
    proj = dot(block.reshape(columns * samples, width), w_cell[...]).astype(BF16)
    proj_ref[at : at + columns] = proj.reshape(block.shape)
    mixed_ref[at : at + columns] = dot(proj, w_mix[...]).astype(BF16).reshape(block.shape)


def project_kernel(own, partner, w_cell, w_mix, proj, mixed, own_in, cell_in, mix_in, sems):
    columns = own.shape[0]
    half = columns // 2
    copies = [
        pltpu.make_async_copy(w_cell, cell_in, sems.at[0]),
        pltpu.make_async_copy(own.at[:half], own_in.at[:half], sems.at[1]),
        pltpu.make_async_copy(w_mix, mix_in, sems.at[2]),
        pltpu.make_async_copy(own.at[half:], own_in.at[half:], sems.at[3]),
    ]
    for copy in copies:
        copy.start()
    for copy in copies[:3]:
        copy.wait()
    project_columns(own_in[:half], cell_in, mix_in, proj, mixed, 0)
    copies[3].wait()
    project_columns(own_in[half:], cell_in, mix_in, proj, mixed, half)
    project_columns(partner[...], cell_in, mix_in, proj, mixed, columns)


def attend_pairs(pairs, proj, mixed, score_scale):
    samples = proj.shape[1]
    inverse = 1.0 / samples
    lane = lax.broadcasted_iota(jnp.int32, (samples, 2 * samples), 1)
    weights = []
    for x, y in pairs:
        left, right = proj[x], proj[y]
        both = dot_nt(
            jnp.concatenate([right, left], axis=0), jnp.concatenate([left, right], axis=0)
        )
        weights.append(jnp.where(lane < samples, both[:samples], both[samples:]) * score_scale)
    weights = [jnp.exp(w - jnp.max(w, axis=0, keepdims=True)) for w in weights]
    weights = [w * (1.0 / jnp.sum(w, axis=0, keepdims=True)) for w in weights]
    attend = [jnp.transpose(w).astype(BF16) for w in weights]
    context = [
        (dot(t[:samples], mixed[y]), dot(t[samples:], mixed[x])) for t, (x, y) in zip(attend, pairs)
    ]
    return [
        [
            jnp.sum(jnp.tanh(mixed[c].astype(F32) + add), axis=0, keepdims=True) * inverse
            for c, add in zip(pair, adds)
        ]
        for pair, adds in zip(pairs, context)
    ]


def round_kernel(count, base, score_scale, *refs):
    index, rows = refs[:count], refs[count : 2 * count]
    remote, w_cell, w_mix, w_pool, _, _, *before = refs[2 * count : -6]
    proj, mixed, out, pool_x, pool_y, fields = refs[-6:]
    project_columns(remote[...], w_cell, w_mix, proj, mixed, base)
    lanes = index[0].shape[1]
    starts = [0]
    for ref in index:
        starts.append(starts[-1] + ref[TOTAL, 0])
    total = starts[-1]

    def column(at):
        x, y = index[0][IX, jnp.minimum(at, lanes - 1)], index[0][IY, jnp.minimum(at, lanes - 1)]
        for ref, start in zip(index[1:], starts[1:]):
            here = jnp.clip(at - start, 0, lanes - 1)
            x = jnp.where(at >= start, ref[IX, here], x)
            y = jnp.where(at >= start, ref[IY, here], y)
        return x, y

    def step(i, carry):
        pairs = [column(i * UNROLL + u) for u in range(UNROLL)]
        for u, (row_x, row_y) in enumerate(attend_pairs(pairs, proj, mixed, score_scale)):
            pool_x[pl.ds(i * UNROLL + u, 1)] = row_x
            pool_y[pl.ds(i * UNROLL + u, 1)] = row_y
        return carry

    lax.fori_loop(0, (total + UNROLL - 1) // UNROLL, step, 0)

    capacity = fields.shape[1]
    lane = lax.broadcasted_iota(jnp.int32, fields.shape, 1)
    joined = jnp.zeros(fields.shape, jnp.int32)
    for ref, start in zip(rows, starts):
        wide = [ref[...]] + [jnp.zeros((8, lanes), jnp.int32)] * (count - 1)
        wide = jnp.concatenate(wide, axis=1) if count > 1 else wide[0]
        joined = jnp.where(lane >= start, pltpu.roll(wide, start, 1), joined)
    fields[...] = joined
    out[...] = before[0][...] if before else jnp.zeros(out.shape, F32)
    block = LANES
    readers, slots = out.shape
    for start in range(0, capacity, block):

        @pl.when(total > start)
        def _():
            both = jnp.concatenate(
                [pool_x[start : start + block], pool_y[start : start + block]], axis=0
            ).astype(BF16)
            z = dot(both, w_pool[...])
            zx, zy = z[:block], z[block:]
            inner = jnp.mean(zx * zy, axis=1, keepdims=True)
            norms = (jnp.mean(zx * zx, axis=1, keepdims=True) + EPSILON) * (
                jnp.mean(zy * zy, axis=1, keepdims=True) + EPSILON
            )
            score = inner / jnp.sqrt(norms) / SOFTMAX_WARMTH
            score = jnp.transpose(jnp.broadcast_to(score, (block, block)))[:1]
            here = fields[:, start : start + block]
            live = (here[VALID : VALID + 1] > 0) & (
                lax.broadcasted_iota(jnp.int32, (1, block), 1) < total - start
            )
            score = jnp.where(live, score, 0.0)
            of_reader = here[READER : READER + 1] == lax.broadcasted_iota(
                jnp.int32, (readers, block), 0
            )
            of_slot = here[SLOT : SLOT + 1] == lax.broadcasted_iota(jnp.int32, (slots, block), 0)
            out[...] += lax.dot_general(
                jnp.where(of_reader, score, 0.0),
                of_slot.astype(F32),
                NT,
                preferred_element_type=F32,
                precision=lax.Precision.HIGHEST,
            )


def prepare_kernel(total_columns, quarter, cells, pairs, counts, share, ids, held, sems):
    first = lax.axis_index("grp") * quarter
    copy = pltpu.make_async_copy(cells.at[pl.ds(first, quarter)], share, sems.at[0])
    copy.start()
    copy_pairs = pltpu.make_async_copy(pairs, held, sems.at[1])
    copy_pairs.start()
    copy_pairs.wait()
    slot = lax.broadcasted_iota(jnp.int32, ids.shape, 1)
    ids[...] = jnp.where(slot < counts[0], held[:1] * total_columns + held[1:], -1)
    copy.wait()


def route_kernel(sizes, whose, *refs):
    lines, shards, per_shard, pair_dev = sizes
    ids_refs, out_refs = refs[:lines], refs[lines + 1 :]
    total_columns = shards * per_shard
    chip_columns = 2 * per_shard
    chips = shards // 2
    quarter = per_shard // lines
    line = lax.axis_index("grp")
    shard = lax.axis_index("shard")
    chip, core = shard // 2, lax.rem(shard, 2)
    ids = jnp.concatenate([ref[...] for ref in ids_refs], axis=0)
    live = ids >= 0
    kept = jnp.maximum(ids, 0)
    a = kept // total_columns
    b = kept - a * total_columns
    b_chip = b // chip_columns
    b_shard = b // per_shard
    a_local = lax.rem(a, per_shard)
    b_local = lax.rem(b, per_shard)
    reader_row = lax.broadcasted_iota(jnp.int32, ids.shape, 0)
    reader_id = lax.rem(line + reader_row, lines) * shards + shard
    slot = lax.broadcasted_iota(jnp.int32, ids.shape, 1)
    b_own = b_local + per_shard * lax.rem(b_shard + core, 2)
    upper = (
        lax.broadcasted_iota(jnp.int32, (pair_dev, pair_dev), 0)
        < lax.broadcasted_iota(jnp.int32, (pair_dev, pair_dev), 1)
    ).astype(BF16)
    lanes = out_refs[0].shape[1]
    place = lax.broadcasted_iota(jnp.int32, (lanes, pair_dev), 0)
    field = lax.broadcasted_iota(jnp.int32, (8, pair_dev), 0)
    for (kind, offset), out_ref in zip(whose, out_refs):
        base = chip_columns + (offset - 1) * quarter
        if kind == "own":
            mine = live & (reader_row == 0) & (b_chip == chip)
            ix, iy = a_local, b_own
        elif kind in ("receive", "partner"):
            here = core if kind == "receive" else 1 - core
            source = ring_place(chip, chips, offset)
            mine = live & (b_shard == source * 2 + here) & (b_local // quarter == line)
            ix = a_local if kind == "receive" else a_local + per_shard
            iy = base + b_local - line * quarter
        else:
            target = ring_place(chip, chips, -offset)
            mine = live & (b_chip == target) & (a_local // quarter == line)
            ix, iy = b_own, base + a_local - line * quarter
        before = dot(mine.astype(BF16), upper)
        row_total = jnp.sum(mine.astype(F32), axis=1, keepdims=True)
        total = jnp.zeros((1, 1), F32)
        packed = jnp.zeros((8, lanes), F32)
        for r in range(lines if kind != "own" else 1):
            position = (before[r : r + 1] + total).astype(jnp.int32)
            position = jnp.where(mine[r : r + 1], position, -1)
            total = total + row_total[r : r + 1]
            chosen = (place == position).astype(BF16)
            fields = jnp.where(field == VALID, 1, 0)
            for which, value in ((IX, ix), (IY, iy), (READER, reader_id), (SLOT, slot)):
                fields = jnp.where(field == which, value[r : r + 1], fields)
            packed = packed + dot_nt(fields.astype(BF16), chosen)
        row = lax.broadcasted_iota(jnp.int32, (8, lanes), 0)
        out_ref[...] = jnp.where(row == TOTAL, total, packed).astype(jnp.int32)


def ring_place(chip, chips, offset):
    half = chips // 2
    place = jnp.where(chip < half, 2 * chip, 2 * (chip - half) + 1)
    other = lax.rem(place + offset + 2 * chips, chips)
    return other // 2 + half * lax.rem(other, 2)


def ring_of(chips):
    half = chips // 2
    return [p // 2 + half * (p % 2) for p in range(chips)]


def local(mesh_shape, cells, w_cell, w_mix, w_pool, pairs, counts):
    lines, shards = mesh_shape["grp"], mesh_shape["shard"]
    chips = shards // 2
    per_shard, samples, width = cells.shape
    pair_dev = pairs.shape[0]
    quarter = per_shard // lines
    score_scale = 1.0 / math.sqrt(width)
    ring = ring_of(chips)

    def from_ahead(offset):
        return [
            (2 * ring[(p + offset) % chips] + c, 2 * ring[p] + c) for p in range(chips) for c in (0, 1)
        ]

    offsets = range(1, chips // 2 + 1)
    swap = [(s, s ^ 1) for s in range(shards)]
    partner = lax.ppermute(cells, "shard", swap)
    share, ids = pl.pallas_call(
        functools.partial(prepare_kernel, shards * per_shard, quarter),
        out_shape=(
            jax.ShapeDtypeStruct((quarter, samples, width), BF16),
            jax.ShapeDtypeStruct((1, pair_dev), jnp.int32),
        ),
        in_specs=[hbm(), hbm(), smem()],
        out_specs=(vmem(), vmem()),
        scratch_shapes=[pltpu.VMEM((2, pair_dev), jnp.int32), pltpu.SemaphoreType.DMA((2,))],
        compiler_params=pltpu.CompilerParams(vmem_limit_bytes=4 * 2**20),
        name="prepare",
    )(in_hbm(cells), in_hbm(pairs.T), counts)
    remote = [lax.ppermute(share, "shard", from_ahead(d)) for d in offsets]
    ids = [ids] + [
        lax.ppermute(ids, "grp", [((g + k) % lines, g) for g in range(lines)])
        for k in range(1, lines)
    ]

    store = jax.ShapeDtypeStruct((2 * per_shard + len(offsets) * quarter, samples, width), BF16)
    store_bytes = 2 * math.prod(store.shape)
    weight_bytes = 2 * width * width
    proj, mixed = pl.pallas_call(
        project_kernel,
        out_shape=(store, store),
        in_specs=[hbm(), vmem(), hbm(), hbm()],
        out_specs=(vmem(), vmem()),
        scratch_shapes=[
            pltpu.VMEM(cells.shape, BF16),
            pltpu.VMEM(w_cell.shape, BF16),
            pltpu.VMEM(w_mix.shape, BF16),
            pltpu.SemaphoreType.DMA((4,)),
        ],
        compiler_params=pltpu.CompilerParams(
            vmem_limit_bytes=2 * store_bytes + 2 * weight_bytes + 16 * 2**20
        ),
        name="project",
    )(in_hbm(cells), pltpu.with_memory_space_constraint(partner, pltpu.VMEM), in_hbm(w_cell), in_hbm(w_mix))

    two_sided = [d for d in offsets if 2 * d != chips]
    whose = (
        [("own", 0)]
        + [("receive", d) for d in offsets]
        + [("partner", d) for d in offsets]
        + [("send", d) for d in two_sided]
    )
    most = lines * min(pair_dev, 4 * pair_dev // shards)
    lanes = -(-max(most, pair_dev) // LANES) * LANES
    lists = pl.pallas_call(
        functools.partial(route_kernel, (lines, shards, per_shard, pair_dev), whose),
        out_shape=[jax.ShapeDtypeStruct((8, lanes), jnp.int32)] * len(whose),
        in_specs=[vmem()] * lines + [pl.BlockSpec(memory_space=pl.ANY)],
        out_specs=[vmem()] * len(whose),
        compiler_params=pltpu.CompilerParams(vmem_limit_bytes=4 * 2**20),
        name="route",
    )(*ids, proj)
    lists = dict(zip(whose, lists))
    in_round = {d: [lists["receive", d]] for d in offsets}
    in_round[offsets[-1]].append(lists["own", 0])
    for d in offsets:
        in_round[d].append(lax.ppermute(lists["partner", d], "shard", swap))
    for d in two_sided:
        in_round[d].append(lax.ppermute(lists["send", d], "shard", from_ahead(d)))

    out = []
    for d in reversed(offsets):
        use = in_round[d]
        count = len(use)
        proj, mixed, *out = pl.pallas_call(
            functools.partial(
                round_kernel, count, 2 * per_shard + (d - 1) * quarter, score_scale
            ),
            out_shape=(store, store, jax.ShapeDtypeStruct((lines * shards, pair_dev), F32)),
            in_specs=[smem()] * count + [vmem()] * (count + 6 + len(out)),
            out_specs=(vmem(),) * 3,
            input_output_aliases={2 * count + 4 + i: i for i in range(2 + len(out))},
            scratch_shapes=[
                pltpu.VMEM((count * lanes, width), F32),
                pltpu.VMEM((count * lanes, width), F32),
                pltpu.VMEM((8, count * lanes), jnp.int32),
            ],
            compiler_params=pltpu.CompilerParams(
                vmem_limit_bytes=2 * store_bytes + 4 * weight_bytes + 12 * 2**20
            ),
            name=f"round{d}",
        )(*use, *use, remote[d - 1], w_cell, w_mix, w_pool, proj, mixed, *out)
    (out,) = out

    back = lax.all_to_all(out, ("grp", "shard"), 0, 0, tiled=True)
    return jnp.sum(back, axis=0)


def solution(mesh):
    placed = (P("shard", None, None), P(), P(), P(), P(("grp", "shard"), None), P(("grp", "shard")))
    return jax.shard_map(
        functools.partial(local, dict(mesh.shape)),
        mesh=mesh,
        in_specs=placed,
        out_specs=P(("grp", "shard")),
        check_vma=False,
    )
```

time: 88.3 us -> 51.1 us (0.58); the launches traced: 89.9 us -> 50.3 us
  Pallas kernels: 39.6 us -> 22.9 us
  blocking collectives: 26.4 us -> 13.2 us
  local copies, waits for them, and re-layouts: 6.28 us -> 0.01 us
  waiting for transfers between devices: 3.68 us -> 2.05 us
  other arithmetic: 2.09 us -> 0.56 us
    pallas_call x3 -> x4, Pallas kernels: 37.2 us -> 22 us  [the longest x2 13.6 us: local(): pl.pallas_call(functools.partial(round_kernel, count, 2 * per_shard + (d...]
    all_to_all x1, blocking collectives: 26.4 us -> 13.2 us  [local(): back = lax.all_to_all(out, ('grp', 'shard'), 0, 0, tiled=True)]
    unnamed x10 -> x6, local copies, waits for them, and re-layouts: 3.96 us -> 0.01 us
    ppermute x3, waiting for transfers between devices: 3.29 us -> 0.01 us  [local(): lax.ppermute(ids, 'grp', [((g + k) % lines, g) for g in range(lines)])]
    ppermute x2, waiting for transfers between devices: 0.03 us -> 2.01 us  [local(): remote = [lax.ppermute(share, 'shard', from_ahead(d)) for d in offsets]]
    pallas_call x1, Pallas kernels: 2.41 us -> 0.89 us  [local(): pl.pallas_call(functools.partial(route_kernel, (lines, shards, per_shard,...]
    select_n x2 -> x0, other arithmetic: 1.52 us -> none  [local(): jnp.where(slot < counts[0], pairs[:, 0] * (shards * per_shard) + pairs[:,...]
    dynamic_slice x1 -> x0, local copies, waits for them, and re-layouts: 1.02 us -> none  [local(): share = lax.dynamic_slice_in_dim(cells, line * quarter, quarter, 0)]
  transfers between devices with their start and end apart: 8 -> 9, of which waited for: 4 -> 1; matrix products, arithmetic and copies ran while one was open for 4% -> 0% of each run, Pallas kernels for 29% -> 33%
where the time goes in v2:
time: 51.1 us; the launch traced here: 50.3 us
  Pallas kernels  22.9 us (45%)
  blocking collectives  13.2 us (26%)
  starting transfers between devices  10.9 us (21%)
  waiting for transfers between devices  2.05 us (4%)
  between operations  0.74 us (1%)
  other arithmetic  0.56 us (1%)
    pallas_call x2, Pallas kernels, local(): pl.pallas_call(functools.partial(round_kernel, count, 2 * per_shard + (d...  13.6 us
    all_to_all x1, blocking collectives, local(): back = lax.all_to_all(out, ('grp', 'shard'), 0, 0, tiled=True)  13.2 us
    pallas_call x1, Pallas kernels, local(): pl.pallas_call(project_kernel, out_shape=(store, store), in_specs=[hbm(),...  7.36 us
    ppermute x2, starting transfers between devices, local(): remote = [lax.ppermute(share, 'shard', from_ahead(d)) for d in offsets]  5.11 us
    ppermute x3, starting transfers between devices, local(): lax.ppermute(ids, 'grp', [((g + k) % lines, g) for g in range(lines)])  4.44 us
    ppermute x2, waiting for transfers between devices, local(): remote = [lax.ppermute(share, 'shard', from_ahead(d)) for d in offsets]  2.01 us
    pallas_call x1, Pallas kernels, local(): pl.pallas_call(functools.partial(prepare_kernel, shards * per_shard, quar...  1.02 us
  transfers between devices with their start and end apart: 9, of which 1 were waited for; matrix products, arithmetic and copies ran while one was open for 0% of the time, Pallas kernels for 33%

profile of v2, /device:TPU:0, one launch (start us, length us, event | category | flops | bytes accessed | tf_op | source)
XLA Modules:
  0.0 50.3 jit_solution(2594865016950141691)
XLA Ops:
  0.0 0.5 collective-permute-start.3
  1.1 1.0 %prepare.1 = (bf16[4,64,768]{2,1,0:T(8,128)(2,1)S(1)}, s32[1,64]{1,0:T(1,128)S(1)}) custom-call(bf16[16,64,768]{2,1,0:T(8,128)(2,1)} %own.1, s32[2,64]{1,0:T(2,128)} %bitcast.5, s32[1]{0:T(128)S(6)} %copy.18.counts), custom_call_target="tpu_custom_call" | custom-call | tf_op jit(solution)/shard_map/prepare/pallas_call | solution.py:272
  2.1 2.6 %collective-permute-start.8 = (bf16[4,64,768]{2,1,0:T(8,128)(2,1)S(1)}, bf16[4,64,768]{2,1,0:T(8,128)(2,1)S(1)}, u32[]{:S(2)}, u32[]{:S(2)}) collective-permute-start(bf16[4,64,768]{2,1,0:T(8,128)(2,1)S(1)} %get-tuple-element.24), channel_id=1, source_target_pairs={{2,0},{3,1},{6,4},{7,5},{0,2},{1,3},{4,6},{5,7},{10,8},{11,9},{14,... | collective-permute-start | bytes 1179656 | tf_op jit(solution)/shard_map/ppermute | solution.py:284
  4.8 2.5 %collective-permute-start.6 = (bf16[4,64,768]{2,1,0:T(8,128)(2,1)S(1)}, bf16[4,64,768]{2,1,0:T(8,128)(2,1)S(1)}, u32[]{:S(2)}, u32[]{:S(2)}) collective-permute-start(bf16[4,64,768]{2,1,0:T(8,128)(2,1)S(1)} %get-tuple-element.24), channel_id=1, source_target_pairs={{4,0},{5,1},{2,4},{3,5},{6,2},{7,3},{0,6},{1,7},{12,8},{13,9},{10,... | collective-permute-start | bytes 1179656 | tf_op jit(solution)/shard_map/ppermute | solution.py:284
  7.3 0.0 copy-start
  7.3 0.0 copy-start.1
  7.3 0.0 copy-start.2
  7.3 1.5 %collective-permute-start.2 = (s32[1,64]{1,0:T(1,128)S(1)}, s32[1,64]{1,0:T(1,128)S(1)}, u32[]{:S(2)}, u32[]{:S(2)}) collective-permute-start(s32[1,64]{1,0:T(1,128)S(1)} %get-tuple-element.19.refs_0_), channel_id=1, source_target_pairs={{24,0},{0,8},{8,16},{16,24},{25,1},{1,9},{9,17},{17,25},{26,2},{2,... | collective-permute-start | bytes 776 | tf_op jit(solution)/shard_map/ppermute | solution.py:286
  8.8 1.5 %collective-permute-start.1 = (s32[1,64]{1,0:T(1,128)S(1)}, s32[1,64]{1,0:T(1,128)S(1)}, u32[]{:S(2)}, u32[]{:S(2)}) collective-permute-start(s32[1,64]{1,0:T(1,128)S(1)} %get-tuple-element.19.refs_0_), channel_id=1, source_target_pairs={{16,0},{24,8},{0,16},{8,24},{17,1},{25,9},{1,17},{9,25},{18,2},{26... | collective-permute-start | bytes 776 | tf_op jit(solution)/shard_map/ppermute | solution.py:286
  10.3 0.0 collective-permute-done.3.partner
  10.3 1.4 %collective-permute-start = (s32[1,64]{1,0:T(1,128)S(1)}, s32[1,64]{1,0:T(1,128)S(1)}, u32[]{:S(2)}, u32[]{:S(2)}) collective-permute-start(s32[1,64]{1,0:T(1,128)S(1)} %get-tuple-element.19.refs_0_), channel_id=1, source_target_pairs={{8,0},{16,8},{24,16},{0,24},{9,1},{17,9},{25,17},{1,25},{10,2},{18... | collective-permute-start | bytes 776 | tf_op jit(solution)/shard_map/ppermute | solution.py:286
  11.7 7.4 %project.1 = (bf16[40,64,768]{2,1,0:T(8,128)(2,1)S(1)}, bf16[40,64,768]{2,1,0:T(8,128)(2,1)S(1)}) custom-call(bf16[16,64,768]{2,1,0:T(8,128)(2,1)} %own.1, bf16[16,64,768]{2,1,0:T(8,128)(2,1)S(1)} %collective-permute-done.3.partner, bf16[768,768]{1,0:T(8,128)(2,1)} %refs_7_.3, bf16[768,768]{1,0:T(8,128)(2,1)} %refs_8_.3), custom_call_target="tpu_custom_call" | custom-call | tf_op jit(solution)/shard_map/project/pallas_call | solution.py:293
  19.1 0.0 collective-permute-done.2.refs_3_
  19.1 0.0 collective-permute-done.1.refs_2_
  19.1 0.0 collective-permute-done.refs_1_
  19.1 0.9 %route.1 = (s32[8,128]{1,0:T(8,128)S(1)}, s32[8,128]{1,0:T(8,128)S(1)}, s32[8,128]{1,0:T(8,128)S(1)}, s32[8,128]{1,0:T(8,128)S(1)}, s32[8,128]{1,0:T(8,128)S(1)}, /*index=5*/s32[8,128]{1,0:T(8,128)S(1)}) custom-call(s32[1,64]{1,0:T(1,128)S(1)} %get-tuple-element.19.refs_0_, s32[1,64]{1,0:T(1,128)S(1)} %collective-permute-done.refs_1_, ...), custom_call_target="tpu_custom_call" | custom-call | tf_op jit(solution)/shard_map/route/pallas_call | solution.py:319
  20.0 0.0 collective-permute-start.7
  20.0 0.5 %collective-permute-start.4 = (s32[8,128]{1,0:T(8,128)S(1)}, s32[8,128]{1,0:T(8,128)S(1)}, u32[]{:S(2)}, u32[]{:S(2)}) collective-permute-start(s32[8,128]{1,0:T(8,128)S(1)} %get-tuple-element.22), channel_id=1, source_target_pairs={{0,1},{1,0},{2,3},{3,2},{4,5},{5,4},{6,7},{7,6},{8,9},{9,8},{10,11... | collective-permute-start | bytes 12296 | tf_op jit(solution)/shard_map/ppermute | solution.py:331
  20.5 0.3 collective-permute-start.5
  20.9 2.0 %collective-permute-done.8.refs_6_ = bf16[4,64,768]{2,1,0:T(8,128)(2,1)S(1)} collective-permute-done((bf16[4,64,768]{2,1,0:T(8,128)(2,1)S(1)}, bf16[4,64,768]{2,1,0:T(8,128)(2,1)S(1)}, u32[]{:S(2)}, u32[]{:S(2)}) %collective-permute-start.8) | collective-permute-done | bytes 393248 | tf_op jit(solution)/shard_map/ppermute | solution.py:284
  22.9 0.0 collective-permute-done.7.refs_2_.refs_5_
  22.9 0.0 copy-done
  22.9 0.0 copy-done.1
  22.9 0.0 copy-done.2
  22.9 7.4 %round2.1 = (bf16[40,64,768]{2,1,0:T(8,128)(2,1)S(1)}, bf16[40,64,768]{2,1,0:T(8,128)(2,1)S(1)}, f32[32,64]{1,0:T(8,128)S(1)}) custom-call(s32[8,128]{1,0:T(8,128)S(1)} %get-tuple-element.25.refs_0_.refs_3_, s32[8,128]{1,0:T(8,128)S(1)} %get-tuple-element.26.refs_1_.refs_4_, ...), custom_call_target="tpu_custom_call", output_to_operand_aliasing={{0}: (10, {}), {1}: (11, {})} | custom-call | tf_op jit(solution)/shard_map/round2/pallas_call | solution.py:339
  30.3 0.0 collective-permute-done.6.refs_6_
  30.3 0.0 collective-permute-done.4.refs_1_.refs_4_
  30.3 0.0 collective-permute-done.5.refs_2_.refs_5_
  30.3 6.2 %round1.1 = (bf16[40,64,768]{2,1,0:T(8,128)(2,1)S(1)}, bf16[40,64,768]{2,1,0:T(8,128)(2,1)S(1)}, f32[32,64]{1,0:T(8,128)S(1)}) custom-call(s32[8,128]{1,0:T(8,128)S(1)} %get-tuple-element.21.refs_0_.refs_3_, s32[8,128]{1,0:T(8,128)S(1)} %collective-permute-done.4.refs_1_.refs_4_, ...), custom_call_target="tpu_custom_call", output_to_operand_aliasing={{0}: (10, {}), {1}: (11, {}), {2}: (12, {})} | custom-call | tf_op jit(solution)/shard_map/round1/pallas_call | solution.py:339
  36.6 13.2 %all_to_all.9 = f32[32,1,64]{2,1,0:T(1,128)S(1)} all-to-all(f32[32,1,64]{2,1,0:T(1,128)S(1)} %bitcast.4), channel_id=1, replica_groups=mesh['grp'=4,'shard'=8] {'grp','shard'}, dimensions={0} | all-to-all | bytes 16384 | tf_op jit(solution)/shard_map/all_to_all | solution.py:359
  49.7 0.6 %reduce_sum.9 = f32[64]{0:T(128)} reduce(f32[32,1,64]{2,1,0:T(1,128)S(1)} %all_to_all.9, f32[]{:T(128)} %constant.0.clone.1), dimensions={0,1}, to_apply=%region_0.0 | reduce | flops 1984 | bytes 8452 | tf_op jit(solution)/shard_map/reduce_sum | solution.py:360
Async XLA Ops:
  0.0 10.3 %collective-permute-start.3 = (bf16[16,64,768]{2,1,0:T(8,128)(2,1)}, bf16[16,64,768]{2,1,0:T(8,128)(2,1)S(1)}, u32[]{:S(2)}, u32[]{:S(2)}) collective-permute-start(bf16[16,64,768]{2,1,0:T(8,128)(2,1)} %own.1), channel_id=1, source_target_pairs={{0,1},{1,0},{2,3},{3,2},{4,5},{5,4},{6,7},{7,6},{8,9},{9,8},{10,11... | collective-permute-start | bytes 4718600 | tf_op jit(solution)/shard_map/ppermute | solution.py:271
  2.1 20.7 %collective-permute-start.8 = (bf16[4,64,768]{2,1,0:T(8,128)(2,1)S(1)}, bf16[4,64,768]{2,1,0:T(8,128)(2,1)S(1)}, u32[]{:S(2)}, u32[]{:S(2)}) collective-permute-start(bf16[4,64,768]{2,1,0:T(8,128)(2,1)S(1)} %get-tuple-element.24), channel_id=1, source_target_pairs={{2,0},{3,1},{6,4},{7,5},{0,2},{1,3},{4,6},{5,7},{10,8},{11,9},{14,... | collective-permute-start | bytes 1179656 | tf_op jit(solution)/shard_map/ppermute | solution.py:284
  4.8 25.5 %collective-permute-start.6 = (bf16[4,64,768]{2,1,0:T(8,128)(2,1)S(1)}, bf16[4,64,768]{2,1,0:T(8,128)(2,1)S(1)}, u32[]{:S(2)}, u32[]{:S(2)}) collective-permute-start(bf16[4,64,768]{2,1,0:T(8,128)(2,1)S(1)} %get-tuple-element.24), channel_id=1, source_target_pairs={{4,0},{5,1},{2,4},{3,5},{6,2},{7,3},{0,6},{1,7},{12,8},{13,9},{10,... | collective-permute-start | bytes 1179656 | tf_op jit(solution)/shard_map/ppermute | solution.py:284
  7.3 15.6 %copy-start = (bf16[768,768]{1,0:T(8,128)(2,1)S(1)}, bf16[768,768]{1,0:T(8,128)(2,1)}, u32[]{:S(2)}) copy-start(bf16[768,768]{1,0:T(8,128)(2,1)} %refs_7_.3) | copy-start | bytes 3538948
  7.3 15.6 %copy-start.1 = (bf16[768,768]{1,0:T(8,128)(2,1)S(1)}, bf16[768,768]{1,0:T(8,128)(2,1)}, u32[]{:S(2)}) copy-start(bf16[768,768]{1,0:T(8,128)(2,1)} %refs_8_.3) | copy-start | bytes 3538948
  7.3 15.6 %copy-start.2 = (bf16[768,768]{1,0:T(8,128)(2,1)S(1)}, bf16[768,768]{1,0:T(8,128)(2,1)}, u32[]{:S(2)}) copy-start(bf16[768,768]{1,0:T(8,128)(2,1)} %refs_9_.3) | copy-start | bytes 3538948
  7.3 11.8 %collective-permute-start.2 = (s32[1,64]{1,0:T(1,128)S(1)}, s32[1,64]{1,0:T(1,128)S(1)}, u32[]{:S(2)}, u32[]{:S(2)}) collective-permute-start(s32[1,64]{1,0:T(1,128)S(1)} %get-tuple-element.19.refs_0_), channel_id=1, source_target_pairs={{24,0},{0,8},{8,16},{16,24},{25,1},{1,9},{9,17},{17,25},{26,2},{2,... | collective-permute-start | bytes 776 | tf_op jit(solution)/shard_map/ppermute | solution.py:286
  8.8 10.3 %collective-permute-start.1 = (s32[1,64]{1,0:T(1,128)S(1)}, s32[1,64]{1,0:T(1,128)S(1)}, u32[]{:S(2)}, u32[]{:S(2)}) collective-permute-start(s32[1,64]{1,0:T(1,128)S(1)} %get-tuple-element.19.refs_0_), channel_id=1, source_target_pairs={{16,0},{24,8},{0,16},{8,24},{17,1},{25,9},{1,17},{9,25},{18,2},{26... | collective-permute-start | bytes 776 | tf_op jit(solution)/shard_map/ppermute | solution.py:286
  10.3 8.8 %collective-permute-start = (s32[1,64]{1,0:T(1,128)S(1)}, s32[1,64]{1,0:T(1,128)S(1)}, u32[]{:S(2)}, u32[]{:S(2)}) collective-permute-start(s32[1,64]{1,0:T(1,128)S(1)} %get-tuple-element.19.refs_0_), channel_id=1, source_target_pairs={{8,0},{16,8},{24,16},{0,24},{9,1},{17,9},{25,17},{1,25},{10,2},{18... | collective-permute-start | bytes 776 | tf_op jit(solution)/shard_map/ppermute | solution.py:286
  20.0 2.9 %collective-permute-start.7 = (s32[8,128]{1,0:T(8,128)S(1)}, s32[8,128]{1,0:T(8,128)S(1)}, u32[]{:S(2)}, u32[]{:S(2)}) collective-permute-start(s32[8,128]{1,0:T(8,128)S(1)} %get-tuple-element.27), channel_id=1, source_target_pairs={{0,1},{1,0},{2,3},{3,2},{4,5},{5,4},{6,7},{7,6},{8,9},{9,8},{10,11... | collective-permute-start | bytes 12296 | tf_op jit(solution)/shard_map/ppermute | solution.py:331
  20.0 10.3 %collective-permute-start.4 = (s32[8,128]{1,0:T(8,128)S(1)}, s32[8,128]{1,0:T(8,128)S(1)}, u32[]{:S(2)}, u32[]{:S(2)}) collective-permute-start(s32[8,128]{1,0:T(8,128)S(1)} %get-tuple-element.22), channel_id=1, source_target_pairs={{0,1},{1,0},{2,3},{3,2},{4,5},{5,4},{6,7},{7,6},{8,9},{9,8},{10,11... | collective-permute-start | bytes 12296 | tf_op jit(solution)/shard_map/ppermute | solution.py:331
  20.5 9.8 %collective-permute-start.5 = (s32[8,128]{1,0:T(8,128)S(1)}, s32[8,128]{1,0:T(8,128)S(1)}, u32[]{:S(2)}, u32[]{:S(2)}) collective-permute-start(s32[8,128]{1,0:T(8,128)S(1)} %get-tuple-element.23), channel_id=1, source_target_pairs={{4,0},{5,1},{2,4},{3,5},{6,2},{7,3},{0,6},{1,7},{12,8},{13,9},{10,... | collective-permute-start | bytes 12296 | tf_op jit(solution)/shard_map/ppermute | solution.py:333

commit v3 on v2

v3 whole, which is shorter than its diff:
```python
import functools
import math

import jax
import jax.numpy as jnp
from jax import lax
from jax.experimental import pallas as pl
from jax.experimental.pallas import tpu as pltpu
from jax.sharding import PartitionSpec as P

SOFTMAX_WARMTH = 0.07
EPSILON = 1e-06
LANES = 128
STEPS = (16, 8, 4)
F32 = jnp.float32
BF16 = jnp.bfloat16
NT = (((1,), (1,)), ((), ()))
IX, IY, READER, SLOT, VALID, TOTAL = range(6)


def vmem():
    return pl.BlockSpec(memory_space=pltpu.VMEM)


def hbm():
    return pl.BlockSpec(memory_space=pltpu.HBM)


def in_hbm(x):
    return pltpu.with_memory_space_constraint(x, pltpu.HBM)


def smem():
    return pl.BlockSpec(memory_space=pltpu.SMEM)


def dot(a, b):
    return jnp.dot(a, b, preferred_element_type=F32)


def dot_nt(a, b):
    return lax.dot_general(a, b, NT, preferred_element_type=F32)


def first_projection(blocks, w_cell, proj, at):
    _, samples, width = blocks[0].shape
    cells = jnp.concatenate([block.reshape(-1, width) for block in blocks], axis=0)
    rows = dot(cells, w_cell[...]).astype(BF16)
    proj[at : at + rows.shape[0] // samples] = rows.reshape(-1, samples, width)
    return rows


def second_projection(rows, w_mix, mixed, at):
    _, samples, width = mixed.shape
    mixed[at : at + rows.shape[0] // samples] = (
        dot(rows, w_mix[...]).astype(BF16).reshape(-1, samples, width)
    )


def project_kernel(own, partner, w_cell, w_mix, w_pool, proj, mixed, mix_in, pool_in, own_in, sems):
    columns = own.shape[0]
    copies = [
        pltpu.make_async_copy(w_mix, mix_in, sems.at[0]),
        pltpu.make_async_copy(own, own_in, sems.at[1]),
        pltpu.make_async_copy(w_pool, pool_in, sems.at[2]),
    ]
    for copy in copies:
        copy.start()
    rows = first_projection([partner[...]], w_cell, proj, columns)
    copies[0].wait()
    second_projection(rows, mix_in, mixed, columns)
    copies[1].wait()
    rows = first_projection([own_in[...]], w_cell, proj, 0)
    second_projection(rows, mix_in, mixed, 0)
    copies[2].wait()


def chip_kernel(score_scale, index, rows, proj, mixed, w_pool, _, out, pool_x, pool_y, fields):
    out[...] = jnp.zeros(out.shape, F32)
    lists = [(index, rows, 0)]
    attend_lists(lists, 0, proj, mixed, score_scale, pool_x, pool_y)
    score_lists(lists, w_pool, out, pool_x, pool_y, fields)


def attend_pairs(pairs, proj, mixed, score_scale):
    samples = proj.shape[1]
    shape = (samples, 2 * samples)
    lane = lax.broadcasted_iota(jnp.int32, shape, 1)
    first = lane < samples
    unit = (lax.rem(lane, samples) == lax.broadcasted_iota(jnp.int32, shape, 0)).astype(F32)
    weights = []
    for x, y in pairs:
        both = dot_nt(
            jnp.concatenate([proj[y], proj[x]], axis=0), jnp.concatenate([proj[x], proj[y]], axis=0)
        )
        weights.append(jnp.where(first, both[:samples], both[samples:]) * score_scale)
    weights = [jnp.exp(w - jnp.max(w, axis=0, keepdims=True)) for w in weights]
    weights = [w * (1.0 / jnp.sum(w, axis=0, keepdims=True)) for w in weights]
    attend = [
        jnp.transpose(
            jnp.concatenate([jnp.where(first, w, unit), jnp.where(first, unit, w)], axis=0)
        ).astype(BF16)
        for w in weights
    ]
    pooled = []
    for t, (x, y) in zip(attend, pairs):
        rows = jnp.tanh(dot(t, jnp.concatenate([mixed[y], mixed[x]], axis=0)))
        pooled.append(
            [jnp.sum(r, axis=0, keepdims=True) * (1.0 / samples) for r in (rows[:samples], rows[samples:])]
        )
    return pooled


def lists_of(held, index, rows):
    return [(i, r, 8 * at) for i, r, number in zip(index, rows, held) for at in range(number)]


def near_kernel(chips, base, held, score_scale, *refs):
    count = len(held)
    index, remote = refs[:count], refs[count : count + chips]
    w_cell, w_mix, _, _, proj, mixed, pool_x, pool_y = refs[count + chips :]
    rows = first_projection([ref[...] for ref in remote], w_cell, proj, base)
    second_projection(rows, w_mix, mixed, base)
    attend_lists(lists_of(held, index, index), 0, proj, mixed, score_scale, pool_x, pool_y)


def far_kernel(held, near, score_scale, *refs):
    count = len(held)
    index, rows = refs[:count], refs[count : 2 * count]
    proj, mixed, w_pool, before, _, _, out, pool_x, pool_y, fields = refs[2 * count :]
    lists = lists_of(held, index, rows)
    out[...] = before[...]
    attend_lists(lists, near, proj, mixed, score_scale, pool_x, pool_y)
    score_lists(lists, w_pool, out, pool_x, pool_y, fields)


def starts_of(lists):
    starts = [0]
    for ref, _, row in lists:
        starts.append(starts[-1] + ref[row + TOTAL, 0])
    return starts


def attend_lists(lists, done, proj, mixed, score_scale, pool_x, pool_y):
    lanes = lists[0][0].shape[1]
    starts = starts_of(lists)
    todo = list(zip(lists, starts))[done:]

    def column(at):
        x = y = 0
        for (ref, _, row), start in todo:
            here = jnp.clip(at - start, 0, lanes - 1)
            x = jnp.where(at >= start, ref[row + IX, here], x)
            y = jnp.where(at >= start, ref[row + IY, here], y)
        return x, y

    def step(first, size, i, carry):
        at = [first + i * size + u for u in range(size)]
        pooled = attend_pairs([column(p) for p in at], proj, mixed, score_scale)
        for p, (row_x, row_y) in zip(at, pooled):
            pool_x[pl.ds(p, 1)] = row_x
            pool_y[pl.ds(p, 1)] = row_y
        return carry

    large, middle, small = STEPS
    left = starts[-1] - starts[done]
    rest = lax.rem(left, large)
    counts = (
        left // large + (rest > middle + small).astype(jnp.int32),
        ((rest > small) & (rest <= middle + small)).astype(jnp.int32),
        (((rest > 0) & (rest <= small)) | ((rest > middle) & (rest <= middle + small))).astype(jnp.int32),
    )
    first = starts[done]
    for size, count in zip(STEPS, counts):
        lax.fori_loop(0, count, functools.partial(step, first, size), 0)
        first = first + size * count


def score_lists(lists, w_pool, out, pool_x, pool_y, fields):
    starts = starts_of(lists)
    total = starts[-1]
    lanes, capacity = lists[0][0].shape[1], fields.shape[1]
    lane = lax.broadcasted_iota(jnp.int32, fields.shape, 1)
    joined = jnp.zeros(fields.shape, jnp.int32)
    for (_, ref, row), start in zip(lists, starts):
        wide = [ref[row : row + 8]] + [jnp.zeros((8, lanes), jnp.int32)] * (capacity // lanes - 1)
        wide = jnp.concatenate(wide, axis=1) if len(wide) > 1 else wide[0]
        joined = jnp.where(lane >= start, pltpu.roll(wide, start, 1), joined)
    fields[...] = joined
    block = LANES
    readers, slots = out.shape

    def step(i, carry):
        here = pl.ds(pl.multiple_of(i * block, block), block)
        z = dot(jnp.concatenate([pool_x[here], pool_y[here]], axis=0).astype(BF16), w_pool[...])
        zx, zy = z[:block], z[block:]
        inner = jnp.mean(zx * zy, axis=1, keepdims=True)
        norms = (jnp.mean(zx * zx, axis=1, keepdims=True) + EPSILON) * (
            jnp.mean(zy * zy, axis=1, keepdims=True) + EPSILON
        )
        score = inner / jnp.sqrt(norms) / SOFTMAX_WARMTH
        score = jnp.transpose(jnp.broadcast_to(score, (block, block)))[:1]
        field = fields[:, here]
        live = (field[VALID : VALID + 1] > 0) & (
            lax.broadcasted_iota(jnp.int32, (1, block), 1) < total - i * block
        )
        score = jnp.where(live, score, 0.0)
        of_reader = field[READER : READER + 1] == lax.broadcasted_iota(
            jnp.int32, (readers, block), 0
        )
        of_slot = field[SLOT : SLOT + 1] == lax.broadcasted_iota(jnp.int32, (slots, block), 0)
        out[...] += lax.dot_general(
            jnp.where(of_reader, score, 0.0),
            of_slot.astype(F32),
            NT,
            preferred_element_type=F32,
            precision=lax.Precision.HIGHEST,
        )
        return carry

    lax.fori_loop(0, (total + block - 1) // block, step, 0)


def share_kernel(quarter, cells, share, sem):
    first = lax.axis_index("grp") * quarter
    copy = pltpu.make_async_copy(cells.at[pl.ds(first, quarter)], share, sem)
    copy.start()
    copy.wait()


def prepare_kernel(sizes, pairs, counts, w_cell, _, ids, own_list, cell_in, held, sems):
    lines, shards, per_shard, pair_dev = sizes
    line, shard = lax.axis_index("grp"), lax.axis_index("shard")
    copy_cell = pltpu.make_async_copy(w_cell, cell_in, sems.at[0])
    copy_pairs = pltpu.make_async_copy(pairs, held, sems.at[1])
    copy_pairs.start()
    copy_cell.start()
    copy_pairs.wait()
    slot = lax.broadcasted_iota(jnp.int32, ids.shape, 1)
    a, b = held[:1], held[1:]
    live = slot < counts[0]
    ids[...] = jnp.where(live, a * (shards * per_shard) + b, -1)
    mine = live & (b // (2 * per_shard) == shard // 2)
    x = lax.rem(a, per_shard)
    y = lax.rem(b, per_shard) + per_shard * lax.rem(b // per_shard + shard, 2)
    reader = jnp.full_like(slot, line * shards + shard)
    own_list[...] = pack_list(mine, (x, y, reader, slot), own_list.shape[1])
    copy_cell.wait()


def pack_list(mine, values, lanes):
    rows, slots = mine.shape
    earlier = (
        lax.broadcasted_iota(jnp.int32, (slots, slots), 0)
        < lax.broadcasted_iota(jnp.int32, (slots, slots), 1)
    ).astype(BF16)
    place = lax.broadcasted_iota(jnp.int32, (lanes, slots), 0)
    field = lax.broadcasted_iota(jnp.int32, (8, slots), 0)
    before = dot(mine.astype(BF16), earlier)
    row_total = jnp.sum(mine.astype(F32), axis=1, keepdims=True)
    total = jnp.zeros((1, 1), F32)
    packed = jnp.zeros((8, lanes), F32)
    for r in range(rows):
        position = (before[r : r + 1] + total).astype(jnp.int32)
        position = jnp.where(mine[r : r + 1], position, -1)
        total = total + row_total[r : r + 1]
        chosen = (place == position).astype(BF16)
        fields = jnp.where(field == VALID, 1, 0)
        for which, value in zip((IX, IY, READER, SLOT), values):
            fields = jnp.where(field == which, value[r : r + 1], fields)
        packed = packed + dot_nt(fields.astype(BF16), chosen)
    row = lax.broadcasted_iota(jnp.int32, (8, lanes), 0)
    return jnp.where(row == TOTAL, total, packed).astype(jnp.int32)


def route_kernel(sizes, whose, *refs):
    lines, shards, per_shard, pair_dev = sizes
    ids_refs, out_refs = refs[:lines], refs[lines + 1 :]
    total_columns = shards * per_shard
    chip_columns = 2 * per_shard
    chips = shards // 2
    quarter = per_shard // lines
    line = lax.axis_index("grp")
    shard = lax.axis_index("shard")
    chip, core = shard // 2, lax.rem(shard, 2)
    ids = jnp.concatenate([ref[...] for ref in ids_refs], axis=0)
    live = ids >= 0
    kept = jnp.maximum(ids, 0)
    a = kept // total_columns
    b = kept - a * total_columns
    b_chip = b // chip_columns
    b_shard = b // per_shard
    a_local = lax.rem(a, per_shard)
    b_local = lax.rem(b, per_shard)
    reader_row = lax.broadcasted_iota(jnp.int32, ids.shape, 0)
    reader_id = lax.rem(line + reader_row, lines) * shards + shard
    slot = lax.broadcasted_iota(jnp.int32, ids.shape, 1)
    b_own = b_local + per_shard * lax.rem(b_shard + core, 2)
    lanes = out_refs[0].shape[1]
    for group, out_ref in zip(whose, out_refs):
        for at, (kind, offset) in enumerate(group):
            base = chip_columns + (offset - 1) * quarter
            if kind in ("receive", "partner"):
                here = core if kind == "receive" else 1 - core
                source = ring_place(chip, chips, offset)
                mine = live & (b_shard == source * 2 + here) & (b_local // quarter == line)
                x = a_local if kind == "receive" else a_local + per_shard
                y = base + b_local - line * quarter
            else:
                target = ring_place(chip, chips, -offset)
                mine = live & (b_chip == target) & (a_local // quarter == line)
                x, y = b_own, base + a_local - line * quarter
            out_ref[8 * at : 8 * at + 8] = pack_list(mine, (x, y, reader_id, slot), lanes)


def ring_place(chip, chips, offset):
    half = chips // 2
    place = jnp.where(chip < half, 2 * chip, 2 * (chip - half) + 1)
    other = lax.rem(place + offset + 2 * chips, chips)
    return other // 2 + half * lax.rem(other, 2)


def ring_of(chips):
    half = chips // 2
    return [p // 2 + half * (p % 2) for p in range(chips)]


def local(mesh_shape, cells, w_cell, w_mix, w_pool, pairs, counts):
    lines, shards = mesh_shape["grp"], mesh_shape["shard"]
    chips = shards // 2
    per_shard, samples, width = cells.shape
    pair_dev = pairs.shape[0]
    quarter = per_shard // lines
    score_scale = 1.0 / math.sqrt(width)
    ring = ring_of(chips)

    def from_ahead(offset):
        return [
            (2 * ring[(p + offset) % chips] + c, 2 * ring[p] + c) for p in range(chips) for c in (0, 1)
        ]

    offsets = range(1, chips // 2 + 1)
    swap = [(s, s ^ 1) for s in range(shards)]
    sizes = (lines, shards, per_shard, pair_dev)
    most = lines * min(pair_dev, 4 * pair_dev // shards)
    lanes = -(-max(most, pair_dev) // LANES) * LANES
    weight = jax.ShapeDtypeStruct(w_cell.shape, BF16)
    weight_bytes = 2 * width * width
    share = pl.pallas_call(
        functools.partial(share_kernel, quarter),
        out_shape=jax.ShapeDtypeStruct((quarter, samples, width), BF16),
        in_specs=[hbm()],
        out_specs=vmem(),
        scratch_shapes=[pltpu.SemaphoreType.DMA(())],
        compiler_params=pltpu.CompilerParams(vmem_limit_bytes=4 * 2**20),
        name="share",
    )(in_hbm(cells))
    remote = {d: lax.ppermute(share, "shard", from_ahead(d)) for d in offsets}
    cells, _ = lax.optimization_barrier((cells, share))
    partner = lax.ppermute(cells, "shard", swap)
    ids, own_list, w_cell = pl.pallas_call(
        functools.partial(prepare_kernel, sizes),
        out_shape=(
            jax.ShapeDtypeStruct((1, pair_dev), jnp.int32),
            jax.ShapeDtypeStruct((8, lanes), jnp.int32),
            weight,
        ),
        in_specs=[hbm(), smem(), hbm(), pl.BlockSpec(memory_space=pl.ANY)],
        out_specs=[vmem()] * 3,
        scratch_shapes=[pltpu.VMEM((2, pair_dev), jnp.int32), pltpu.SemaphoreType.DMA((2,))],
        compiler_params=pltpu.CompilerParams(vmem_limit_bytes=weight_bytes + 4 * 2**20),
        name="prepare",
    )(in_hbm(pairs.T), counts, in_hbm(w_cell), share)
    ids = [ids] + [
        lax.ppermute(ids, "grp", [((g + k) % lines, g) for g in range(lines)])
        for k in range(1, lines)
    ]

    store = jax.ShapeDtypeStruct((2 * per_shard + len(offsets) * quarter, samples, width), BF16)
    scores = jax.ShapeDtypeStruct((lines * shards, pair_dev), F32)
    store_bytes = 2 * math.prod(store.shape)
    weight_bytes = 2 * width * width

    def pool(count):
        return jax.ShapeDtypeStruct((count * lanes + STEPS[0], width), F32)

    def limit(spare):
        return pltpu.CompilerParams(
            vmem_limit_bytes=2 * store_bytes + 3 * weight_bytes + spare * 2**20
        )

    proj, mixed, w_mix, w_pool = pl.pallas_call(
        project_kernel,
        out_shape=[store, store, weight, weight],
        in_specs=[hbm(), vmem(), vmem(), hbm(), hbm()],
        out_specs=[vmem()] * 4,
        scratch_shapes=[pltpu.VMEM(cells.shape, BF16), pltpu.SemaphoreType.DMA((3,))],
        compiler_params=limit(16),
        name="project",
    )(in_hbm(cells), partner, w_cell, in_hbm(w_mix), in_hbm(w_pool))

    groups = [offsets[i : i + 2] for i in range(0, len(offsets), 2)]
    whose, spans = [], []
    for group in groups:
        near = [[(kind, d) for d in group] for kind in ("receive", "partner")]
        far = [[("send", d)] for d in group if 2 * d != chips]
        spans.append((len(whose), len(whose) + len(near), len(whose) + len(near + far)))
        whose += near + far
    lists = pl.pallas_call(
        functools.partial(route_kernel, sizes, whose),
        out_shape=[jax.ShapeDtypeStruct((8 * len(kinds), lanes), jnp.int32) for kinds in whose],
        in_specs=[vmem()] * lines + [pl.BlockSpec(memory_space=pl.ANY)],
        out_specs=[vmem()] * len(whose),
        compiler_params=pltpu.CompilerParams(vmem_limit_bytes=4 * 2**20),
        name="route",
    )(*ids, proj)
    arrived = []
    for kinds, packed in zip(whose, lists):
        kind, d = kinds[0]
        if kind == "partner":
            packed = lax.ppermute(packed, "shard", swap)
        elif kind == "send":
            packed = lax.ppermute(packed, "shard", from_ahead(d))
        arrived.append(packed)

    out = pl.pallas_call(
        functools.partial(chip_kernel, score_scale),
        out_shape=scores,
        in_specs=[smem()] + [vmem()] * 4 + [pl.BlockSpec(memory_space=pl.ANY)],
        out_specs=vmem(),
        scratch_shapes=[
            pltpu.VMEM(pool(1).shape, F32),
            pltpu.VMEM(pool(1).shape, F32),
            pltpu.VMEM((8, lanes), jnp.int32),
        ],
        compiler_params=limit(16),
        name="chip",
    )(own_list, own_list, proj, mixed, w_pool, lists[-1])

    for group, (first, middle, last) in zip(groups, spans):
        use = arrived[first:last]
        held = [x.shape[0] // 8 for x in use]
        number = middle - first
        at = number + len(group) + 2
        proj, mixed, pool_x, pool_y = pl.pallas_call(
            functools.partial(
                near_kernel,
                len(group),
                2 * per_shard + (group[0] - 1) * quarter,
                held[:number],
                score_scale,
            ),
            out_shape=(store, store, pool(sum(held)), pool(sum(held))),
            in_specs=[smem()] * number + [vmem()] * (len(group) + 4),
            out_specs=[vmem()] * 4,
            input_output_aliases={at: 0, at + 1: 1},
            compiler_params=limit(20),
            name="near" + "_".join(map(str, group)),
        )(*use[:number], *(remote[d] for d in group), w_cell, w_mix, proj, mixed)
        at = 2 * len(use) + 3
        out, *_ = pl.pallas_call(
            functools.partial(far_kernel, held, sum(held[:number]), score_scale),
            out_shape=(scores, pool(sum(held)), pool(sum(held))),
            in_specs=[smem()] * len(use) + [vmem()] * (len(use) + 6),
            out_specs=[vmem()] * 3,
            input_output_aliases={at: 0, at + 1: 1, at + 2: 2},
            scratch_shapes=[pltpu.VMEM((8, sum(held) * lanes), jnp.int32)],
            compiler_params=limit(20),
            name="far" + "_".join(map(str, group)),
        )(*use, *use, proj, mixed, w_pool, out, pool_x, pool_y)

    back = lax.all_to_all(out, ("grp", "shard"), 0, 0, tiled=True)
    return jnp.sum(back, axis=0)


def solution(mesh):
    placed = (P("shard", None, None), P(), P(), P(), P(("grp", "shard"), None), P(("grp", "shard")))
    return jax.shard_map(
        functools.partial(local, dict(mesh.shape)),
        mesh=mesh,
        in_specs=placed,
        out_specs=P(("grp", "shard")),
        check_vma=False,
    )
```

time: 51.1 us -> 46.7 us (0.914)
  blocking collectives: 13.2 us -> 9.74 us
  waiting for transfers between devices: 2.05 us -> 0.72 us
  Pallas kernels: 22.9 us -> 24.1 us
    all_to_all x1, blocking collectives: 13.2 us -> 9.74 us  [local(): back = lax.all_to_all(out, ('grp', 'shard'), 0, 0, tiled=True)]
    ppermute x5 -> x4, waiting for transfers between devices: 2.04 us -> 0.71 us  [the longest x2 0.7 us: local(): remote = {d: lax.ppermute(share, 'shard', from_ahead(d)) for d in offsets}]
    pallas_call x5 -> x7, Pallas kernels: 22.9 us -> 24.1 us  [the longest x1 7.48 us: local(): pl.pallas_call(functools.partial(near_kernel, len(group), 2 * per_shard +...]
    ppermute x5 -> x4, starting transfers between devices: 5.97 us -> 5.51 us  [the longest x2 5.13 us: local(): remote = {d: lax.ppermute(share, 'shard', from_ahead(d)) for d in offsets}]
  transfers between devices with their start and end apart: 9 -> 8, of which waited for: 1 -> 1; matrix products, arithmetic and copies ran while one was open for 0% -> 0% of each run, Pallas kernels for 33% -> 42%
where the time goes in v3:
time: 46.7 us; the launch traced here: 46.4 us
  Pallas kernels  24.1 us (52%)
  starting transfers between devices  10.5 us (22%)
  blocking collectives  9.74 us (21%)
  waiting for transfers between devices  0.72 us (2%)
  between operations  0.72 us (2%)
  other arithmetic  0.56 us (1%)
    all_to_all x1, blocking collectives, local(): back = lax.all_to_all(out, ('grp', 'shard'), 0, 0, tiled=True)  9.74 us
    pallas_call x1, Pallas kernels, local(): pl.pallas_call(functools.partial(near_kernel, len(group), 2 * per_shard +...  7.48 us
    pallas_call x1, Pallas kernels, local(): pl.pallas_call(project_kernel, out_shape=[store, store, weight, weight],...  6.33 us
    ppermute x2, starting transfers between devices, local(): remote = {d: lax.ppermute(share, 'shard', from_ahead(d)) for d in offsets}  5.13 us
    ppermute x3, starting transfers between devices, local(): lax.ppermute(ids, 'grp', [((g + k) % lines, g) for g in range(lines)])  4.5 us
    pallas_call x1, Pallas kernels, local(): pl.pallas_call(functools.partial(far_kernel, held, sum(held[:number]), sc...  3.73 us
    pallas_call x1, Pallas kernels, local(): pl.pallas_call(functools.partial(chip_kernel, score_scale), out_shape=sco...  3.37 us
    pallas_call x1, Pallas kernels, local(): pl.pallas_call(functools.partial(prepare_kernel, sizes), out_shape=(jax.S...  1.31 us
  transfers between devices with their start and end apart: 8, of which 1 were waited for; matrix products, arithmetic and copies ran while one was open for 0% of the time, Pallas kernels for 42%

profile of v3, /device:TPU:0, one launch (start us, length us, event | category | flops | bytes accessed | tf_op | source)
XLA Modules:
  0.0 46.4 jit_solution(16495015853716516954)
XLA Ops:
  0.0 1.0 %share.1._ = bf16[4,64,768]{2,1,0:T(8,128)(2,1)S(1)} custom-call(bf16[16,64,768]{2,1,0:T(8,128)(2,1)} %own), custom_call_target="tpu_custom_call" | custom-call | tf_op jit(solution)/shard_map/share/pallas_call | solution.py:349
  1.0 0.5 %collective-permute-start.3 = (bf16[16,64,768]{2,1,0:T(8,128)(2,1)}, bf16[16,64,768]{2,1,0:T(8,128)(2,1)S(1)}, u32[]{:S(2)}, u32[]{:S(2)}) collective-permute-start(bf16[16,64,768]{2,1,0:T(8,128)(2,1)} %own), channel_id=1, source_target_pairs={{0,1},{1,0},{2,3},{3,2},{4,5},{5,4},{6,7},{7,6},{8,9},{9,8},{10,11... | collective-permute-start | bytes 4718600 | tf_op jit(solution)/shard_map/ppermute | solution.py:360
  1.5 2.7 %collective-permute-start.7 = (bf16[4,64,768]{2,1,0:T(8,128)(2,1)S(1)}, bf16[4,64,768]{2,1,0:T(8,128)(2,1)S(1)}, u32[]{:S(2)}, u32[]{:S(2)}) collective-permute-start(bf16[4,64,768]{2,1,0:T(8,128)(2,1)S(1)} %share.1._), channel_id=1, source_target_pairs={{2,0},{3,1},{6,4},{7,5},{0,2},{1,3},{4,6},{5,7},{10,8},{11,9},{14,... | collective-permute-start | bytes 1179656 | tf_op jit(solution)/shard_map/ppermute | solution.py:358
  4.2 2.5 %collective-permute-start.6 = (bf16[4,64,768]{2,1,0:T(8,128)(2,1)S(1)}, bf16[4,64,768]{2,1,0:T(8,128)(2,1)S(1)}, u32[]{:S(2)}, u32[]{:S(2)}) collective-permute-start(bf16[4,64,768]{2,1,0:T(8,128)(2,1)S(1)} %share.1._), channel_id=1, source_target_pairs={{4,0},{5,1},{2,4},{3,5},{6,2},{7,3},{0,6},{1,7},{12,8},{13,9},{10,... | collective-permute-start | bytes 1179656 | tf_op jit(solution)/shard_map/ppermute | solution.py:358
  7.3 1.3 %prepare.1 = (s32[1,64]{1,0:T(1,128)S(1)}, s32[8,128]{1,0:T(8,128)S(1)}, bf16[768,768]{1,0:T(8,128)(2,1)S(1)}) custom-call(s32[2,64]{1,0:T(2,128)} %bitcast.5, s32[1]{0:T(128)S(6)} %copy.18.counts, bf16[768,768]{1,0:T(8,128)(2,1)} %w_cell.1, bf16[4,64,768]{2,1,0:T(8,128)(2,1)S(1)} %share.1._), custom_call_target="tpu_custom_call" | custom-call | tf_op jit(solution)/shard_map/prepare/pallas_call | solution.py:361
  8.6 1.5 %collective-permute-start.2 = (s32[1,64]{1,0:T(1,128)S(1)}, s32[1,64]{1,0:T(1,128)S(1)}, u32[]{:S(2)}, u32[]{:S(2)}) collective-permute-start(s32[1,64]{1,0:T(1,128)S(1)} %get-tuple-element.21.refs_0_), channel_id=1, source_target_pairs={{24,0},{0,8},{8,16},{16,24},{25,1},{1,9},{9,17},{17,25},{26,2},{2,... | collective-permute-start | bytes 776 | tf_op jit(solution)/shard_map/ppermute | solution.py:375
  10.2 1.5 %collective-permute-start.1 = (s32[1,64]{1,0:T(1,128)S(1)}, s32[1,64]{1,0:T(1,128)S(1)}, u32[]{:S(2)}, u32[]{:S(2)}) collective-permute-start(s32[1,64]{1,0:T(1,128)S(1)} %get-tuple-element.21.refs_0_), channel_id=1, source_target_pairs={{16,0},{24,8},{0,16},{8,24},{17,1},{25,9},{1,17},{9,25},{18,2},{26... | collective-permute-start | bytes 776 | tf_op jit(solution)/shard_map/ppermute | solution.py:375
  11.7 0.0 collective-permute-done.3.partner
  11.7 1.4 %collective-permute-start = (s32[1,64]{1,0:T(1,128)S(1)}, s32[1,64]{1,0:T(1,128)S(1)}, u32[]{:S(2)}, u32[]{:S(2)}) collective-permute-start(s32[1,64]{1,0:T(1,128)S(1)} %get-tuple-element.21.refs_0_), channel_id=1, source_target_pairs={{8,0},{16,8},{24,16},{0,24},{9,1},{17,9},{25,17},{1,25},{10,2},{18... | collective-permute-start | bytes 776 | tf_op jit(solution)/shard_map/ppermute | solution.py:375
  13.1 6.3 %project.1 = (bf16[40,64,768]{2,1,0:T(8,128)(2,1)S(1)}, bf16[40,64,768]{2,1,0:T(8,128)(2,1)S(1)}, bf16[768,768]{1,0:T(8,128)(2,1)S(1)}, bf16[768,768]{1,0:T(8,128)(2,1)S(1)}) custom-call(bf16[16,64,768]{2,1,0:T(8,128)(2,1)} %own, bf16[16,64,768]{2,1,0:T(8,128)(2,1)S(1)} %collective-permute-done.3.partner, ...), custom_call_target="tpu_custom_call" | custom-call | tf_op jit(solution)/shard_map/project/pallas_call | solution.py:392
  19.5 0.0 collective-permute-done.2.refs_3_
  19.5 0.0 collective-permute-done.1.refs_2_
  19.5 0.0 collective-permute-done.refs_1_
  19.5 0.9 %route.1 = (s32[16,128]{1,0:T(8,128)S(1)}, s32[16,128]{1,0:T(8,128)S(1)}, s32[8,128]{1,0:T(8,128)S(1)}) custom-call(s32[1,64]{1,0:T(1,128)S(1)} %get-tuple-element.21.refs_0_, s32[1,64]{1,0:T(1,128)S(1)} %collective-permute-done.refs_1_, s32[1,64]{1,0:T(1,128)S(1)} %collective-permute-done.1.refs_2_, s32[1,64]{1,0:T(1,128)S(1)} %collective-permute-done.2.refs_3_, ...), custom_call_target="tpu_custom_call" | custom-call | tf_op jit(solution)/shard_map/route/pallas_call | solution.py:409
  20.4 0.0 collective-permute-start.4
  20.4 0.4 collective-permute-start.5
  20.8 3.4 %chip.1.refs_9_ = f32[32,64]{1,0:T(8,128)S(1)} custom-call(s32[8,128]{1,0:T(8,128)S(1)} %get-tuple-element.33.index.rows, s32[8,128]{1,0:T(8,128)S(1)} %get-tuple-element.33.index.rows, bf16[40,64,768]{2,1,0:T(8,128)(2,1)S(1)} %get-tuple-element.24.refs_4_.refs_6_.proj, bf16[40,64,768]{2,1,0:T(8,128)(2,1)S(1)} %get-tuple-element.29.refs_7_.mixed, ...), custom_call_target="tpu_custom_call" | custom-call | tf_op jit(solution)/shard_map/chip/pallas_call | solution.py:426
  24.1 0.0 collective-permute-done.7.refs_3_
  24.1 0.7 %collective-permute-done.6.refs_2_ = bf16[4,64,768]{2,1,0:T(8,128)(2,1)S(1)} collective-permute-done((bf16[4,64,768]{2,1,0:T(8,128)(2,1)S(1)}, bf16[4,64,768]{2,1,0:T(8,128)(2,1)S(1)}, u32[]{:S(2)}, u32[]{:S(2)}) %collective-permute-start.6) | collective-permute-done | bytes 393248 | tf_op jit(solution)/shard_map/ppermute | solution.py:358
  24.8 0.0 collective-permute-done.4.refs_1_.refs_4_
  24.8 7.5 %near1_2.1 = (bf16[40,64,768]{2,1,0:T(8,128)(2,1)S(1)}, bf16[40,64,768]{2,1,0:T(8,128)(2,1)S(1)}, f32[656,768]{1,0:T(8,128)S(1)}, f32[656,768]{1,0:T(8,128)S(1)}) custom-call(s32[16,128]{1,0:T(8,128)S(1)} %get-tuple-element.25.refs_0_.refs_3_, s32[16,128]{1,0:T(8,128)S(1)} %collective-permute-done.4.refs_1_.refs_4_, ...), custom_call_target="tpu_custom_call", output_to_operand_aliasing={{0}: (6, {}), {1}: (7, {})} | custom-call | tf_op jit(solution)/shard_map/near1_2/pallas_call | solution.py:445
  32.3 0.0 collective-permute-done.5.refs_2_.refs_5_
  32.3 3.7 %far1_2.1 = (f32[32,64]{1,0:T(8,128)S(1)}, f32[656,768]{1,0:T(8,128)S(1)}, f32[656,768]{1,0:T(8,128)S(1)}) custom-call(s32[16,128]{1,0:T(8,128)S(1)} %get-tuple-element.25.refs_0_.refs_3_, s32[16,128]{1,0:T(8,128)S(1)} %collective-permute-done.4.refs_1_.refs_4_, ...), custom_call_target="tpu_custom_call", output_to_operand_aliasing={{0}: (9, {}), {1}: (10, {}), {2}: (11, {})} | custom-call | tf_op jit(solution)/shard_map/far1_2/pallas_call | solution.py:461
  36.1 9.7 %all_to_all.9 = f32[32,1,64]{2,1,0:T(1,128)S(1)} all-to-all(f32[32,1,64]{2,1,0:T(1,128)S(1)} %bitcast.4), channel_id=1, replica_groups=mesh['grp'=4,'shard'=8] {'grp','shard'}, dimensions={0} | all-to-all | bytes 16384 | tf_op jit(solution)/shard_map/all_to_all | solution.py:472
  45.8 0.6 %reduce_sum.9 = f32[64]{0:T(128)} reduce(f32[32,1,64]{2,1,0:T(1,128)S(1)} %all_to_all.9, f32[]{:T(128)} %constant.0.clone.1), dimensions={0,1}, to_apply=%region_0.0 | reduce | flops 1984 | bytes 8452 | tf_op jit(solution)/shard_map/reduce_sum | solution.py:473
Async XLA Ops:
  1.0 10.7 %collective-permute-start.3 = (bf16[16,64,768]{2,1,0:T(8,128)(2,1)}, bf16[16,64,768]{2,1,0:T(8,128)(2,1)S(1)}, u32[]{:S(2)}, u32[]{:S(2)}) collective-permute-start(bf16[16,64,768]{2,1,0:T(8,128)(2,1)} %own), channel_id=1, source_target_pairs={{0,1},{1,0},{2,3},{3,2},{4,5},{5,4},{6,7},{7,6},{8,9},{9,8},{10,11... | collective-permute-start | bytes 4718600 | tf_op jit(solution)/shard_map/ppermute | solution.py:360
  1.5 22.6 %collective-permute-start.7 = (bf16[4,64,768]{2,1,0:T(8,128)(2,1)S(1)}, bf16[4,64,768]{2,1,0:T(8,128)(2,1)S(1)}, u32[]{:S(2)}, u32[]{:S(2)}) collective-permute-start(bf16[4,64,768]{2,1,0:T(8,128)(2,1)S(1)} %share.1._), channel_id=1, source_target_pairs={{2,0},{3,1},{6,4},{7,5},{0,2},{1,3},{4,6},{5,7},{10,8},{11,9},{14,... | collective-permute-start | bytes 1179656 | tf_op jit(solution)/shard_map/ppermute | solution.py:358
  4.2 20.6 %collective-permute-start.6 = (bf16[4,64,768]{2,1,0:T(8,128)(2,1)S(1)}, bf16[4,64,768]{2,1,0:T(8,128)(2,1)S(1)}, u32[]{:S(2)}, u32[]{:S(2)}) collective-permute-start(bf16[4,64,768]{2,1,0:T(8,128)(2,1)S(1)} %share.1._), channel_id=1, source_target_pairs={{4,0},{5,1},{2,4},{3,5},{6,2},{7,3},{0,6},{1,7},{12,8},{13,9},{10,... | collective-permute-start | bytes 1179656 | tf_op jit(solution)/shard_map/ppermute | solution.py:358
  8.6 10.8 %collective-permute-start.2 = (s32[1,64]{1,0:T(1,128)S(1)}, s32[1,64]{1,0:T(1,128)S(1)}, u32[]{:S(2)}, u32[]{:S(2)}) collective-permute-start(s32[1,64]{1,0:T(1,128)S(1)} %get-tuple-element.21.refs_0_), channel_id=1, source_target_pairs={{24,0},{0,8},{8,16},{16,24},{25,1},{1,9},{9,17},{17,25},{26,2},{2,... | collective-permute-start | bytes 776 | tf_op jit(solution)/shard_map/ppermute | solution.py:375
  10.2 9.3 %collective-permute-start.1 = (s32[1,64]{1,0:T(1,128)S(1)}, s32[1,64]{1,0:T(1,128)S(1)}, u32[]{:S(2)}, u32[]{:S(2)}) collective-permute-start(s32[1,64]{1,0:T(1,128)S(1)} %get-tuple-element.21.refs_0_), channel_id=1, source_target_pairs={{16,0},{24,8},{0,16},{8,24},{17,1},{25,9},{1,17},{9,25},{18,2},{26... | collective-permute-start | bytes 776 | tf_op jit(solution)/shard_map/ppermute | solution.py:375
  11.7 7.8 %collective-permute-start = (s32[1,64]{1,0:T(1,128)S(1)}, s32[1,64]{1,0:T(1,128)S(1)}, u32[]{:S(2)}, u32[]{:S(2)}) collective-permute-start(s32[1,64]{1,0:T(1,128)S(1)} %get-tuple-element.21.refs_0_), channel_id=1, source_target_pairs={{8,0},{16,8},{24,16},{0,24},{9,1},{17,9},{25,17},{1,25},{10,2},{18... | collective-permute-start | bytes 776 | tf_op jit(solution)/shard_map/ppermute | solution.py:375
  20.4 4.5 %collective-permute-start.4 = (s32[16,128]{1,0:T(8,128)S(1)}, s32[16,128]{1,0:T(8,128)S(1)}, u32[]{:S(2)}, u32[]{:S(2)}) collective-permute-start(s32[16,128]{1,0:T(8,128)S(1)} %get-tuple-element.26), channel_id=1, source_target_pairs={{0,1},{1,0},{2,3},{3,2},{4,5},{5,4},{6,7},{7,6},{8,9},{9,8},{10,11... | collective-permute-start | bytes 24584 | tf_op jit(solution)/shard_map/ppermute | solution.py:421
  20.4 12.0 %collective-permute-start.5 = (s32[8,128]{1,0:T(8,128)S(1)}, s32[8,128]{1,0:T(8,128)S(1)}, u32[]{:S(2)}, u32[]{:S(2)}) collective-permute-start(s32[8,128]{1,0:T(8,128)S(1)} %get-tuple-element.27._), channel_id=1, source_target_pairs={{4,0},{5,1},{2,4},{3,5},{6,2},{7,3},{0,6},{1,7},{12,8},{13,9},{10,... | collective-permute-start | bytes 12296 | tf_op jit(solution)/shard_map/ppermute | solution.py:423

commit v4 on v3

--- a/solution.py
+++ b/solution.py
@@ -57,29 +57,25 @@
     )
 
 
-def project_kernel(own, partner, w_cell, w_mix, w_pool, proj, mixed, mix_in, pool_in, own_in, sems):
+def project_kernel(own, partner, w_cell, w_mix, proj, mixed, own_in, sem):
     columns = own.shape[0]
-    copies = [
-        pltpu.make_async_copy(w_mix, mix_in, sems.at[0]),
-        pltpu.make_async_copy(own, own_in, sems.at[1]),
-        pltpu.make_async_copy(w_pool, pool_in, sems.at[2]),
-    ]
-    for copy in copies:
-        copy.start()
+    copy = pltpu.make_async_copy(own, own_in, sem)
+    copy.start()
     rows = first_projection([partner[...]], w_cell, proj, columns)
-    copies[0].wait()
-    second_projection(rows, mix_in, mixed, columns)
-    copies[1].wait()
+    second_projection(rows, w_mix, mixed, columns)
+    copy.wait()
     rows = first_projection([own_in[...]], w_cell, proj, 0)
-    second_projection(rows, mix_in, mixed, 0)
-    copies[2].wait()
-
-
-def chip_kernel(score_scale, index, rows, proj, mixed, w_pool, _, out, pool_x, pool_y, fields):
+    second_projection(rows, w_mix, mixed, 0)
+
+
+def chip_kernel(score_scale, index, proj, mixed, w_pool, _, out, pool_in, pool_x, pool_y, sem):
+    copy = pltpu.make_async_copy(w_pool, pool_in, sem)
+    copy.start()
     out[...] = jnp.zeros(out.shape, F32)
-    lists = [(index, rows, 0)]
+    lists = [(index, 0)]
     attend_lists(lists, 0, proj, mixed, score_scale, pool_x, pool_y)
-    score_lists(lists, w_pool, out, pool_x, pool_y, fields)
+    copy.wait()
+    score_lists(lists, pool_in, out, pool_x, pool_y)
 
 
 def attend_pairs(pairs, proj, mixed, score_scale):
@@ -111,32 +107,41 @@
     return pooled
 
 
-def lists_of(held, index, rows):
-    return [(i, r, 8 * at) for i, r, number in zip(index, rows, held) for at in range(number)]
+def lists_of(held, index):
+    return [(ref, 8 * at) for ref, number in zip(index, held) for at in range(number)]
 
 
 def near_kernel(chips, base, held, score_scale, *refs):
     count = len(held)
-    index, remote = refs[:count], refs[count : count + chips]
-    w_cell, w_mix, _, _, proj, mixed, pool_x, pool_y = refs[count + chips :]
+    lists, remote = refs[:count], refs[count : count + chips]
+    w_cell, w_mix, _, _, proj, mixed, pool_x, pool_y = refs[count + chips : -1 - count]
+    index, sems = refs[-1 - count : -1], refs[-1]
+    copies = [
+        pltpu.make_async_copy(ref, held_in, sems.at[i])
+        for i, (ref, held_in) in enumerate(zip(lists, index))
+    ]
+    for copy in copies:
+        copy.start()
     rows = first_projection([ref[...] for ref in remote], w_cell, proj, base)
     second_projection(rows, w_mix, mixed, base)
-    attend_lists(lists_of(held, index, index), 0, proj, mixed, score_scale, pool_x, pool_y)
+    for copy in copies:
+        copy.wait()
+    attend_lists(lists_of(held, index), 0, proj, mixed, score_scale, pool_x, pool_y)
 
 
 def far_kernel(held, near, score_scale, *refs):
     count = len(held)
-    index, rows = refs[:count], refs[count : 2 * count]
-    proj, mixed, w_pool, before, _, _, out, pool_x, pool_y, fields = refs[2 * count :]
-    lists = lists_of(held, index, rows)
+    index = refs[:count]
+    proj, mixed, w_pool, before, _, _, out, pool_x, pool_y = refs[count:]
+    lists = lists_of(held, index)
+    attend_lists(lists, near, proj, mixed, score_scale, pool_x, pool_y)
     out[...] = before[...]
-    attend_lists(lists, near, proj, mixed, score_scale, pool_x, pool_y)
-    score_lists(lists, w_pool, out, pool_x, pool_y, fields)
+    score_lists(lists, w_pool, out, pool_x, pool_y)
 
 
 def starts_of(lists):
     starts = [0]
-    for ref, _, row in lists:
+    for ref, row in lists:
         starts.append(starts[-1] + ref[row + TOTAL, 0])
     return starts
 
@@ -145,20 +150,25 @@
     lanes = lists[0][0].shape[1]
     starts = starts_of(lists)
     todo = list(zip(lists, starts))[done:]
+    lane = lax.broadcasted_iota(jnp.int32, (1, LANES), 1)
 
     def column(at):
-        x = y = 0
-        for (ref, _, row), start in todo:
+        found = [0, 0, 0, 0]
+        for (ref, row), start in todo:
             here = jnp.clip(at - start, 0, lanes - 1)
-            x = jnp.where(at >= start, ref[row + IX, here], x)
-            y = jnp.where(at >= start, ref[row + IY, here], y)
-        return x, y
+            found = [
+                jnp.where(at >= start, ref[row + field, here], value)
+                for field, value in zip((IX, IY, READER, SLOT), found)
+            ]
+        return found
 
     def step(first, size, i, carry):
         at = [first + i * size + u for u in range(size)]
-        pooled = attend_pairs([column(p) for p in at], proj, mixed, score_scale)
-        for p, (row_x, row_y) in zip(at, pooled):
-            pool_x[pl.ds(p, 1)] = row_x
+        columns = [column(p) for p in at]
+        pooled = attend_pairs([(x, y) for x, y, _, _ in columns], proj, mixed, score_scale)
+        for p, (_, _, reader, slot), (row_x, row_y) in zip(at, columns, pooled):
+            tag = jnp.where(lane == 0, reader, slot).astype(F32)
+            pool_x[pl.ds(p, 1)] = jnp.concatenate([row_x, tag], axis=1)
             pool_y[pl.ds(p, 1)] = row_y
         return carry
 
@@ -176,43 +186,31 @@
         first = first + size * count
 
 
-def score_lists(lists, w_pool, out, pool_x, pool_y, fields):
-    starts = starts_of(lists)
-    total = starts[-1]
-    lanes, capacity = lists[0][0].shape[1], fields.shape[1]
-    lane = lax.broadcasted_iota(jnp.int32, fields.shape, 1)
-    joined = jnp.zeros(fields.shape, jnp.int32)
-    for (_, ref, row), start in zip(lists, starts):
-        wide = [ref[row : row + 8]] + [jnp.zeros((8, lanes), jnp.int32)] * (capacity // lanes - 1)
-        wide = jnp.concatenate(wide, axis=1) if len(wide) > 1 else wide[0]
-        joined = jnp.where(lane >= start, pltpu.roll(wide, start, 1), joined)
-    fields[...] = joined
-    block = LANES
+def score_lists(lists, w_pool, out, pool_x, pool_y):
+    total = starts_of(lists)[-1]
+    block = LANES // 2
+    width = w_pool.shape[0]
     readers, slots = out.shape
 
     def step(i, carry):
         here = pl.ds(pl.multiple_of(i * block, block), block)
-        z = dot(jnp.concatenate([pool_x[here], pool_y[here]], axis=0).astype(BF16), w_pool[...])
+        pooled = jnp.concatenate([pool_x[here, :width], pool_y[here]], axis=0).astype(BF16)
+        z = dot(pooled, w_pool[...])
         zx, zy = z[:block], z[block:]
         inner = jnp.mean(zx * zy, axis=1, keepdims=True)
         norms = (jnp.mean(zx * zx, axis=1, keepdims=True) + EPSILON) * (
             jnp.mean(zy * zy, axis=1, keepdims=True) + EPSILON
         )
         score = inner / jnp.sqrt(norms) / SOFTMAX_WARMTH
-        score = jnp.transpose(jnp.broadcast_to(score, (block, block)))[:1]
-        field = fields[:, here]
-        live = (field[VALID : VALID + 1] > 0) & (
-            lax.broadcasted_iota(jnp.int32, (1, block), 1) < total - i * block
-        )
+        live = lax.broadcasted_iota(jnp.int32, (block, 1), 0) < total - i * block
+        tags = jnp.where(live, pool_x[here, width:], -1.0).astype(jnp.int32)
         score = jnp.where(live, score, 0.0)
-        of_reader = field[READER : READER + 1] == lax.broadcasted_iota(
-            jnp.int32, (readers, block), 0
-        )
-        of_slot = field[SLOT : SLOT + 1] == lax.broadcasted_iota(jnp.int32, (slots, block), 0)
+        of_reader = tags[:, :1] == lax.broadcasted_iota(jnp.int32, (block, readers), 1)
+        of_slot = tags[:, 1:2] == lax.broadcasted_iota(jnp.int32, (block, slots), 1)
         out[...] += lax.dot_general(
             jnp.where(of_reader, score, 0.0),
             of_slot.astype(F32),
-            NT,
+            (((0,), (0,)), ((), ())),
             preferred_element_type=F32,
             precision=lax.Precision.HIGHEST,
         )
@@ -228,13 +226,15 @@
     copy.wait()
 
 
-def prepare_kernel(sizes, pairs, counts, w_cell, _, ids, own_list, cell_in, held, sems):
+def prepare_kernel(sizes, pairs, counts, w_cell, w_mix, _, ids, own_list, cell_in, mix_in, held, sems):
     lines, shards, per_shard, pair_dev = sizes
     line, shard = lax.axis_index("grp"), lax.axis_index("shard")
     copy_cell = pltpu.make_async_copy(w_cell, cell_in, sems.at[0])
     copy_pairs = pltpu.make_async_copy(pairs, held, sems.at[1])
+    copy_mix = pltpu.make_async_copy(w_mix, mix_in, sems.at[2])
     copy_pairs.start()
     copy_cell.start()
+    copy_mix.start()
     copy_pairs.wait()
     slot = lax.broadcasted_iota(jnp.int32, ids.shape, 1)
     a, b = held[:1], held[1:]
@@ -246,6 +246,7 @@
     reader = jnp.full_like(slot, line * shards + shard)
     own_list[...] = pack_list(mine, (x, y, reader, slot), own_list.shape[1])
     copy_cell.wait()
+    copy_mix.wait()
 
 
 def pack_list(mine, values, lanes):
@@ -358,19 +359,20 @@
     remote = {d: lax.ppermute(share, "shard", from_ahead(d)) for d in offsets}
     cells, _ = lax.optimization_barrier((cells, share))
     partner = lax.ppermute(cells, "shard", swap)
-    ids, own_list, w_cell = pl.pallas_call(
+    ids, own_list, w_cell, w_mix = pl.pallas_call(
         functools.partial(prepare_kernel, sizes),
         out_shape=(
             jax.ShapeDtypeStruct((1, pair_dev), jnp.int32),
             jax.ShapeDtypeStruct((8, lanes), jnp.int32),
             weight,
+            weight,
         ),
-        in_specs=[hbm(), smem(), hbm(), pl.BlockSpec(memory_space=pl.ANY)],
-        out_specs=[vmem()] * 3,
-        scratch_shapes=[pltpu.VMEM((2, pair_dev), jnp.int32), pltpu.SemaphoreType.DMA((2,))],
-        compiler_params=pltpu.CompilerParams(vmem_limit_bytes=weight_bytes + 4 * 2**20),
+        in_specs=[hbm(), smem(), hbm(), hbm(), pl.BlockSpec(memory_space=pl.ANY)],
+        out_specs=[vmem()] * 4,
+        scratch_shapes=[pltpu.VMEM((2, pair_dev), jnp.int32), pltpu.SemaphoreType.DMA((3,))],
+        compiler_params=pltpu.CompilerParams(vmem_limit_bytes=2 * weight_bytes + 4 * 2**20),
         name="prepare",
-    )(in_hbm(pairs.T), counts, in_hbm(w_cell), share)
+    )(in_hbm(pairs.T), counts, in_hbm(w_cell), in_hbm(w_mix), share)
     ids = [ids] + [
         lax.ppermute(ids, "grp", [((g + k) % lines, g) for g in range(lines)])
         for k in range(1, lines)
@@ -381,23 +383,24 @@
     store_bytes = 2 * math.prod(store.shape)
     weight_bytes = 2 * width * width
 
-    def pool(count):
-        return jax.ShapeDtypeStruct((count * lanes + STEPS[0], width), F32)
+    def pools(count):
+        rows = count * lanes + LANES
+        return [jax.ShapeDtypeStruct((rows, n), F32) for n in (width + LANES, width)]
 
     def limit(spare):
         return pltpu.CompilerParams(
             vmem_limit_bytes=2 * store_bytes + 3 * weight_bytes + spare * 2**20
         )
 
-    proj, mixed, w_mix, w_pool = pl.pallas_call(
+    proj, mixed = pl.pallas_call(
         project_kernel,
-        out_shape=[store, store, weight, weight],
-        in_specs=[hbm(), vmem(), vmem(), hbm(), hbm()],
-        out_specs=[vmem()] * 4,
-        scratch_shapes=[pltpu.VMEM(cells.shape, BF16), pltpu.SemaphoreType.DMA((3,))],
+        out_shape=[store, store],
+        in_specs=[hbm()] + [vmem()] * 3,
+        out_specs=[vmem()] * 2,
+        scratch_shapes=[pltpu.VMEM(cells.shape, BF16), pltpu.SemaphoreType.DMA(())],
         compiler_params=limit(16),
         name="project",
-    )(in_hbm(cells), partner, w_cell, in_hbm(w_mix), in_hbm(w_pool))
+    )(in_hbm(cells), partner, w_cell, w_mix)
 
     groups = [offsets[i : i + 2] for i in range(0, len(offsets), 2)]
     whose, spans = [], []
@@ -423,26 +426,25 @@
             packed = lax.ppermute(packed, "shard", from_ahead(d))
         arrived.append(packed)
 
-    out = pl.pallas_call(
+    out, w_pool = pl.pallas_call(
         functools.partial(chip_kernel, score_scale),
-        out_shape=scores,
-        in_specs=[smem()] + [vmem()] * 4 + [pl.BlockSpec(memory_space=pl.ANY)],
-        out_specs=vmem(),
+        out_shape=[scores, weight],
+        in_specs=[smem(), vmem(), vmem(), hbm(), pl.BlockSpec(memory_space=pl.ANY)],
+        out_specs=[vmem()] * 2,
         scratch_shapes=[
-            pltpu.VMEM(pool(1).shape, F32),
-            pltpu.VMEM(pool(1).shape, F32),
-            pltpu.VMEM((8, lanes), jnp.int32),
+            *(pltpu.VMEM(x.shape, F32) for x in pools(1)),
+            pltpu.SemaphoreType.DMA(()),
         ],
         compiler_params=limit(16),
         name="chip",
-    )(own_list, own_list, proj, mixed, w_pool, lists[-1])
+    )(own_list, proj, mixed, in_hbm(w_pool), lists[-1])
 
     for group, (first, middle, last) in zip(groups, spans):
         use = arrived[first:last]
         held = [x.shape[0] // 8 for x in use]
         number = middle - first
         at = number + len(group) + 2
-        proj, mixed, pool_x, pool_y = pl.pallas_call(
+        proj, mixed, *pooled = pl.pallas_call(
             functools.partial(
                 near_kernel,
                 len(group),
@@ -450,24 +452,27 @@
                 held[:number],
                 score_scale,
             ),
-            out_shape=(store, store, pool(sum(held)), pool(sum(held))),
-            in_specs=[smem()] * number + [vmem()] * (len(group) + 4),
+            out_shape=[store, store, *pools(sum(held))],
+            in_specs=[vmem()] * (number + len(group) + 4),
             out_specs=[vmem()] * 4,
             input_output_aliases={at: 0, at + 1: 1},
+            scratch_shapes=[
+                *(pltpu.SMEM(x.shape, jnp.int32) for x in use[:number]),
+                pltpu.SemaphoreType.DMA((number,)),
+            ],
             compiler_params=limit(20),
             name="near" + "_".join(map(str, group)),
         )(*use[:number], *(remote[d] for d in group), w_cell, w_mix, proj, mixed)
-        at = 2 * len(use) + 3
+        at = len(use) + 3
         out, *_ = pl.pallas_call(
             functools.partial(far_kernel, held, sum(held[:number]), score_scale),
-            out_shape=(scores, pool(sum(held)), pool(sum(held))),
-            in_specs=[smem()] * len(use) + [vmem()] * (len(use) + 6),
+            out_shape=[scores, *pools(sum(held))],
+            in_specs=[smem()] * len(use) + [vmem()] * 6,
             out_specs=[vmem()] * 3,
             input_output_aliases={at: 0, at + 1: 1, at + 2: 2},
-            scratch_shapes=[pltpu.VMEM((8, sum(held) * lanes), jnp.int32)],
             compiler_params=limit(20),
             name="far" + "_".join(map(str, group)),
-        )(*use, *use, proj, mixed, w_pool, out, pool_x, pool_y)
+        )(*use, proj, mixed, w_pool, out, *pooled)
 
     back = lax.all_to_all(out, ("grp", "shard"), 0, 0, tiled=True)
     return jnp.sum(back, axis=0)

time: 46.7 us -> 45.7 us (0.979)
  Pallas kernels: 24.1 us -> 19.9 us
  blocking collectives: 9.74 us -> 12.4 us
  waiting for transfers between devices: 0.72 us -> 1.27 us
    pallas_call x1, Pallas kernels: 7.48 us -> 4.8 us  [local(): pl.pallas_call(functools.partial(near_kernel, len(group), 2 * per_shard +...]
    all_to_all x1, blocking collectives: 9.74 us -> 12.4 us  [local(): back = lax.all_to_all(out, ('grp', 'shard'), 0, 0, tiled=True)]
    pallas_call x1, Pallas kernels: 3.73 us -> 2.74 us  [local(): pl.pallas_call(functools.partial(far_kernel, held, sum(held[:number]), sc...]
    pallas_call x2, Pallas kernels: 9.7 us -> 8.81 us  [the longest x1 5.47 us: local(): pl.pallas_call(project_kernel, out_shape=[store, store], in_specs=[hbm()]...]
    ppermute x2, waiting for transfers between devices: 0.7 us -> 1.26 us  [local(): remote = {d: lax.ppermute(share, 'shard', from_ahead(d)) for d in offsets}]
  transfers between devices with their start and end apart: 8 -> 8, of which waited for: 1 -> 1; matrix products, arithmetic and copies ran while one was open for 0% -> 0% of each run, Pallas kernels for 42% -> 36%
where the time goes in v4:
time: 45.7 us; the launch traced here: 45.4 us
  Pallas kernels  19.9 us (44%)
  blocking collectives  12.4 us (27%)
  starting transfers between devices  10.5 us (23%)
  waiting for transfers between devices  1.27 us (3%)
  between operations  0.74 us (2%)
  other arithmetic  0.56 us (1%)
    all_to_all x1, blocking collectives, local(): back = lax.all_to_all(out, ('grp', 'shard'), 0, 0, tiled=True)  12.4 us
    pallas_call x1, Pallas kernels, local(): pl.pallas_call(project_kernel, out_shape=[store, store], in_specs=[hbm()]...  5.47 us
    ppermute x2, starting transfers between devices, local(): remote = {d: lax.ppermute(share, 'shard', from_ahead(d)) for d in offsets}  5.13 us
    pallas_call x1, Pallas kernels, local(): pl.pallas_call(functools.partial(near_kernel, len(group), 2 * per_shard +...  4.8 us
    ppermute x3, starting transfers between devices, local(): lax.ppermute(ids, 'grp', [((g + k) % lines, g) for g in range(lines)])  4.5 us
    pallas_call x1, Pallas kernels, local(): pl.pallas_call(functools.partial(chip_kernel, score_scale), out_shape=[sc...  3.34 us
    pallas_call x1, Pallas kernels, local(): pl.pallas_call(functools.partial(far_kernel, held, sum(held[:number]), sc...  2.74 us
    pallas_call x1, Pallas kernels, local(): pl.pallas_call(functools.partial(prepare_kernel, sizes), out_shape=(jax.S...  1.67 us
  transfers between devices with their start and end apart: 8, of which 1 were waited for; matrix products, arithmetic and copies ran while one was open for 0% of the time, Pallas kernels for 36%

profile of v4, /device:TPU:0, one launch (start us, length us, event | category | flops | bytes accessed | tf_op | source)
XLA Modules:
  0.0 45.4 jit_solution(2091586682000046598)
XLA Ops:
  0.0 1.0 %share.1._ = bf16[4,64,768]{2,1,0:T(8,128)(2,1)S(1)} custom-call(bf16[16,64,768]{2,1,0:T(8,128)(2,1)} %own), custom_call_target="tpu_custom_call" | custom-call | tf_op jit(solution)/shard_map/share/pallas_call | solution.py:350
  1.0 0.5 %collective-permute-start.3 = (bf16[16,64,768]{2,1,0:T(8,128)(2,1)}, bf16[16,64,768]{2,1,0:T(8,128)(2,1)S(1)}, u32[]{:S(2)}, u32[]{:S(2)}) collective-permute-start(bf16[16,64,768]{2,1,0:T(8,128)(2,1)} %own), channel_id=1, source_target_pairs={{0,1},{1,0},{2,3},{3,2},{4,5},{5,4},{6,7},{7,6},{8,9},{9,8},{10,11... | collective-permute-start | bytes 4718600 | tf_op jit(solution)/shard_map/ppermute | solution.py:361
  1.5 2.7 %collective-permute-start.7 = (bf16[4,64,768]{2,1,0:T(8,128)(2,1)S(1)}, bf16[4,64,768]{2,1,0:T(8,128)(2,1)S(1)}, u32[]{:S(2)}, u32[]{:S(2)}) collective-permute-start(bf16[4,64,768]{2,1,0:T(8,128)(2,1)S(1)} %share.1._), channel_id=1, source_target_pairs={{2,0},{3,1},{6,4},{7,5},{0,2},{1,3},{4,6},{5,7},{10,8},{11,9},{14,... | collective-permute-start | bytes 1179656 | tf_op jit(solution)/shard_map/ppermute | solution.py:359
  4.2 2.5 %collective-permute-start.6 = (bf16[4,64,768]{2,1,0:T(8,128)(2,1)S(1)}, bf16[4,64,768]{2,1,0:T(8,128)(2,1)S(1)}, u32[]{:S(2)}, u32[]{:S(2)}) collective-permute-start(bf16[4,64,768]{2,1,0:T(8,128)(2,1)S(1)} %share.1._), channel_id=1, source_target_pairs={{4,0},{5,1},{2,4},{3,5},{6,2},{7,3},{0,6},{1,7},{12,8},{13,9},{10,... | collective-permute-start | bytes 1179656 | tf_op jit(solution)/shard_map/ppermute | solution.py:359
  7.3 1.7 %prepare.1 = (s32[1,64]{1,0:T(1,128)S(1)}, s32[8,128]{1,0:T(8,128)S(1)}, bf16[768,768]{1,0:T(8,128)(2,1)S(1)}, bf16[768,768]{1,0:T(8,128)(2,1)S(1)}) custom-call(s32[2,64]{1,0:T(2,128)} %bitcast.5, s32[1]{0:T(128)S(6)} %copy.18.counts, bf16[768,768]{1,0:T(8,128)(2,1)} %w_cell.1, bf16[768,768]{1,0:T(8,128)(2,1)} %w_mix.1, bf16[4,64,768]{2,1,0:T(8,128)(2,1)S(1)} %share.1._), custom_call_target="tpu_custom_call" | custom-call | tf_op jit(solution)/shard_map/prepare/pallas_call | solution.py:362
  9.0 1.5 %collective-permute-start.2 = (s32[1,64]{1,0:T(1,128)S(1)}, s32[1,64]{1,0:T(1,128)S(1)}, u32[]{:S(2)}, u32[]{:S(2)}) collective-permute-start(s32[1,64]{1,0:T(1,128)S(1)} %get-tuple-element.22.refs_0_), channel_id=1, source_target_pairs={{24,0},{0,8},{8,16},{16,24},{25,1},{1,9},{9,17},{17,25},{26,2},{2,... | collective-permute-start | bytes 776 | tf_op jit(solution)/shard_map/ppermute | solution.py:377
  10.5 1.5 %collective-permute-start.1 = (s32[1,64]{1,0:T(1,128)S(1)}, s32[1,64]{1,0:T(1,128)S(1)}, u32[]{:S(2)}, u32[]{:S(2)}) collective-permute-start(s32[1,64]{1,0:T(1,128)S(1)} %get-tuple-element.22.refs_0_), channel_id=1, source_target_pairs={{16,0},{24,8},{0,16},{8,24},{17,1},{25,9},{1,17},{9,25},{18,2},{26... | collective-permute-start | bytes 776 | tf_op jit(solution)/shard_map/ppermute | solution.py:377
  12.1 0.0 collective-permute-done.3.partner
  12.1 1.4 %collective-permute-start = (s32[1,64]{1,0:T(1,128)S(1)}, s32[1,64]{1,0:T(1,128)S(1)}, u32[]{:S(2)}, u32[]{:S(2)}) collective-permute-start(s32[1,64]{1,0:T(1,128)S(1)} %get-tuple-element.22.refs_0_), channel_id=1, source_target_pairs={{8,0},{16,8},{24,16},{0,24},{9,1},{17,9},{25,17},{1,25},{10,2},{18... | collective-permute-start | bytes 776 | tf_op jit(solution)/shard_map/ppermute | solution.py:377
  13.5 5.5 %project.1 = (bf16[40,64,768]{2,1,0:T(8,128)(2,1)S(1)}, bf16[40,64,768]{2,1,0:T(8,128)(2,1)S(1)}) custom-call(bf16[16,64,768]{2,1,0:T(8,128)(2,1)} %own, bf16[16,64,768]{2,1,0:T(8,128)(2,1)S(1)} %collective-permute-done.3.partner, bf16[768,768]{1,0:T(8,128)(2,1)S(1)} %get-tuple-element.24.w_cell.refs_4_, bf16[768,768]{1,0:T(8,128)(2,1)S(1)} %get-tuple-element.25.w_mix.refs_5_), custom_call_target="tpu_custom_call" | custom-call | tf_op jit(solution)/shard_map/project/pallas_call | solution.py:395
  19.0 0.0 collective-permute-done.2.refs_3_
  19.0 0.0 collective-permute-done.1.refs_2_
  19.0 0.0 collective-permute-done.refs_1_
  19.0 0.9 %route.1 = (s32[16,128]{1,0:T(8,128)S(1)}, s32[16,128]{1,0:T(8,128)S(1)}, s32[8,128]{1,0:T(8,128)S(1)}) custom-call(s32[1,64]{1,0:T(1,128)S(1)} %get-tuple-element.22.refs_0_, s32[1,64]{1,0:T(1,128)S(1)} %collective-permute-done.refs_1_, s32[1,64]{1,0:T(1,128)S(1)} %collective-permute-done.1.refs_2_, s32[1,64]{1,0:T(1,128)S(1)} %collective-permute-done.2.refs_3_, ...), custom_call_target="tpu_custom_call" | custom-call | tf_op jit(solution)/shard_map/route/pallas_call | solution.py:412
  19.9 0.0 collective-permute-start.4
  19.9 0.4 collective-permute-start.5
  20.3 3.3 %chip.1 = (f32[32,64]{1,0:T(8,128)S(1)}, bf16[768,768]{1,0:T(8,128)(2,1)S(1)}) custom-call(s32[8,128]{1,0:T(8,128)S(1)} %get-tuple-element.33.index, bf16[40,64,768]{2,1,0:T(8,128)(2,1)S(1)} %get-tuple-element.26.refs_4_.refs_6_.proj, bf16[40,64,768]{2,1,0:T(8,128)(2,1)S(1)} %get-tuple-element.30.refs_7_.mixed, bf16[768,768]{1,0:T(8,128)(2,1)} %w_pool.1, ...), custom_call_target="tpu_custom_call" | custom-call | tf_op jit(solution)/shard_map/chip/pallas_call | solution.py:429
  23.6 0.0 collective-permute-done.7.refs_3_
  23.6 1.3 %collective-permute-done.6.refs_2_ = bf16[4,64,768]{2,1,0:T(8,128)(2,1)S(1)} collective-permute-done((bf16[4,64,768]{2,1,0:T(8,128)(2,1)S(1)}, bf16[4,64,768]{2,1,0:T(8,128)(2,1)S(1)}, u32[]{:S(2)}, u32[]{:S(2)}) %collective-permute-start.6) | collective-permute-done | bytes 393248 | tf_op jit(solution)/shard_map/ppermute | solution.py:359
  24.9 0.0 collective-permute-done.4.refs_1_
  24.9 4.8 %near1_2.1 = (bf16[40,64,768]{2,1,0:T(8,128)(2,1)S(1)}, bf16[40,64,768]{2,1,0:T(8,128)(2,1)S(1)}, f32[768,896]{1,0:T(8,128)S(1)}, f32[768,768]{1,0:T(8,128)S(1)}) custom-call(s32[16,128]{1,0:T(8,128)S(1)} %get-tuple-element.27.refs_0_, s32[16,128]{1,0:T(8,128)S(1)} %collective-permute-done.4.refs_1_, ...), custom_call_target="tpu_custom_call", output_to_operand_aliasing={{0}: (6, {}), {1}: (7, {})} | custom-call | tf_op jit(solution)/shard_map/near1_2/pallas_call | solution.py:447
  29.7 0.0 collective-permute-done.5.refs_2_
  29.7 2.7 %far1_2.1 = (f32[32,64]{1,0:T(8,128)S(1)}, f32[768,896]{1,0:T(8,128)S(1)}, f32[768,768]{1,0:T(8,128)S(1)}) custom-call(s32[16,128]{1,0:T(8,128)S(1)} %get-tuple-element.27.refs_0_, s32[16,128]{1,0:T(8,128)S(1)} %collective-permute-done.4.refs_1_, ...), custom_call_target="tpu_custom_call", output_to_operand_aliasing={{0}: (6, {}), {1}: (7, {}), {2}: (8, {})} | custom-call | tf_op jit(solution)/shard_map/far1_2/pallas_call | solution.py:467
  32.4 12.4 %all_to_all.9 = f32[32,1,64]{2,1,0:T(1,128)S(1)} all-to-all(f32[32,1,64]{2,1,0:T(1,128)S(1)} %bitcast.4), channel_id=1, replica_groups=mesh['grp'=4,'shard'=8] {'grp','shard'}, dimensions={0} | all-to-all | bytes 16384 | tf_op jit(solution)/shard_map/all_to_all | solution.py:477
  44.8 0.6 %reduce_sum.9 = f32[64]{0:T(128)} reduce(f32[32,1,64]{2,1,0:T(1,128)S(1)} %all_to_all.9, f32[]{:T(128)} %constant.0.clone.1), dimensions={0,1}, to_apply=%region_0.0 | reduce | flops 1984 | bytes 8452 | tf_op jit(solution)/shard_map/reduce_sum | solution.py:478
Async XLA Ops:
  1.0 11.0 %collective-permute-start.3 = (bf16[16,64,768]{2,1,0:T(8,128)(2,1)}, bf16[16,64,768]{2,1,0:T(8,128)(2,1)S(1)}, u32[]{:S(2)}, u32[]{:S(2)}) collective-permute-start(bf16[16,64,768]{2,1,0:T(8,128)(2,1)} %own), channel_id=1, source_target_pairs={{0,1},{1,0},{2,3},{3,2},{4,5},{5,4},{6,7},{7,6},{8,9},{9,8},{10,11... | collective-permute-start | bytes 4718600 | tf_op jit(solution)/shard_map/ppermute | solution.py:361
  1.5 22.1 %collective-permute-start.7 = (bf16[4,64,768]{2,1,0:T(8,128)(2,1)S(1)}, bf16[4,64,768]{2,1,0:T(8,128)(2,1)S(1)}, u32[]{:S(2)}, u32[]{:S(2)}) collective-permute-start(bf16[4,64,768]{2,1,0:T(8,128)(2,1)S(1)} %share.1._), channel_id=1, source_target_pairs={{2,0},{3,1},{6,4},{7,5},{0,2},{1,3},{4,6},{5,7},{10,8},{11,9},{14,... | collective-permute-start | bytes 1179656 | tf_op jit(solution)/shard_map/ppermute | solution.py:359
  4.2 20.7 %collective-permute-start.6 = (bf16[4,64,768]{2,1,0:T(8,128)(2,1)S(1)}, bf16[4,64,768]{2,1,0:T(8,128)(2,1)S(1)}, u32[]{:S(2)}, u32[]{:S(2)}) collective-permute-start(bf16[4,64,768]{2,1,0:T(8,128)(2,1)S(1)} %share.1._), channel_id=1, source_target_pairs={{4,0},{5,1},{2,4},{3,5},{6,2},{7,3},{0,6},{1,7},{12,8},{13,9},{10,... | collective-permute-start | bytes 1179656 | tf_op jit(solution)/shard_map/ppermute | solution.py:359
  9.0 10.0 %collective-permute-start.2 = (s32[1,64]{1,0:T(1,128)S(1)}, s32[1,64]{1,0:T(1,128)S(1)}, u32[]{:S(2)}, u32[]{:S(2)}) collective-permute-start(s32[1,64]{1,0:T(1,128)S(1)} %get-tuple-element.22.refs_0_), channel_id=1, source_target_pairs={{24,0},{0,8},{8,16},{16,24},{25,1},{1,9},{9,17},{17,25},{26,2},{2,... | collective-permute-start | bytes 776 | tf_op jit(solution)/shard_map/ppermute | solution.py:377
  10.5 8.4 %collective-permute-start.1 = (s32[1,64]{1,0:T(1,128)S(1)}, s32[1,64]{1,0:T(1,128)S(1)}, u32[]{:S(2)}, u32[]{:S(2)}) collective-permute-start(s32[1,64]{1,0:T(1,128)S(1)} %get-tuple-element.22.refs_0_), channel_id=1, source_target_pairs={{16,0},{24,8},{0,16},{8,24},{17,1},{25,9},{1,17},{9,25},{18,2},{26... | collective-permute-start | bytes 776 | tf_op jit(solution)/shard_map/ppermute | solution.py:377
  12.1 6.9 %collective-permute-start = (s32[1,64]{1,0:T(1,128)S(1)}, s32[1,64]{1,0:T(1,128)S(1)}, u32[]{:S(2)}, u32[]{:S(2)}) collective-permute-start(s32[1,64]{1,0:T(1,128)S(1)} %get-tuple-element.22.refs_0_), channel_id=1, source_target_pairs={{8,0},{16,8},{24,16},{0,24},{9,1},{17,9},{25,17},{1,25},{10,2},{18... | collective-permute-start | bytes 776 | tf_op jit(solution)/shard_map/ppermute | solution.py:377
  19.9 5.0 %collective-permute-start.4 = (s32[16,128]{1,0:T(8,128)S(1)}, s32[16,128]{1,0:T(8,128)S(1)}, u32[]{:S(2)}, u32[]{:S(2)}) collective-permute-start(s32[16,128]{1,0:T(8,128)S(1)} %get-tuple-element.28), channel_id=1, source_target_pairs={{0,1},{1,0},{2,3},{3,2},{4,5},{5,4},{6,7},{7,6},{8,9},{9,8},{10,11... | collective-permute-start | bytes 24584 | tf_op jit(solution)/shard_map/ppermute | solution.py:424
  19.9 9.8 %collective-permute-start.5 = (s32[8,128]{1,0:T(8,128)S(1)}, s32[8,128]{1,0:T(8,128)S(1)}, u32[]{:S(2)}, u32[]{:S(2)}) collective-permute-start(s32[8,128]{1,0:T(8,128)S(1)} %get-tuple-element.29._), channel_id=1, source_target_pairs={{4,0},{5,1},{2,4},{3,5},{6,2},{7,3},{0,6},{1,7},{12,8},{13,9},{10,... | collective-permute-start | bytes 12296 | tf_op jit(solution)/shard_map/ppermute | solution.py:426

commit v5 on v4

--- a/solution.py
+++ b/solution.py
@@ -15,7 +15,7 @@
 F32 = jnp.float32
 BF16 = jnp.bfloat16
 NT = (((1,), (1,)), ((), ()))
-IX, IY, READER, SLOT, VALID, TOTAL = range(6)
+CODE_BITS = 8
 
 
 def vmem():
@@ -108,7 +108,17 @@
 
 
 def lists_of(held, index):
-    return [(ref, 8 * at) for ref, number in zip(index, held) for at in range(number)]
+    return [(ref, 2 * at) for ref, number in zip(index, held) for at in range(number)]
+
+
+def start_copies(sources, targets, sems):
+    copies = [
+        pltpu.make_async_copy(source, target, sems.at[i])
+        for i, (source, target) in enumerate(zip(sources, targets))
+    ]
+    for copy in copies:
+        copy.start()
+    return copies
 
 
 def near_kernel(chips, base, held, score_scale, *refs):
@@ -116,51 +126,53 @@
     lists, remote = refs[:count], refs[count : count + chips]
     w_cell, w_mix, _, _, proj, mixed, pool_x, pool_y = refs[count + chips : -1 - count]
     index, sems = refs[-1 - count : -1], refs[-1]
-    copies = [
-        pltpu.make_async_copy(ref, held_in, sems.at[i])
-        for i, (ref, held_in) in enumerate(zip(lists, index))
-    ]
-    for copy in copies:
-        copy.start()
+    copies = start_copies(lists, index, sems)
     rows = first_projection([ref[...] for ref in remote], w_cell, proj, base)
     second_projection(rows, w_mix, mixed, base)
     for copy in copies:
         copy.wait()
-    attend_lists(lists_of(held, index), 0, proj, mixed, score_scale, pool_x, pool_y)
+    attend_lists(lists_of(held, index), 0, proj, mixed, score_scale, pool_x, pool_y, last=False)
 
 
 def far_kernel(held, near, score_scale, *refs):
     count = len(held)
-    index = refs[:count]
-    proj, mixed, w_pool, before, _, _, out, pool_x, pool_y = refs[count:]
-    lists = lists_of(held, index)
-    attend_lists(lists, near, proj, mixed, score_scale, pool_x, pool_y)
+    lists = refs[:count]
+    proj, mixed, w_pool, before, _, _, out, pool_x, pool_y = refs[count : -1 - count]
+    index, sems = refs[-1 - count : -1], refs[-1]
+    copies = start_copies(lists, index, sems)
     out[...] = before[...]
-    score_lists(lists, w_pool, out, pool_x, pool_y)
+    for copy in copies:
+        copy.wait()
+    every = lists_of(held, index)
+    attend_lists(every, near, proj, mixed, score_scale, pool_x, pool_y)
+    score_lists(every, w_pool, out, pool_x, pool_y)
 
 
 def starts_of(lists):
     starts = [0]
     for ref, row in lists:
-        starts.append(starts[-1] + ref[row + TOTAL, 0])
+        starts.append(starts[-1] + ref[row + 1, 0])
     return starts
 
 
-def attend_lists(lists, done, proj, mixed, score_scale, pool_x, pool_y):
+def attend_lists(lists, near, proj, mixed, score_scale, pool_x, pool_y, last=True):
     lanes = lists[0][0].shape[1]
     starts = starts_of(lists)
-    todo = list(zip(lists, starts))[done:]
+    todo = list(zip(lists, starts))
     lane = lax.broadcasted_iota(jnp.int32, (1, LANES), 1)
 
     def column(at):
-        found = [0, 0, 0, 0]
+        code = 0
         for (ref, row), start in todo:
             here = jnp.clip(at - start, 0, lanes - 1)
-            found = [
-                jnp.where(at >= start, ref[row + field, here], value)
-                for field, value in zip((IX, IY, READER, SLOT), found)
-            ]
-        return found
+            code = jnp.where(at >= start, ref[row, here], code)
+        mask = 2**CODE_BITS - 1
+        return (
+            code & mask,
+            (code >> CODE_BITS) & mask,
+            (code >> 2 * CODE_BITS) & mask,
+            code >> 3 * CODE_BITS,
+        )
 
     def step(first, size, i, carry):
         at = [first + i * size + u for u in range(size)]
@@ -173,15 +185,15 @@
         return carry
 
     large, middle, small = STEPS
-    left = starts[-1] - starts[done]
-    rest = lax.rem(left, large)
+    first = starts[near] // large * large
+    left = starts[-1] - first
+    rest = lax.rem(left, large) if last else jnp.int32(0)
     counts = (
         left // large + (rest > middle + small).astype(jnp.int32),
         ((rest > small) & (rest <= middle + small)).astype(jnp.int32),
         (((rest > 0) & (rest <= small)) | ((rest > middle) & (rest <= middle + small))).astype(jnp.int32),
     )
-    first = starts[done]
-    for size, count in zip(STEPS, counts):
+    for size, count in zip(STEPS if last else STEPS[:1], counts):
         lax.fori_loop(0, count, functools.partial(step, first, size), 0)
         first = first + size * count
 
@@ -266,12 +278,15 @@
         position = jnp.where(mine[r : r + 1], position, -1)
         total = total + row_total[r : r + 1]
         chosen = (place == position).astype(BF16)
-        fields = jnp.where(field == VALID, 1, 0)
-        for which, value in zip((IX, IY, READER, SLOT), values):
+        fields = jnp.zeros_like(field)
+        for which, value in enumerate(values):
             fields = jnp.where(field == which, value[r : r + 1], fields)
         packed = packed + dot_nt(fields.astype(BF16), chosen)
-    row = lax.broadcasted_iota(jnp.int32, (8, lanes), 0)
-    return jnp.where(row == TOTAL, total, packed).astype(jnp.int32)
+    packed = packed.astype(jnp.int32)
+    code = packed[:1]
+    for which in range(1, len(values)):
+        code = code + packed[which : which + 1] * 2 ** (which * CODE_BITS)
+    return jnp.concatenate([code, jnp.broadcast_to(total, code.shape).astype(jnp.int32)], axis=0)
 
 
 def route_kernel(sizes, whose, *refs):
@@ -311,7 +326,7 @@
                 target = ring_place(chip, chips, -offset)
                 mine = live & (b_chip == target) & (a_local // quarter == line)
                 x, y = b_own, base + a_local - line * quarter
-            out_ref[8 * at : 8 * at + 8] = pack_list(mine, (x, y, reader_id, slot), lanes)
+            out_ref[2 * at : 2 * at + 2] = pack_list(mine, (x, y, reader_id, slot), lanes)
 
 
 def ring_place(chip, chips, offset):
@@ -343,6 +358,8 @@
     offsets = range(1, chips // 2 + 1)
     swap = [(s, s ^ 1) for s in range(shards)]
     sizes = (lines, shards, per_shard, pair_dev)
+    assert max(2 * per_shard + len(offsets) * quarter, lines * shards) <= 2**CODE_BITS
+    assert pair_dev <= 2 ** (31 - 3 * CODE_BITS)
     most = lines * min(pair_dev, 4 * pair_dev // shards)
     lanes = -(-max(most, pair_dev) // LANES) * LANES
     weight = jax.ShapeDtypeStruct(w_cell.shape, BF16)
@@ -363,7 +380,7 @@
         functools.partial(prepare_kernel, sizes),
         out_shape=(
             jax.ShapeDtypeStruct((1, pair_dev), jnp.int32),
-            jax.ShapeDtypeStruct((8, lanes), jnp.int32),
+            jax.ShapeDtypeStruct((2, lanes), jnp.int32),
             weight,
             weight,
         ),
@@ -411,7 +428,7 @@
         whose += near + far
     lists = pl.pallas_call(
         functools.partial(route_kernel, sizes, whose),
-        out_shape=[jax.ShapeDtypeStruct((8 * len(kinds), lanes), jnp.int32) for kinds in whose],
+        out_shape=[jax.ShapeDtypeStruct((2 * len(kinds), lanes), jnp.int32) for kinds in whose],
         in_specs=[vmem()] * lines + [pl.BlockSpec(memory_space=pl.ANY)],
         out_specs=[vmem()] * len(whose),
         compiler_params=pltpu.CompilerParams(vmem_limit_bytes=4 * 2**20),
@@ -441,7 +458,7 @@
 
     for group, (first, middle, last) in zip(groups, spans):
         use = arrived[first:last]
-        held = [x.shape[0] // 8 for x in use]
+        held = [x.shape[0] // 2 for x in use]
         number = middle - first
         at = number + len(group) + 2
         proj, mixed, *pooled = pl.pallas_call(
@@ -467,9 +484,13 @@
         out, *_ = pl.pallas_call(
             functools.partial(far_kernel, held, sum(held[:number]), score_scale),
             out_shape=[scores, *pools(sum(held))],
-            in_specs=[smem()] * len(use) + [vmem()] * 6,
+            in_specs=[vmem()] * (len(use) + 6),
             out_specs=[vmem()] * 3,
             input_output_aliases={at: 0, at + 1: 1, at + 2: 2},
+            scratch_shapes=[
+                *(pltpu.SMEM(x.shape, jnp.int32) for x in use),
+                pltpu.SemaphoreType.DMA((len(use),)),
+            ],
             compiler_params=limit(20),
             name="far" + "_".join(map(str, group)),
         )(*use, proj, mixed, w_pool, out, *pooled)

time: 45.7 us -> 45 us (0.985)
  blocking collectives: 12.4 us -> 10.7 us
  Pallas kernels: 19.9 us -> 20.5 us
    pallas_call x1, Pallas kernels: 2.74 us -> 4.54 us  [local(): pl.pallas_call(functools.partial(far_kernel, held, sum(held[:number]), sc...]
    all_to_all x1, blocking collectives: 12.4 us -> 10.7 us  [local(): back = lax.all_to_all(out, ('grp', 'shard'), 0, 0, tiled=True)]
    pallas_call x1, Pallas kernels: 4.8 us -> 3.76 us  [local(): pl.pallas_call(functools.partial(near_kernel, len(group), 2 * per_shard +...]
  transfers between devices with their start and end apart: 8 -> 8, of which waited for: 1 -> 1; matrix products, arithmetic and copies ran while one was open for 0% -> 0% of each run, Pallas kernels for 36% -> 34%
where the time goes in v5:
time: 45 us; the launch traced here: 44.3 us
  Pallas kernels  20.5 us (46%)
  blocking collectives  10.7 us (24%)
  starting transfers between devices  10.6 us (24%)
  waiting for transfers between devices  1.25 us (3%)
  between operations  0.75 us (2%)
  other arithmetic  0.56 us (1%)
    all_to_all x1, blocking collectives, local(): back = lax.all_to_all(out, ('grp', 'shard'), 0, 0, tiled=True)  10.7 us
    pallas_call x1, Pallas kernels, local(): pl.pallas_call(project_kernel, out_shape=[store, store], in_specs=[hbm()]...  5.47 us
    ppermute x2, starting transfers between devices, local(): remote = {d: lax.ppermute(share, 'shard', from_ahead(d)) for d in offsets}  5.13 us
    pallas_call x1, Pallas kernels, local(): pl.pallas_call(functools.partial(far_kernel, held, sum(held[:number]), sc...  4.54 us
    ppermute x3, starting transfers between devices, local(): lax.ppermute(ids, 'grp', [((g + k) % lines, g) for g in range(lines)])  4.5 us
    pallas_call x1, Pallas kernels, local(): pl.pallas_call(functools.partial(near_kernel, len(group), 2 * per_shard +...  3.76 us
    pallas_call x1, Pallas kernels, local(): pl.pallas_call(functools.partial(chip_kernel, score_scale), out_shape=[sc...  3.18 us
    pallas_call x1, Pallas kernels, local(): pl.pallas_call(functools.partial(prepare_kernel, sizes), out_shape=(jax.S...  1.67 us
  transfers between devices with their start and end apart: 8, of which 1 were waited for; matrix products, arithmetic and copies ran while one was open for 0% of the time, Pallas kernels for 34%

profile of v5, /device:TPU:0, one launch (start us, length us, event | category | flops | bytes accessed | tf_op | source)
XLA Modules:
  0.0 44.3 jit_solution(9758070642886167622)
XLA Ops:
  0.0 1.0 %share.1._ = bf16[4,64,768]{2,1,0:T(8,128)(2,1)S(1)} custom-call(bf16[16,64,768]{2,1,0:T(8,128)(2,1)} %own), custom_call_target="tpu_custom_call" | custom-call | tf_op jit(solution)/shard_map/share/pallas_call | solution.py:367
  1.0 0.5 %collective-permute-start.3 = (bf16[16,64,768]{2,1,0:T(8,128)(2,1)}, bf16[16,64,768]{2,1,0:T(8,128)(2,1)S(1)}, u32[]{:S(2)}, u32[]{:S(2)}) collective-permute-start(bf16[16,64,768]{2,1,0:T(8,128)(2,1)} %own), channel_id=1, source_target_pairs={{0,1},{1,0},{2,3},{3,2},{4,5},{5,4},{6,7},{7,6},{8,9},{9,8},{10,11... | collective-permute-start | bytes 4718600 | tf_op jit(solution)/shard_map/ppermute | solution.py:378
  1.5 2.7 %collective-permute-start.7 = (bf16[4,64,768]{2,1,0:T(8,128)(2,1)S(1)}, bf16[4,64,768]{2,1,0:T(8,128)(2,1)S(1)}, u32[]{:S(2)}, u32[]{:S(2)}) collective-permute-start(bf16[4,64,768]{2,1,0:T(8,128)(2,1)S(1)} %share.1._), channel_id=1, source_target_pairs={{2,0},{3,1},{6,4},{7,5},{0,2},{1,3},{4,6},{5,7},{10,8},{11,9},{14,... | collective-permute-start | bytes 1179656 | tf_op jit(solution)/shard_map/ppermute | solution.py:376
  4.2 2.5 %collective-permute-start.6 = (bf16[4,64,768]{2,1,0:T(8,128)(2,1)S(1)}, bf16[4,64,768]{2,1,0:T(8,128)(2,1)S(1)}, u32[]{:S(2)}, u32[]{:S(2)}) collective-permute-start(bf16[4,64,768]{2,1,0:T(8,128)(2,1)S(1)} %share.1._), channel_id=1, source_target_pairs={{4,0},{5,1},{2,4},{3,5},{6,2},{7,3},{0,6},{1,7},{12,8},{13,9},{10,... | collective-permute-start | bytes 1179656 | tf_op jit(solution)/shard_map/ppermute | solution.py:376
  7.3 1.7 %prepare.1 = (s32[1,64]{1,0:T(1,128)S(1)}, s32[2,128]{1,0:T(2,128)S(1)}, bf16[768,768]{1,0:T(8,128)(2,1)S(1)}, bf16[768,768]{1,0:T(8,128)(2,1)S(1)}) custom-call(s32[2,64]{1,0:T(2,128)} %bitcast.5, s32[1]{0:T(128)S(6)} %copy.18.counts, bf16[768,768]{1,0:T(8,128)(2,1)} %w_cell.1, bf16[768,768]{1,0:T(8,128)(2,1)} %w_mix.1, bf16[4,64,768]{2,1,0:T(8,128)(2,1)S(1)} %share.1._), custom_call_target="tpu_custom_call" | custom-call | tf_op jit(solution)/shard_map/prepare/pallas_call | solution.py:379
  9.0 1.5 %collective-permute-start.2 = (s32[1,64]{1,0:T(1,128)S(1)}, s32[1,64]{1,0:T(1,128)S(1)}, u32[]{:S(2)}, u32[]{:S(2)}) collective-permute-start(s32[1,64]{1,0:T(1,128)S(1)} %get-tuple-element.22.refs_0_), channel_id=1, source_target_pairs={{24,0},{0,8},{8,16},{16,24},{25,1},{1,9},{9,17},{17,25},{26,2},{2,... | collective-permute-start | bytes 776 | tf_op jit(solution)/shard_map/ppermute | solution.py:394
  10.5 1.5 %collective-permute-start.1 = (s32[1,64]{1,0:T(1,128)S(1)}, s32[1,64]{1,0:T(1,128)S(1)}, u32[]{:S(2)}, u32[]{:S(2)}) collective-permute-start(s32[1,64]{1,0:T(1,128)S(1)} %get-tuple-element.22.refs_0_), channel_id=1, source_target_pairs={{16,0},{24,8},{0,16},{8,24},{17,1},{25,9},{1,17},{9,25},{18,2},{26... | collective-permute-start | bytes 776 | tf_op jit(solution)/shard_map/ppermute | solution.py:394
  12.1 0.0 collective-permute-done.3.partner
  12.1 1.4 %collective-permute-start = (s32[1,64]{1,0:T(1,128)S(1)}, s32[1,64]{1,0:T(1,128)S(1)}, u32[]{:S(2)}, u32[]{:S(2)}) collective-permute-start(s32[1,64]{1,0:T(1,128)S(1)} %get-tuple-element.22.refs_0_), channel_id=1, source_target_pairs={{8,0},{16,8},{24,16},{0,24},{9,1},{17,9},{25,17},{1,25},{10,2},{18... | collective-permute-start | bytes 776 | tf_op jit(solution)/shard_map/ppermute | solution.py:394
  13.5 5.5 %project.1 = (bf16[40,64,768]{2,1,0:T(8,128)(2,1)S(1)}, bf16[40,64,768]{2,1,0:T(8,128)(2,1)S(1)}) custom-call(bf16[16,64,768]{2,1,0:T(8,128)(2,1)} %own, bf16[16,64,768]{2,1,0:T(8,128)(2,1)S(1)} %collective-permute-done.3.partner, bf16[768,768]{1,0:T(8,128)(2,1)S(1)} %get-tuple-element.24.w_cell.refs_4_, bf16[768,768]{1,0:T(8,128)(2,1)S(1)} %get-tuple-element.25.w_mix.refs_5_), custom_call_target="tpu_custom_call" | custom-call | tf_op jit(solution)/shard_map/project/pallas_call | solution.py:412
  19.0 0.0 collective-permute-done.2.refs_3_
  19.0 0.0 collective-permute-done.1.refs_2_
  19.0 0.0 collective-permute-done.refs_1_
  19.0 0.9 %route.1 = (s32[4,128]{1,0:T(4,128)S(1)}, s32[4,128]{1,0:T(4,128)S(1)}, s32[2,128]{1,0:T(2,128)S(1)}) custom-call(s32[1,64]{1,0:T(1,128)S(1)} %get-tuple-element.22.refs_0_, s32[1,64]{1,0:T(1,128)S(1)} %collective-permute-done.refs_1_, s32[1,64]{1,0:T(1,128)S(1)} %collective-permute-done.1.refs_2_, s32[1,64]{1,0:T(1,128)S(1)} %collective-permute-done.2.refs_3_, ...), custom_call_target="tpu_custom_call" | custom-call | tf_op jit(solution)/shard_map/route/pallas_call | solution.py:429
  19.9 0.1 collective-permute-start.4
  20.0 0.4 collective-permute-start.5
  20.3 3.2 %chip.1 = (f32[32,64]{1,0:T(8,128)S(1)}, bf16[768,768]{1,0:T(8,128)(2,1)S(1)}) custom-call(s32[2,128]{1,0:T(2,128)S(1)} %get-tuple-element.33.index, bf16[40,64,768]{2,1,0:T(8,128)(2,1)S(1)} %get-tuple-element.26.refs_4_.refs_6_.proj, bf16[40,64,768]{2,1,0:T(8,128)(2,1)S(1)} %get-tuple-element.30.refs_7_.mixed, bf16[768,768]{1,0:T(8,128)(2,1)} %w_pool.1, ...), custom_call_target="tpu_custom_call" | custom-call | tf_op jit(solution)/shard_map/chip/pallas_call | solution.py:446
  23.5 0.0 collective-permute-done.7.refs_3_
  23.5 1.2 %collective-permute-done.6.refs_2_ = bf16[4,64,768]{2,1,0:T(8,128)(2,1)S(1)} collective-permute-done((bf16[4,64,768]{2,1,0:T(8,128)(2,1)S(1)}, bf16[4,64,768]{2,1,0:T(8,128)(2,1)S(1)}, u32[]{:S(2)}, u32[]{:S(2)}) %collective-permute-start.6) | collective-permute-done | bytes 393248 | tf_op jit(solution)/shard_map/ppermute | solution.py:376
  24.8 0.0 collective-permute-done.4.refs_1_
  24.8 3.8 %near1_2.1 = (bf16[40,64,768]{2,1,0:T(8,128)(2,1)S(1)}, bf16[40,64,768]{2,1,0:T(8,128)(2,1)S(1)}, f32[768,896]{1,0:T(8,128)S(1)}, f32[768,768]{1,0:T(8,128)S(1)}) custom-call(s32[4,128]{1,0:T(4,128)S(1)} %get-tuple-element.27.refs_0_, s32[4,128]{1,0:T(4,128)S(1)} %collective-permute-done.4.refs_1_, ...), custom_call_target="tpu_custom_call", output_to_operand_aliasing={{0}: (6, {}), {1}: (7, {})} | custom-call | tf_op jit(solution)/shard_map/near1_2/pallas_call | solution.py:464
  28.5 0.0 collective-permute-done.5.refs_2_
  28.6 4.5 %far1_2.1 = (f32[32,64]{1,0:T(8,128)S(1)}, f32[768,896]{1,0:T(8,128)S(1)}, f32[768,768]{1,0:T(8,128)S(1)}) custom-call(s32[4,128]{1,0:T(4,128)S(1)} %get-tuple-element.27.refs_0_, s32[4,128]{1,0:T(4,128)S(1)} %collective-permute-done.4.refs_1_, ...), custom_call_target="tpu_custom_call", output_to_operand_aliasing={{0}: (6, {}), {1}: (7, {}), {2}: (8, {})} | custom-call | tf_op jit(solution)/shard_map/far1_2/pallas_call | solution.py:484
  33.1 10.7 %all_to_all.9 = f32[32,1,64]{2,1,0:T(1,128)S(1)} all-to-all(f32[32,1,64]{2,1,0:T(1,128)S(1)} %bitcast.4), channel_id=1, replica_groups=mesh['grp'=4,'shard'=8] {'grp','shard'}, dimensions={0} | all-to-all | bytes 16384 | tf_op jit(solution)/shard_map/all_to_all | solution.py:498
  43.8 0.6 %reduce_sum.9 = f32[64]{0:T(128)} reduce(f32[32,1,64]{2,1,0:T(1,128)S(1)} %all_to_all.9, f32[]{:T(128)} %constant.0.clone.1), dimensions={0,1}, to_apply=%region_0.0 | reduce | flops 1984 | bytes 8452 | tf_op jit(solution)/shard_map/reduce_sum | solution.py:499
Async XLA Ops:
  1.0 11.0 %collective-permute-start.3 = (bf16[16,64,768]{2,1,0:T(8,128)(2,1)}, bf16[16,64,768]{2,1,0:T(8,128)(2,1)S(1)}, u32[]{:S(2)}, u32[]{:S(2)}) collective-permute-start(bf16[16,64,768]{2,1,0:T(8,128)(2,1)} %own), channel_id=1, source_target_pairs={{0,1},{1,0},{2,3},{3,2},{4,5},{5,4},{6,7},{7,6},{8,9},{9,8},{10,11... | collective-permute-start | bytes 4718600 | tf_op jit(solution)/shard_map/ppermute | solution.py:378
  1.5 22.0 %collective-permute-start.7 = (bf16[4,64,768]{2,1,0:T(8,128)(2,1)S(1)}, bf16[4,64,768]{2,1,0:T(8,128)(2,1)S(1)}, u32[]{:S(2)}, u32[]{:S(2)}) collective-permute-start(bf16[4,64,768]{2,1,0:T(8,128)(2,1)S(1)} %share.1._), channel_id=1, source_target_pairs={{2,0},{3,1},{6,4},{7,5},{0,2},{1,3},{4,6},{5,7},{10,8},{11,9},{14,... | collective-permute-start | bytes 1179656 | tf_op jit(solution)/shard_map/ppermute | solution.py:376
  4.2 20.6 %collective-permute-start.6 = (bf16[4,64,768]{2,1,0:T(8,128)(2,1)S(1)}, bf16[4,64,768]{2,1,0:T(8,128)(2,1)S(1)}, u32[]{:S(2)}, u32[]{:S(2)}) collective-permute-start(bf16[4,64,768]{2,1,0:T(8,128)(2,1)S(1)} %share.1._), channel_id=1, source_target_pairs={{4,0},{5,1},{2,4},{3,5},{6,2},{7,3},{0,6},{1,7},{12,8},{13,9},{10,... | collective-permute-start | bytes 1179656 | tf_op jit(solution)/shard_map/ppermute | solution.py:376
  9.0 10.0 %collective-permute-start.2 = (s32[1,64]{1,0:T(1,128)S(1)}, s32[1,64]{1,0:T(1,128)S(1)}, u32[]{:S(2)}, u32[]{:S(2)}) collective-permute-start(s32[1,64]{1,0:T(1,128)S(1)} %get-tuple-element.22.refs_0_), channel_id=1, source_target_pairs={{24,0},{0,8},{8,16},{16,24},{25,1},{1,9},{9,17},{17,25},{26,2},{2,... | collective-permute-start | bytes 776 | tf_op jit(solution)/shard_map/ppermute | solution.py:394
  10.5 8.4 %collective-permute-start.1 = (s32[1,64]{1,0:T(1,128)S(1)}, s32[1,64]{1,0:T(1,128)S(1)}, u32[]{:S(2)}, u32[]{:S(2)}) collective-permute-start(s32[1,64]{1,0:T(1,128)S(1)} %get-tuple-element.22.refs_0_), channel_id=1, source_target_pairs={{16,0},{24,8},{0,16},{8,24},{17,1},{25,9},{1,17},{9,25},{18,2},{26... | collective-permute-start | bytes 776 | tf_op jit(solution)/shard_map/ppermute | solution.py:394
  12.1 6.9 %collective-permute-start = (s32[1,64]{1,0:T(1,128)S(1)}, s32[1,64]{1,0:T(1,128)S(1)}, u32[]{:S(2)}, u32[]{:S(2)}) collective-permute-start(s32[1,64]{1,0:T(1,128)S(1)} %get-tuple-element.22.refs_0_), channel_id=1, source_target_pairs={{8,0},{16,8},{24,16},{0,24},{9,1},{17,9},{25,17},{1,25},{10,2},{18... | collective-permute-start | bytes 776 | tf_op jit(solution)/shard_map/ppermute | solution.py:394
  19.9 4.9 %collective-permute-start.4 = (s32[4,128]{1,0:T(4,128)S(1)}, s32[4,128]{1,0:T(4,128)S(1)}, u32[]{:S(2)}, u32[]{:S(2)}) collective-permute-start(s32[4,128]{1,0:T(4,128)S(1)} %get-tuple-element.28), channel_id=1, source_target_pairs={{0,1},{1,0},{2,3},{3,2},{4,5},{5,4},{6,7},{7,6},{8,9},{9,8},{10,11... | collective-permute-start | bytes 6152 | tf_op jit(solution)/shard_map/ppermute | solution.py:441
  20.0 8.6 %collective-permute-start.5 = (s32[2,128]{1,0:T(2,128)S(1)}, s32[2,128]{1,0:T(2,128)S(1)}, u32[]{:S(2)}, u32[]{:S(2)}) collective-permute-start(s32[2,128]{1,0:T(2,128)S(1)} %get-tuple-element.29._), channel_id=1, source_target_pairs={{4,0},{5,1},{2,4},{3,5},{6,2},{7,3},{0,6},{1,7},{12,8},{13,9},{10,... | collective-permute-start | bytes 3080 | tf_op jit(solution)/shard_map/ppermute | solution.py:443

commit v6 on v5

--- a/solution.py
+++ b/solution.py
@@ -42,11 +42,10 @@
     return lax.dot_general(a, b, NT, preferred_element_type=F32)
 
 
-def first_projection(blocks, w_cell, proj, at):
-    _, samples, width = blocks[0].shape
-    cells = jnp.concatenate([block.reshape(-1, width) for block in blocks], axis=0)
-    rows = dot(cells, w_cell[...]).astype(BF16)
-    proj[at : at + rows.shape[0] // samples] = rows.reshape(-1, samples, width)
+def first_projection(block, w_cell, proj, at):
+    columns, samples, width = block.shape
+    rows = dot(block.reshape(-1, width), w_cell[...]).astype(BF16)
+    proj[at : at + columns] = rows.reshape(columns, samples, width)
     return rows
 
 
@@ -61,10 +60,10 @@
     columns = own.shape[0]
     copy = pltpu.make_async_copy(own, own_in, sem)
     copy.start()
-    rows = first_projection([partner[...]], w_cell, proj, columns)
+    rows = first_projection(partner[...], w_cell, proj, columns)
     second_projection(rows, w_mix, mixed, columns)
     copy.wait()
-    rows = first_projection([own_in[...]], w_cell, proj, 0)
+    rows = first_projection(own_in[...], w_cell, proj, 0)
     second_projection(rows, w_mix, mixed, 0)
 
 
@@ -127,8 +126,10 @@
     w_cell, w_mix, _, _, proj, mixed, pool_x, pool_y = refs[count + chips : -1 - count]
     index, sems = refs[-1 - count : -1], refs[-1]
     copies = start_copies(lists, index, sems)
-    rows = first_projection([ref[...] for ref in remote], w_cell, proj, base)
-    second_projection(rows, w_mix, mixed, base)
+    places = [base + i * remote[0].shape[0] for i in range(chips)]
+    rows = [first_projection(ref[...], w_cell, proj, at) for ref, at in zip(remote, places)]
+    for block, at in zip(rows, places):
+        second_projection(block, w_mix, mixed, at)
     for copy in copies:
         copy.wait()
     attend_lists(lists_of(held, index), 0, proj, mixed, score_scale, pool_x, pool_y, last=False)
@@ -231,7 +232,8 @@
     lax.fori_loop(0, (total + block - 1) // block, step, 0)
 
 
-def share_kernel(quarter, cells, share, sem):
+def share_kernel(cells, share, sem):
+    quarter = share.shape[0]
     first = lax.axis_index("grp") * quarter
     copy = pltpu.make_async_copy(cells.at[pl.ds(first, quarter)], share, sem)
     copy.start()
@@ -365,7 +367,7 @@
     weight = jax.ShapeDtypeStruct(w_cell.shape, BF16)
     weight_bytes = 2 * width * width
     share = pl.pallas_call(
-        functools.partial(share_kernel, quarter),
+        share_kernel,
         out_shape=jax.ShapeDtypeStruct((quarter, samples, width), BF16),
         in_specs=[hbm()],
         out_specs=vmem(),

time: 45 us -> 45.5 us (1.011); the launches traced: 44.3 us -> 45.3 us
  Pallas kernels: 20.5 us -> 23 us
  waiting for transfers between devices: 1.25 us -> 0.32 us
  blocking collectives: 10.7 us -> 10.1 us
    pallas_call x1, Pallas kernels: 3.76 us -> 5.67 us  [local(): pl.pallas_call(functools.partial(near_kernel, len(group), 2 * per_shard +...]
    ppermute x2, waiting for transfers between devices: 1.23 us -> 0.31 us  [local(): remote = {d: lax.ppermute(share, 'shard', from_ahead(d)) for d in offsets}]
    pallas_call x1, Pallas kernels: 3.18 us -> 4.11 us  [local(): pl.pallas_call(functools.partial(chip_kernel, score_scale), out_shape=[sc...]
    all_to_all x1, blocking collectives: 10.7 us -> 10.1 us  [local(): back = lax.all_to_all(out, ('grp', 'shard'), 0, 0, tiled=True)]
  transfers between devices with their start and end apart: 8 -> 8, of which waited for: 1 -> 1; matrix products, arithmetic and copies ran while one was open for 0% -> 0% of each run, Pallas kernels for 34% -> 39%
where the time goes in v6:
time: 45.5 us; the launch traced here: 45.3 us
  Pallas kernels  23 us (51%)
  starting transfers between devices  10.6 us (23%)
  blocking collectives  10.1 us (22%)
  between operations  0.75 us (2%)
  other arithmetic  0.56 us (1%)
    all_to_all x1, blocking collectives, local(): back = lax.all_to_all(out, ('grp', 'shard'), 0, 0, tiled=True)  10.1 us
    pallas_call x1, Pallas kernels, local(): pl.pallas_call(functools.partial(near_kernel, len(group), 2 * per_shard +...  5.67 us
    pallas_call x1, Pallas kernels, local(): pl.pallas_call(project_kernel, out_shape=[store, store], in_specs=[hbm()]...  5.47 us
    ppermute x2, starting transfers between devices, local(): remote = {d: lax.ppermute(share, 'shard', from_ahead(d)) for d in offsets}  5.13 us
    ppermute x3, starting transfers between devices, local(): lax.ppermute(ids, 'grp', [((g + k) % lines, g) for g in range(lines)])  4.5 us
    pallas_call x1, Pallas kernels, local(): pl.pallas_call(functools.partial(far_kernel, held, sum(held[:number]), sc...  4.2 us
    pallas_call x1, Pallas kernels, local(): pl.pallas_call(functools.partial(chip_kernel, score_scale), out_shape=[sc...  4.11 us
    pallas_call x1, Pallas kernels, local(): pl.pallas_call(functools.partial(prepare_kernel, sizes), out_shape=(jax.S...  1.67 us
  transfers between devices with their start and end apart: 8, of which 1 were waited for; matrix products, arithmetic and copies ran while one was open for 0% of the time, Pallas kernels for 39%

profile of v6, /device:TPU:0, one launch (start us, length us, event | category | flops | bytes accessed | tf_op | source)
XLA Modules:
  0.0 45.3 jit_solution(6777517393817305708)
XLA Ops:
  0.0 1.0 %share.1._ = bf16[4,64,768]{2,1,0:T(8,128)(2,1)S(1)} custom-call(bf16[16,64,768]{2,1,0:T(8,128)(2,1)} %own), custom_call_target="tpu_custom_call" | custom-call | tf_op jit(solution)/shard_map/share/pallas_call | solution.py:369
  1.0 0.5 %collective-permute-start.3 = (bf16[16,64,768]{2,1,0:T(8,128)(2,1)}, bf16[16,64,768]{2,1,0:T(8,128)(2,1)S(1)}, u32[]{:S(2)}, u32[]{:S(2)}) collective-permute-start(bf16[16,64,768]{2,1,0:T(8,128)(2,1)} %own), channel_id=1, source_target_pairs={{0,1},{1,0},{2,3},{3,2},{4,5},{5,4},{6,7},{7,6},{8,9},{9,8},{10,11... | collective-permute-start | bytes 4718600 | tf_op jit(solution)/shard_map/ppermute | solution.py:380
  1.5 2.7 %collective-permute-start.7 = (bf16[4,64,768]{2,1,0:T(8,128)(2,1)S(1)}, bf16[4,64,768]{2,1,0:T(8,128)(2,1)S(1)}, u32[]{:S(2)}, u32[]{:S(2)}) collective-permute-start(bf16[4,64,768]{2,1,0:T(8,128)(2,1)S(1)} %share.1._), channel_id=1, source_target_pairs={{2,0},{3,1},{6,4},{7,5},{0,2},{1,3},{4,6},{5,7},{10,8},{11,9},{14,... | collective-permute-start | bytes 1179656 | tf_op jit(solution)/shard_map/ppermute | solution.py:378
  4.2 2.5 %collective-permute-start.6 = (bf16[4,64,768]{2,1,0:T(8,128)(2,1)S(1)}, bf16[4,64,768]{2,1,0:T(8,128)(2,1)S(1)}, u32[]{:S(2)}, u32[]{:S(2)}) collective-permute-start(bf16[4,64,768]{2,1,0:T(8,128)(2,1)S(1)} %share.1._), channel_id=1, source_target_pairs={{4,0},{5,1},{2,4},{3,5},{6,2},{7,3},{0,6},{1,7},{12,8},{13,9},{10,... | collective-permute-start | bytes 1179656 | tf_op jit(solution)/shard_map/ppermute | solution.py:378
  7.3 1.7 %prepare.1 = (s32[1,64]{1,0:T(1,128)S(1)}, s32[2,128]{1,0:T(2,128)S(1)}, bf16[768,768]{1,0:T(8,128)(2,1)S(1)}, bf16[768,768]{1,0:T(8,128)(2,1)S(1)}) custom-call(s32[2,64]{1,0:T(2,128)} %bitcast.5, s32[1]{0:T(128)S(6)} %copy.18.counts, bf16[768,768]{1,0:T(8,128)(2,1)} %w_cell.1, bf16[768,768]{1,0:T(8,128)(2,1)} %w_mix.1, bf16[4,64,768]{2,1,0:T(8,128)(2,1)S(1)} %share.1._), custom_call_target="tpu_custom_call" | custom-call | tf_op jit(solution)/shard_map/prepare/pallas_call | solution.py:381
  9.0 1.5 %collective-permute-start.2 = (s32[1,64]{1,0:T(1,128)S(1)}, s32[1,64]{1,0:T(1,128)S(1)}, u32[]{:S(2)}, u32[]{:S(2)}) collective-permute-start(s32[1,64]{1,0:T(1,128)S(1)} %get-tuple-element.22.refs_0_), channel_id=1, source_target_pairs={{24,0},{0,8},{8,16},{16,24},{25,1},{1,9},{9,17},{17,25},{26,2},{2,... | collective-permute-start | bytes 776 | tf_op jit(solution)/shard_map/ppermute | solution.py:396
  10.5 1.5 %collective-permute-start.1 = (s32[1,64]{1,0:T(1,128)S(1)}, s32[1,64]{1,0:T(1,128)S(1)}, u32[]{:S(2)}, u32[]{:S(2)}) collective-permute-start(s32[1,64]{1,0:T(1,128)S(1)} %get-tuple-element.22.refs_0_), channel_id=1, source_target_pairs={{16,0},{24,8},{0,16},{8,24},{17,1},{25,9},{1,17},{9,25},{18,2},{26... | collective-permute-start | bytes 776 | tf_op jit(solution)/shard_map/ppermute | solution.py:396
  12.1 0.0 collective-permute-done.3.partner
  12.1 1.4 %collective-permute-start = (s32[1,64]{1,0:T(1,128)S(1)}, s32[1,64]{1,0:T(1,128)S(1)}, u32[]{:S(2)}, u32[]{:S(2)}) collective-permute-start(s32[1,64]{1,0:T(1,128)S(1)} %get-tuple-element.22.refs_0_), channel_id=1, source_target_pairs={{8,0},{16,8},{24,16},{0,24},{9,1},{17,9},{25,17},{1,25},{10,2},{18... | collective-permute-start | bytes 776 | tf_op jit(solution)/shard_map/ppermute | solution.py:396
  13.5 5.5 %project.1 = (bf16[40,64,768]{2,1,0:T(8,128)(2,1)S(1)}, bf16[40,64,768]{2,1,0:T(8,128)(2,1)S(1)}) custom-call(bf16[16,64,768]{2,1,0:T(8,128)(2,1)} %own, bf16[16,64,768]{2,1,0:T(8,128)(2,1)S(1)} %collective-permute-done.3.partner, bf16[768,768]{1,0:T(8,128)(2,1)S(1)} %get-tuple-element.24.w_cell.refs_4_, bf16[768,768]{1,0:T(8,128)(2,1)S(1)} %get-tuple-element.25.w_mix.refs_5_), custom_call_target="tpu_custom_call" | custom-call | tf_op jit(solution)/shard_map/project/pallas_call | solution.py:414
  19.0 0.0 collective-permute-done.2.refs_3_
  19.0 0.0 collective-permute-done.1.refs_2_
  19.0 0.0 collective-permute-done.refs_1_
  19.0 0.9 %route.1 = (s32[4,128]{1,0:T(4,128)S(1)}, s32[4,128]{1,0:T(4,128)S(1)}, s32[2,128]{1,0:T(2,128)S(1)}) custom-call(s32[1,64]{1,0:T(1,128)S(1)} %get-tuple-element.22.refs_0_, s32[1,64]{1,0:T(1,128)S(1)} %collective-permute-done.refs_1_, s32[1,64]{1,0:T(1,128)S(1)} %collective-permute-done.1.refs_2_, s32[1,64]{1,0:T(1,128)S(1)} %collective-permute-done.2.refs_3_, ...), custom_call_target="tpu_custom_call" | custom-call | tf_op jit(solution)/shard_map/route/pallas_call | solution.py:431
  19.9 0.1 collective-permute-start.4
  20.0 0.4 collective-permute-start.5
  20.3 4.1 %chip.1 = (f32[32,64]{1,0:T(8,128)S(1)}, bf16[768,768]{1,0:T(8,128)(2,1)S(1)}) custom-call(s32[2,128]{1,0:T(2,128)S(1)} %get-tuple-element.33.index, bf16[40,64,768]{2,1,0:T(8,128)(2,1)S(1)} %get-tuple-element.26.refs_4_.refs_6_.proj, bf16[40,64,768]{2,1,0:T(8,128)(2,1)S(1)} %get-tuple-element.30.refs_7_.mixed, bf16[768,768]{1,0:T(8,128)(2,1)} %w_pool.1, ...), custom_call_target="tpu_custom_call" | custom-call | tf_op jit(solution)/shard_map/chip/pallas_call | solution.py:448
  24.5 0.0 collective-permute-done.7.refs_3_
  24.5 0.3 collective-permute-done.6.refs_2_
  24.8 0.0 collective-permute-done.4.refs_1_
  24.8 5.7 %near1_2.1 = (bf16[40,64,768]{2,1,0:T(8,128)(2,1)S(1)}, bf16[40,64,768]{2,1,0:T(8,128)(2,1)S(1)}, f32[768,896]{1,0:T(8,128)S(1)}, f32[768,768]{1,0:T(8,128)S(1)}) custom-call(s32[4,128]{1,0:T(4,128)S(1)} %get-tuple-element.27.refs_0_, s32[4,128]{1,0:T(4,128)S(1)} %collective-permute-done.4.refs_1_, ...), custom_call_target="tpu_custom_call", output_to_operand_aliasing={{0}: (6, {}), {1}: (7, {})} | custom-call | tf_op jit(solution)/shard_map/near1_2/pallas_call | solution.py:466
  30.5 0.0 collective-permute-done.5.refs_2_
  30.5 4.2 %far1_2.1 = (f32[32,64]{1,0:T(8,128)S(1)}, f32[768,896]{1,0:T(8,128)S(1)}, f32[768,768]{1,0:T(8,128)S(1)}) custom-call(s32[4,128]{1,0:T(4,128)S(1)} %get-tuple-element.27.refs_0_, s32[4,128]{1,0:T(4,128)S(1)} %collective-permute-done.4.refs_1_, ...), custom_call_target="tpu_custom_call", output_to_operand_aliasing={{0}: (6, {}), {1}: (7, {}), {2}: (8, {})} | custom-call | tf_op jit(solution)/shard_map/far1_2/pallas_call | solution.py:486
  34.7 10.1 %all_to_all.9 = f32[32,1,64]{2,1,0:T(1,128)S(1)} all-to-all(f32[32,1,64]{2,1,0:T(1,128)S(1)} %bitcast.4), channel_id=1, replica_groups=mesh['grp'=4,'shard'=8] {'grp','shard'}, dimensions={0} | all-to-all | bytes 16384 | tf_op jit(solution)/shard_map/all_to_all | solution.py:500
  44.8 0.6 %reduce_sum.9 = f32[64]{0:T(128)} reduce(f32[32,1,64]{2,1,0:T(1,128)S(1)} %all_to_all.9, f32[]{:T(128)} %constant.0.clone.1), dimensions={0,1}, to_apply=%region_0.0 | reduce | flops 1984 | bytes 8452 | tf_op jit(solution)/shard_map/reduce_sum | solution.py:501
Async XLA Ops:
  1.0 11.0 %collective-permute-start.3 = (bf16[16,64,768]{2,1,0:T(8,128)(2,1)}, bf16[16,64,768]{2,1,0:T(8,128)(2,1)S(1)}, u32[]{:S(2)}, u32[]{:S(2)}) collective-permute-start(bf16[16,64,768]{2,1,0:T(8,128)(2,1)} %own), channel_id=1, source_target_pairs={{0,1},{1,0},{2,3},{3,2},{4,5},{5,4},{6,7},{7,6},{8,9},{9,8},{10,11... | collective-permute-start | bytes 4718600 | tf_op jit(solution)/shard_map/ppermute | solution.py:380
  1.5 22.9 %collective-permute-start.7 = (bf16[4,64,768]{2,1,0:T(8,128)(2,1)S(1)}, bf16[4,64,768]{2,1,0:T(8,128)(2,1)S(1)}, u32[]{:S(2)}, u32[]{:S(2)}) collective-permute-start(bf16[4,64,768]{2,1,0:T(8,128)(2,1)S(1)} %share.1._), channel_id=1, source_target_pairs={{2,0},{3,1},{6,4},{7,5},{0,2},{1,3},{4,6},{5,7},{10,8},{11,9},{14,... | collective-permute-start | bytes 1179656 | tf_op jit(solution)/shard_map/ppermute | solution.py:378
  4.2 20.6 %collective-permute-start.6 = (bf16[4,64,768]{2,1,0:T(8,128)(2,1)S(1)}, bf16[4,64,768]{2,1,0:T(8,128)(2,1)S(1)}, u32[]{:S(2)}, u32[]{:S(2)}) collective-permute-start(bf16[4,64,768]{2,1,0:T(8,128)(2,1)S(1)} %share.1._), channel_id=1, source_target_pairs={{4,0},{5,1},{2,4},{3,5},{6,2},{7,3},{0,6},{1,7},{12,8},{13,9},{10,... | collective-permute-start | bytes 1179656 | tf_op jit(solution)/shard_map/ppermute | solution.py:378
  9.0 10.0 %collective-permute-start.2 = (s32[1,64]{1,0:T(1,128)S(1)}, s32[1,64]{1,0:T(1,128)S(1)}, u32[]{:S(2)}, u32[]{:S(2)}) collective-permute-start(s32[1,64]{1,0:T(1,128)S(1)} %get-tuple-element.22.refs_0_), channel_id=1, source_target_pairs={{24,0},{0,8},{8,16},{16,24},{25,1},{1,9},{9,17},{17,25},{26,2},{2,... | collective-permute-start | bytes 776 | tf_op jit(solution)/shard_map/ppermute | solution.py:396
  10.5 8.4 %collective-permute-start.1 = (s32[1,64]{1,0:T(1,128)S(1)}, s32[1,64]{1,0:T(1,128)S(1)}, u32[]{:S(2)}, u32[]{:S(2)}) collective-permute-start(s32[1,64]{1,0:T(1,128)S(1)} %get-tuple-element.22.refs_0_), channel_id=1, source_target_pairs={{16,0},{24,8},{0,16},{8,24},{17,1},{25,9},{1,17},{9,25},{18,2},{26... | collective-permute-start | bytes 776 | tf_op jit(solution)/shard_map/ppermute | solution.py:396
  12.1 6.9 %collective-permute-start = (s32[1,64]{1,0:T(1,128)S(1)}, s32[1,64]{1,0:T(1,128)S(1)}, u32[]{:S(2)}, u32[]{:S(2)}) collective-permute-start(s32[1,64]{1,0:T(1,128)S(1)} %get-tuple-element.22.refs_0_), channel_id=1, source_target_pairs={{8,0},{16,8},{24,16},{0,24},{9,1},{17,9},{25,17},{1,25},{10,2},{18... | collective-permute-start | bytes 776 | tf_op jit(solution)/shard_map/ppermute | solution.py:396
  19.9 4.9 %collective-permute-start.4 = (s32[4,128]{1,0:T(4,128)S(1)}, s32[4,128]{1,0:T(4,128)S(1)}, u32[]{:S(2)}, u32[]{:S(2)}) collective-permute-start(s32[4,128]{1,0:T(4,128)S(1)} %get-tuple-element.28), channel_id=1, source_target_pairs={{0,1},{1,0},{2,3},{3,2},{4,5},{5,4},{6,7},{7,6},{8,9},{9,8},{10,11... | collective-permute-start | bytes 6152 | tf_op jit(solution)/shard_map/ppermute | solution.py:443
  20.0 10.5 %collective-permute-start.5 = (s32[2,128]{1,0:T(2,128)S(1)}, s32[2,128]{1,0:T(2,128)S(1)}, u32[]{:S(2)}, u32[]{:S(2)}) collective-permute-start(s32[2,128]{1,0:T(2,128)S(1)} %get-tuple-element.29._), channel_id=1, source_target_pairs={{4,0},{5,1},{2,4},{3,5},{6,2},{7,3},{0,6},{1,7},{12,8},{13,9},{10,... | collective-permute-start | bytes 3080 | tf_op jit(solution)/shard_map/ppermute | solution.py:445

commit v7 on v6

--- a/solution.py
+++ b/solution.py
@@ -83,26 +83,35 @@
     lane = lax.broadcasted_iota(jnp.int32, shape, 1)
     first = lane < samples
     unit = (lax.rem(lane, samples) == lax.broadcasted_iota(jnp.int32, shape, 0)).astype(F32)
-    weights = []
-    for x, y in pairs:
+    weights, attend, pooled = [], [], []
+
+    def score(x, y):
         both = dot_nt(
             jnp.concatenate([proj[y], proj[x]], axis=0), jnp.concatenate([proj[x], proj[y]], axis=0)
         )
         weights.append(jnp.where(first, both[:samples], both[samples:]) * score_scale)
-    weights = [jnp.exp(w - jnp.max(w, axis=0, keepdims=True)) for w in weights]
-    weights = [w * (1.0 / jnp.sum(w, axis=0, keepdims=True)) for w in weights]
-    attend = [
-        jnp.transpose(
-            jnp.concatenate([jnp.where(first, w, unit), jnp.where(first, unit, w)], axis=0)
-        ).astype(BF16)
-        for w in weights
-    ]
-    pooled = []
-    for t, (x, y) in zip(attend, pairs):
+
+    def soften(w):
+        w = jnp.exp(w - jnp.max(w, axis=0, keepdims=True))
+        w = w * (1.0 / jnp.sum(w, axis=0, keepdims=True))
+        blocks = [jnp.where(first, w, unit), jnp.where(first, unit, w)]
+        attend.append(jnp.transpose(jnp.concatenate(blocks, axis=0)).astype(BF16))
+
+    def mix(t, x, y):
         rows = jnp.tanh(dot(t, jnp.concatenate([mixed[y], mixed[x]], axis=0)))
         pooled.append(
             [jnp.sum(r, axis=0, keepdims=True) * (1.0 / samples) for r in (rows[:samples], rows[samples:])]
         )
+
+    group = STEPS[-1]
+    for at in range(len(pairs) + 2 * group):
+        early, late = at - group, at - 2 * group
+        if late >= 0:
+            mix(attend[late], *pairs[late])
+        if at < len(pairs):
+            score(*pairs[at])
+        if 0 <= early < len(pairs):
+            soften(weights[early])
     return pooled
 
 

time: 45.5 us -> 44.4 us (0.976)
  Pallas kernels: 23 us -> 20.9 us
  waiting for transfers between devices: 0.32 us -> 1.25 us
    pallas_call x1, Pallas kernels: 5.67 us -> 3.52 us  [local(): pl.pallas_call(functools.partial(near_kernel, len(group), 2 * per_shard +...]
    pallas_call x1, Pallas kernels: 4.2 us -> 5.22 us  [local(): pl.pallas_call(functools.partial(far_kernel, held, sum(held[:number]), sc...]
    ppermute x2, waiting for transfers between devices: 0.31 us -> 1.23 us  [local(): remote = {d: lax.ppermute(share, 'shard', from_ahead(d)) for d in offsets}]
    pallas_call x1, Pallas kernels: 4.11 us -> 3.18 us  [local(): pl.pallas_call(functools.partial(chip_kernel, score_scale), out_shape=[sc...]
  transfers between devices with their start and end apart: 8 -> 8, of which waited for: 1 -> 1; matrix products, arithmetic and copies ran while one was open for 0% -> 0% of each run, Pallas kernels for 39% -> 33%
where the time goes in v7:
time: 44.4 us; the launch traced here: 44.5 us
  Pallas kernels  20.9 us (47%)
  starting transfers between devices  10.6 us (24%)
  blocking collectives  10.4 us (23%)
  waiting for transfers between devices  1.25 us (3%)
  between operations  0.75 us (2%)
  other arithmetic  0.56 us (1%)
    all_to_all x1, blocking collectives, local(): back = lax.all_to_all(out, ('grp', 'shard'), 0, 0, tiled=True)  10.4 us
    pallas_call x1, Pallas kernels, local(): pl.pallas_call(project_kernel, out_shape=[store, store], in_specs=[hbm()]...  5.47 us
    pallas_call x1, Pallas kernels, local(): pl.pallas_call(functools.partial(far_kernel, held, sum(held[:number]), sc...  5.22 us
    ppermute x2, starting transfers between devices, local(): remote = {d: lax.ppermute(share, 'shard', from_ahead(d)) for d in offsets}  5.13 us
    ppermute x3, starting transfers between devices, local(): lax.ppermute(ids, 'grp', [((g + k) % lines, g) for g in range(lines)])  4.5 us
    pallas_call x1, Pallas kernels, local(): pl.pallas_call(functools.partial(near_kernel, len(group), 2 * per_shard +...  3.52 us
    pallas_call x1, Pallas kernels, local(): pl.pallas_call(functools.partial(chip_kernel, score_scale), out_shape=[sc...  3.18 us
    pallas_call x1, Pallas kernels, local(): pl.pallas_call(functools.partial(prepare_kernel, sizes), out_shape=(jax.S...  1.67 us
  transfers between devices with their start and end apart: 8, of which 1 were waited for; matrix products, arithmetic and copies ran while one was open for 0% of the time, Pallas kernels for 33%

profile of v7, /device:TPU:0, one launch (start us, length us, event | category | flops | bytes accessed | tf_op | source)
XLA Modules:
  0.0 44.5 jit_solution(18223228389589260610)
XLA Ops:
  0.0 1.0 %share.1._ = bf16[4,64,768]{2,1,0:T(8,128)(2,1)S(1)} custom-call(bf16[16,64,768]{2,1,0:T(8,128)(2,1)} %own), custom_call_target="tpu_custom_call" | custom-call | tf_op jit(solution)/shard_map/share/pallas_call | solution.py:378
  1.0 0.5 %collective-permute-start.3 = (bf16[16,64,768]{2,1,0:T(8,128)(2,1)}, bf16[16,64,768]{2,1,0:T(8,128)(2,1)S(1)}, u32[]{:S(2)}, u32[]{:S(2)}) collective-permute-start(bf16[16,64,768]{2,1,0:T(8,128)(2,1)} %own), channel_id=1, source_target_pairs={{0,1},{1,0},{2,3},{3,2},{4,5},{5,4},{6,7},{7,6},{8,9},{9,8},{10,11... | collective-permute-start | bytes 4718600 | tf_op jit(solution)/shard_map/ppermute | solution.py:389
  1.5 2.7 %collective-permute-start.7 = (bf16[4,64,768]{2,1,0:T(8,128)(2,1)S(1)}, bf16[4,64,768]{2,1,0:T(8,128)(2,1)S(1)}, u32[]{:S(2)}, u32[]{:S(2)}) collective-permute-start(bf16[4,64,768]{2,1,0:T(8,128)(2,1)S(1)} %share.1._), channel_id=1, source_target_pairs={{2,0},{3,1},{6,4},{7,5},{0,2},{1,3},{4,6},{5,7},{10,8},{11,9},{14,... | collective-permute-start | bytes 1179656 | tf_op jit(solution)/shard_map/ppermute | solution.py:387
  4.2 2.5 %collective-permute-start.6 = (bf16[4,64,768]{2,1,0:T(8,128)(2,1)S(1)}, bf16[4,64,768]{2,1,0:T(8,128)(2,1)S(1)}, u32[]{:S(2)}, u32[]{:S(2)}) collective-permute-start(bf16[4,64,768]{2,1,0:T(8,128)(2,1)S(1)} %share.1._), channel_id=1, source_target_pairs={{4,0},{5,1},{2,4},{3,5},{6,2},{7,3},{0,6},{1,7},{12,8},{13,9},{10,... | collective-permute-start | bytes 1179656 | tf_op jit(solution)/shard_map/ppermute | solution.py:387
  7.3 1.7 %prepare.1 = (s32[1,64]{1,0:T(1,128)S(1)}, s32[2,128]{1,0:T(2,128)S(1)}, bf16[768,768]{1,0:T(8,128)(2,1)S(1)}, bf16[768,768]{1,0:T(8,128)(2,1)S(1)}) custom-call(s32[2,64]{1,0:T(2,128)} %bitcast.5, s32[1]{0:T(128)S(6)} %copy.18.counts, bf16[768,768]{1,0:T(8,128)(2,1)} %w_cell.1, bf16[768,768]{1,0:T(8,128)(2,1)} %w_mix.1, bf16[4,64,768]{2,1,0:T(8,128)(2,1)S(1)} %share.1._), custom_call_target="tpu_custom_call" | custom-call | tf_op jit(solution)/shard_map/prepare/pallas_call | solution.py:390
  9.0 1.5 %collective-permute-start.2 = (s32[1,64]{1,0:T(1,128)S(1)}, s32[1,64]{1,0:T(1,128)S(1)}, u32[]{:S(2)}, u32[]{:S(2)}) collective-permute-start(s32[1,64]{1,0:T(1,128)S(1)} %get-tuple-element.22.refs_0_), channel_id=1, source_target_pairs={{24,0},{0,8},{8,16},{16,24},{25,1},{1,9},{9,17},{17,25},{26,2},{2,... | collective-permute-start | bytes 776 | tf_op jit(solution)/shard_map/ppermute | solution.py:405
  10.5 1.5 %collective-permute-start.1 = (s32[1,64]{1,0:T(1,128)S(1)}, s32[1,64]{1,0:T(1,128)S(1)}, u32[]{:S(2)}, u32[]{:S(2)}) collective-permute-start(s32[1,64]{1,0:T(1,128)S(1)} %get-tuple-element.22.refs_0_), channel_id=1, source_target_pairs={{16,0},{24,8},{0,16},{8,24},{17,1},{25,9},{1,17},{9,25},{18,2},{26... | collective-permute-start | bytes 776 | tf_op jit(solution)/shard_map/ppermute | solution.py:405
  12.1 0.0 collective-permute-done.3.partner
  12.1 1.4 %collective-permute-start = (s32[1,64]{1,0:T(1,128)S(1)}, s32[1,64]{1,0:T(1,128)S(1)}, u32[]{:S(2)}, u32[]{:S(2)}) collective-permute-start(s32[1,64]{1,0:T(1,128)S(1)} %get-tuple-element.22.refs_0_), channel_id=1, source_target_pairs={{8,0},{16,8},{24,16},{0,24},{9,1},{17,9},{25,17},{1,25},{10,2},{18... | collective-permute-start | bytes 776 | tf_op jit(solution)/shard_map/ppermute | solution.py:405
  13.5 5.5 %project.1 = (bf16[40,64,768]{2,1,0:T(8,128)(2,1)S(1)}, bf16[40,64,768]{2,1,0:T(8,128)(2,1)S(1)}) custom-call(bf16[16,64,768]{2,1,0:T(8,128)(2,1)} %own, bf16[16,64,768]{2,1,0:T(8,128)(2,1)S(1)} %collective-permute-done.3.partner, bf16[768,768]{1,0:T(8,128)(2,1)S(1)} %get-tuple-element.24.w_cell.refs_4_, bf16[768,768]{1,0:T(8,128)(2,1)S(1)} %get-tuple-element.25.w_mix.refs_5_), custom_call_target="tpu_custom_call" | custom-call | tf_op jit(solution)/shard_map/project/pallas_call | solution.py:423
  19.0 0.0 collective-permute-done.2.refs_3_
  19.0 0.0 collective-permute-done.1.refs_2_
  19.0 0.0 collective-permute-done.refs_1_
  19.0 0.9 %route.1 = (s32[4,128]{1,0:T(4,128)S(1)}, s32[4,128]{1,0:T(4,128)S(1)}, s32[2,128]{1,0:T(2,128)S(1)}) custom-call(s32[1,64]{1,0:T(1,128)S(1)} %get-tuple-element.22.refs_0_, s32[1,64]{1,0:T(1,128)S(1)} %collective-permute-done.refs_1_, s32[1,64]{1,0:T(1,128)S(1)} %collective-permute-done.1.refs_2_, s32[1,64]{1,0:T(1,128)S(1)} %collective-permute-done.2.refs_3_, ...), custom_call_target="tpu_custom_call" | custom-call | tf_op jit(solution)/shard_map/route/pallas_call | solution.py:440
  19.9 0.1 collective-permute-start.4
  20.0 0.4 collective-permute-start.5
  20.3 3.2 %chip.1 = (f32[32,64]{1,0:T(8,128)S(1)}, bf16[768,768]{1,0:T(8,128)(2,1)S(1)}) custom-call(s32[2,128]{1,0:T(2,128)S(1)} %get-tuple-element.33.index, bf16[40,64,768]{2,1,0:T(8,128)(2,1)S(1)} %get-tuple-element.26.refs_4_.refs_6_.proj, bf16[40,64,768]{2,1,0:T(8,128)(2,1)S(1)} %get-tuple-element.30.refs_7_.mixed, bf16[768,768]{1,0:T(8,128)(2,1)} %w_pool.1, ...), custom_call_target="tpu_custom_call" | custom-call | tf_op jit(solution)/shard_map/chip/pallas_call | solution.py:457
  23.5 0.0 collective-permute-done.7.refs_3_
  23.5 1.2 %collective-permute-done.6.refs_2_ = bf16[4,64,768]{2,1,0:T(8,128)(2,1)S(1)} collective-permute-done((bf16[4,64,768]{2,1,0:T(8,128)(2,1)S(1)}, bf16[4,64,768]{2,1,0:T(8,128)(2,1)S(1)}, u32[]{:S(2)}, u32[]{:S(2)}) %collective-permute-start.6) | collective-permute-done | bytes 393248 | tf_op jit(solution)/shard_map/ppermute | solution.py:387
  24.8 0.0 collective-permute-done.4.refs_1_
  24.8 3.5 %near1_2.1 = (bf16[40,64,768]{2,1,0:T(8,128)(2,1)S(1)}, bf16[40,64,768]{2,1,0:T(8,128)(2,1)S(1)}, f32[768,896]{1,0:T(8,128)S(1)}, f32[768,768]{1,0:T(8,128)S(1)}) custom-call(s32[4,128]{1,0:T(4,128)S(1)} %get-tuple-element.27.refs_0_, s32[4,128]{1,0:T(4,128)S(1)} %collective-permute-done.4.refs_1_, ...), custom_call_target="tpu_custom_call", output_to_operand_aliasing={{0}: (6, {}), {1}: (7, {})} | custom-call | tf_op jit(solution)/shard_map/near1_2/pallas_call | solution.py:475
  28.3 0.0 collective-permute-done.5.refs_2_
  28.3 5.2 %far1_2.1 = (f32[32,64]{1,0:T(8,128)S(1)}, f32[768,896]{1,0:T(8,128)S(1)}, f32[768,768]{1,0:T(8,128)S(1)}) custom-call(s32[4,128]{1,0:T(4,128)S(1)} %get-tuple-element.27.refs_0_, s32[4,128]{1,0:T(4,128)S(1)} %collective-permute-done.4.refs_1_, ...), custom_call_target="tpu_custom_call", output_to_operand_aliasing={{0}: (6, {}), {1}: (7, {}), {2}: (8, {})} | custom-call | tf_op jit(solution)/shard_map/far1_2/pallas_call | solution.py:495
  33.5 10.4 %all_to_all.9 = f32[32,1,64]{2,1,0:T(1,128)S(1)} all-to-all(f32[32,1,64]{2,1,0:T(1,128)S(1)} %bitcast.4), channel_id=1, replica_groups=mesh['grp'=4,'shard'=8] {'grp','shard'}, dimensions={0} | all-to-all | bytes 16384 | tf_op jit(solution)/shard_map/all_to_all | solution.py:509
  43.9 0.6 %reduce_sum.9 = f32[64]{0:T(128)} reduce(f32[32,1,64]{2,1,0:T(1,128)S(1)} %all_to_all.9, f32[]{:T(128)} %constant.0.clone.1), dimensions={0,1}, to_apply=%region_0.0 | reduce | flops 1984 | bytes 8452 | tf_op jit(solution)/shard_map/reduce_sum | solution.py:510
Async XLA Ops:
  1.0 11.0 %collective-permute-start.3 = (bf16[16,64,768]{2,1,0:T(8,128)(2,1)}, bf16[16,64,768]{2,1,0:T(8,128)(2,1)S(1)}, u32[]{:S(2)}, u32[]{:S(2)}) collective-permute-start(bf16[16,64,768]{2,1,0:T(8,128)(2,1)} %own), channel_id=1, source_target_pairs={{0,1},{1,0},{2,3},{3,2},{4,5},{5,4},{6,7},{7,6},{8,9},{9,8},{10,11... | collective-permute-start | bytes 4718600 | tf_op jit(solution)/shard_map/ppermute | solution.py:389
  1.5 22.0 %collective-permute-start.7 = (bf16[4,64,768]{2,1,0:T(8,128)(2,1)S(1)}, bf16[4,64,768]{2,1,0:T(8,128)(2,1)S(1)}, u32[]{:S(2)}, u32[]{:S(2)}) collective-permute-start(bf16[4,64,768]{2,1,0:T(8,128)(2,1)S(1)} %share.1._), channel_id=1, source_target_pairs={{2,0},{3,1},{6,4},{7,5},{0,2},{1,3},{4,6},{5,7},{10,8},{11,9},{14,... | collective-permute-start | bytes 1179656 | tf_op jit(solution)/shard_map/ppermute | solution.py:387
  4.2 20.6 %collective-permute-start.6 = (bf16[4,64,768]{2,1,0:T(8,128)(2,1)S(1)}, bf16[4,64,768]{2,1,0:T(8,128)(2,1)S(1)}, u32[]{:S(2)}, u32[]{:S(2)}) collective-permute-start(bf16[4,64,768]{2,1,0:T(8,128)(2,1)S(1)} %share.1._), channel_id=1, source_target_pairs={{4,0},{5,1},{2,4},{3,5},{6,2},{7,3},{0,6},{1,7},{12,8},{13,9},{10,... | collective-permute-start | bytes 1179656 | tf_op jit(solution)/shard_map/ppermute | solution.py:387
  9.0 10.0 %collective-permute-start.2 = (s32[1,64]{1,0:T(1,128)S(1)}, s32[1,64]{1,0:T(1,128)S(1)}, u32[]{:S(2)}, u32[]{:S(2)}) collective-permute-start(s32[1,64]{1,0:T(1,128)S(1)} %get-tuple-element.22.refs_0_), channel_id=1, source_target_pairs={{24,0},{0,8},{8,16},{16,24},{25,1},{1,9},{9,17},{17,25},{26,2},{2,... | collective-permute-start | bytes 776 | tf_op jit(solution)/shard_map/ppermute | solution.py:405
  10.5 8.4 %collective-permute-start.1 = (s32[1,64]{1,0:T(1,128)S(1)}, s32[1,64]{1,0:T(1,128)S(1)}, u32[]{:S(2)}, u32[]{:S(2)}) collective-permute-start(s32[1,64]{1,0:T(1,128)S(1)} %get-tuple-element.22.refs_0_), channel_id=1, source_target_pairs={{16,0},{24,8},{0,16},{8,24},{17,1},{25,9},{1,17},{9,25},{18,2},{26... | collective-permute-start | bytes 776 | tf_op jit(solution)/shard_map/ppermute | solution.py:405
  12.1 6.9 %collective-permute-start = (s32[1,64]{1,0:T(1,128)S(1)}, s32[1,64]{1,0:T(1,128)S(1)}, u32[]{:S(2)}, u32[]{:S(2)}) collective-permute-start(s32[1,64]{1,0:T(1,128)S(1)} %get-tuple-element.22.refs_0_), channel_id=1, source_target_pairs={{8,0},{16,8},{24,16},{0,24},{9,1},{17,9},{25,17},{1,25},{10,2},{18... | collective-permute-start | bytes 776 | tf_op jit(solution)/shard_map/ppermute | solution.py:405
  19.9 4.9 %collective-permute-start.4 = (s32[4,128]{1,0:T(4,128)S(1)}, s32[4,128]{1,0:T(4,128)S(1)}, u32[]{:S(2)}, u32[]{:S(2)}) collective-permute-start(s32[4,128]{1,0:T(4,128)S(1)} %get-tuple-element.28), channel_id=1, source_target_pairs={{0,1},{1,0},{2,3},{3,2},{4,5},{5,4},{6,7},{7,6},{8,9},{9,8},{10,11... | collective-permute-start | bytes 6152 | tf_op jit(solution)/shard_map/ppermute | solution.py:452
  20.0 8.4 %collective-permute-start.5 = (s32[2,128]{1,0:T(2,128)S(1)}, s32[2,128]{1,0:T(2,128)S(1)}, u32[]{:S(2)}, u32[]{:S(2)}) collective-permute-start(s32[2,128]{1,0:T(2,128)S(1)} %get-tuple-element.29._), channel_id=1, source_target_pairs={{4,0},{5,1},{2,4},{3,5},{6,2},{7,3},{0,6},{1,7},{12,8},{13,9},{10,... | collective-permute-start | bytes 3080 | tf_op jit(solution)/shard_map/ppermute | solution.py:454

commit v8 on v7

--- a/solution.py
+++ b/solution.py
@@ -385,7 +385,6 @@
         name="share",
     )(in_hbm(cells))
     remote = {d: lax.ppermute(share, "shard", from_ahead(d)) for d in offsets}
-    cells, _ = lax.optimization_barrier((cells, share))
     partner = lax.ppermute(cells, "shard", swap)
     ids, own_list, w_cell, w_mix = pl.pallas_call(
         functools.partial(prepare_kernel, sizes),

time: 44.4 us -> 45.2 us (1.018); the launches traced: 44.5 us -> 45.7 us
  Pallas kernels: 20.9 us -> 21.8 us
  blocking collectives: 10.4 us -> 10.9 us
    pallas_call x1, Pallas kernels: 3.52 us -> 5.41 us  [local(): pl.pallas_call(functools.partial(near_kernel, len(group), 2 * per_shard +...]
    pallas_call x1, Pallas kernels: 5.22 us -> 4.08 us  [local(): pl.pallas_call(functools.partial(far_kernel, held, sum(held[:number]), sc...]
    all_to_all x1, blocking collectives: 10.4 us -> 10.9 us  [local(): back = lax.all_to_all(out, ('grp', 'shard'), 0, 0, tiled=True)]
  transfers between devices with their start and end apart: 8 -> 8, of which waited for: 1 -> 1; matrix products, arithmetic and copies ran while one was open for 0% -> 0% of each run, Pallas kernels for 33% -> 39%
where the time goes in v8:
time: 45.2 us; the launch traced here: 45.7 us
  Pallas kernels  21.8 us (48%)
  blocking collectives  10.9 us (24%)
  starting transfers between devices  10.5 us (23%)
  waiting for transfers between devices  1.25 us (3%)
  between operations  0.75 us (2%)
  other arithmetic  0.56 us (1%)
    all_to_all x1, blocking collectives, local(): back = lax.all_to_all(out, ('grp', 'shard'), 0, 0, tiled=True)  10.9 us
    pallas_call x1, Pallas kernels, local(): pl.pallas_call(project_kernel, out_shape=[store, store], in_specs=[hbm()]...  5.47 us
    pallas_call x1, Pallas kernels, local(): pl.pallas_call(functools.partial(near_kernel, len(group), 2 * per_shard +...  5.41 us
    ppermute x2, starting transfers between devices, local(): remote = {d: lax.ppermute(share, 'shard', from_ahead(d)) for d in offsets}  5.11 us
    ppermute x3, starting transfers between devices, local(): lax.ppermute(ids, 'grp', [((g + k) % lines, g) for g in range(lines)])  4.5 us
    pallas_call x1, Pallas kernels, local(): pl.pallas_call(functools.partial(far_kernel, held, sum(held[:number]), sc...  4.08 us
    pallas_call x1, Pallas kernels, local(): pl.pallas_call(functools.partial(chip_kernel, score_scale), out_shape=[sc...  3.24 us
    pallas_call x1, Pallas kernels, local(): pl.pallas_call(functools.partial(prepare_kernel, sizes), out_shape=(jax.S...  1.67 us
  transfers between devices with their start and end apart: 8, of which 1 were waited for; matrix products, arithmetic and copies ran while one was open for 0% of the time, Pallas kernels for 39%

profile of v8, /device:TPU:0, one launch (start us, length us, event | category | flops | bytes accessed | tf_op | source)
XLA Modules:
  0.0 45.7 jit_solution(3005540235529591644)
XLA Ops:
  0.0 0.5 collective-permute-start.3
  0.5 1.0 %share.1._ = bf16[4,64,768]{2,1,0:T(8,128)(2,1)S(1)} custom-call(bf16[16,64,768]{2,1,0:T(8,128)(2,1)} %own.1), custom_call_target="tpu_custom_call" | custom-call | tf_op jit(solution)/shard_map/share/pallas_call | solution.py:378
  1.5 2.6 %collective-permute-start.7 = (bf16[4,64,768]{2,1,0:T(8,128)(2,1)S(1)}, bf16[4,64,768]{2,1,0:T(8,128)(2,1)S(1)}, u32[]{:S(2)}, u32[]{:S(2)}) collective-permute-start(bf16[4,64,768]{2,1,0:T(8,128)(2,1)S(1)} %share.1._), channel_id=1, source_target_pairs={{2,0},{3,1},{6,4},{7,5},{0,2},{1,3},{4,6},{5,7},{10,8},{11,9},{14,... | collective-permute-start | bytes 1179656 | tf_op jit(solution)/shard_map/ppermute | solution.py:387
  4.1 2.5 %collective-permute-start.6 = (bf16[4,64,768]{2,1,0:T(8,128)(2,1)S(1)}, bf16[4,64,768]{2,1,0:T(8,128)(2,1)S(1)}, u32[]{:S(2)}, u32[]{:S(2)}) collective-permute-start(bf16[4,64,768]{2,1,0:T(8,128)(2,1)S(1)} %share.1._), channel_id=1, source_target_pairs={{4,0},{5,1},{2,4},{3,5},{6,2},{7,3},{0,6},{1,7},{12,8},{13,9},{10,... | collective-permute-start | bytes 1179656 | tf_op jit(solution)/shard_map/ppermute | solution.py:387
  7.2 1.7 %prepare.1 = (s32[1,64]{1,0:T(1,128)S(1)}, s32[2,128]{1,0:T(2,128)S(1)}, bf16[768,768]{1,0:T(8,128)(2,1)S(1)}, bf16[768,768]{1,0:T(8,128)(2,1)S(1)}) custom-call(s32[2,64]{1,0:T(2,128)} %bitcast.5, s32[1]{0:T(128)S(6)} %copy.18.counts, bf16[768,768]{1,0:T(8,128)(2,1)} %w_cell.1, bf16[768,768]{1,0:T(8,128)(2,1)} %w_mix.1, bf16[4,64,768]{2,1,0:T(8,128)(2,1)S(1)} %share.1._), custom_call_target="tpu_custom_call" | custom-call | tf_op jit(solution)/shard_map/prepare/pallas_call | solution.py:389
  8.9 1.5 %collective-permute-start.2 = (s32[1,64]{1,0:T(1,128)S(1)}, s32[1,64]{1,0:T(1,128)S(1)}, u32[]{:S(2)}, u32[]{:S(2)}) collective-permute-start(s32[1,64]{1,0:T(1,128)S(1)} %get-tuple-element.21.refs_0_), channel_id=1, source_target_pairs={{24,0},{0,8},{8,16},{16,24},{25,1},{1,9},{9,17},{17,25},{26,2},{2,... | collective-permute-start | bytes 776 | tf_op jit(solution)/shard_map/ppermute | solution.py:404
  10.5 1.5 %collective-permute-start.1 = (s32[1,64]{1,0:T(1,128)S(1)}, s32[1,64]{1,0:T(1,128)S(1)}, u32[]{:S(2)}, u32[]{:S(2)}) collective-permute-start(s32[1,64]{1,0:T(1,128)S(1)} %get-tuple-element.21.refs_0_), channel_id=1, source_target_pairs={{16,0},{24,8},{0,16},{8,24},{17,1},{25,9},{1,17},{9,25},{18,2},{26... | collective-permute-start | bytes 776 | tf_op jit(solution)/shard_map/ppermute | solution.py:404
  12.0 0.0 collective-permute-done.3.partner
  12.0 1.4 %collective-permute-start = (s32[1,64]{1,0:T(1,128)S(1)}, s32[1,64]{1,0:T(1,128)S(1)}, u32[]{:S(2)}, u32[]{:S(2)}) collective-permute-start(s32[1,64]{1,0:T(1,128)S(1)} %get-tuple-element.21.refs_0_), channel_id=1, source_target_pairs={{8,0},{16,8},{24,16},{0,24},{9,1},{17,9},{25,17},{1,25},{10,2},{18... | collective-permute-start | bytes 776 | tf_op jit(solution)/shard_map/ppermute | solution.py:404
  13.4 5.5 %project.1 = (bf16[40,64,768]{2,1,0:T(8,128)(2,1)S(1)}, bf16[40,64,768]{2,1,0:T(8,128)(2,1)S(1)}) custom-call(bf16[16,64,768]{2,1,0:T(8,128)(2,1)} %own.1, bf16[16,64,768]{2,1,0:T(8,128)(2,1)S(1)} %collective-permute-done.3.partner, bf16[768,768]{1,0:T(8,128)(2,1)S(1)} %get-tuple-element.22.w_cell.refs_4_, bf16[768,768]{1,0:T(8,128)(2,1)S(1)} %get-tuple-element.23.w_mix.refs_5_), custom_call_target="tpu_custom_call" | custom-call | tf_op jit(solution)/shard_map/project/pallas_call | solution.py:422
  18.9 0.0 collective-permute-done.2.refs_3_
  18.9 0.0 collective-permute-done.1.refs_2_
  18.9 0.0 collective-permute-done.refs_1_
  18.9 0.9 %route.1 = (s32[4,128]{1,0:T(4,128)S(1)}, s32[4,128]{1,0:T(4,128)S(1)}, s32[2,128]{1,0:T(2,128)S(1)}) custom-call(s32[1,64]{1,0:T(1,128)S(1)} %get-tuple-element.21.refs_0_, s32[1,64]{1,0:T(1,128)S(1)} %collective-permute-done.refs_1_, s32[1,64]{1,0:T(1,128)S(1)} %collective-permute-done.1.refs_2_, s32[1,64]{1,0:T(1,128)S(1)} %collective-permute-done.2.refs_3_, ...), custom_call_target="tpu_custom_call" | custom-call | tf_op jit(solution)/shard_map/route/pallas_call | solution.py:439
  19.8 0.1 collective-permute-start.4
  19.9 0.4 collective-permute-start.5
  20.3 3.2 %chip.1 = (f32[32,64]{1,0:T(8,128)S(1)}, bf16[768,768]{1,0:T(8,128)(2,1)S(1)}) custom-call(s32[2,128]{1,0:T(2,128)S(1)} %get-tuple-element.31.index, bf16[40,64,768]{2,1,0:T(8,128)(2,1)S(1)} %get-tuple-element.24.refs_4_.refs_6_.proj, bf16[40,64,768]{2,1,0:T(8,128)(2,1)S(1)} %get-tuple-element.28.refs_7_.mixed, bf16[768,768]{1,0:T(8,128)(2,1)} %w_pool.1, ...), custom_call_target="tpu_custom_call" | custom-call | tf_op jit(solution)/shard_map/chip/pallas_call | solution.py:456
  23.5 0.0 collective-permute-done.7.refs_3_
  23.5 1.2 %collective-permute-done.6.refs_2_ = bf16[4,64,768]{2,1,0:T(8,128)(2,1)S(1)} collective-permute-done((bf16[4,64,768]{2,1,0:T(8,128)(2,1)S(1)}, bf16[4,64,768]{2,1,0:T(8,128)(2,1)S(1)}, u32[]{:S(2)}, u32[]{:S(2)}) %collective-permute-start.6) | collective-permute-done | bytes 393248 | tf_op jit(solution)/shard_map/ppermute | solution.py:387
  24.8 0.0 collective-permute-done.4.refs_1_
  24.8 5.4 %near1_2.1 = (bf16[40,64,768]{2,1,0:T(8,128)(2,1)S(1)}, bf16[40,64,768]{2,1,0:T(8,128)(2,1)S(1)}, f32[768,896]{1,0:T(8,128)S(1)}, f32[768,768]{1,0:T(8,128)S(1)}) custom-call(s32[4,128]{1,0:T(4,128)S(1)} %get-tuple-element.25.refs_0_, s32[4,128]{1,0:T(4,128)S(1)} %collective-permute-done.4.refs_1_, ...), custom_call_target="tpu_custom_call", output_to_operand_aliasing={{0}: (6, {}), {1}: (7, {})} | custom-call | tf_op jit(solution)/shard_map/near1_2/pallas_call | solution.py:474
  30.2 0.0 collective-permute-done.5.refs_2_
  30.2 4.1 %far1_2.1 = (f32[32,64]{1,0:T(8,128)S(1)}, f32[768,896]{1,0:T(8,128)S(1)}, f32[768,768]{1,0:T(8,128)S(1)}) custom-call(s32[4,128]{1,0:T(4,128)S(1)} %get-tuple-element.25.refs_0_, s32[4,128]{1,0:T(4,128)S(1)} %collective-permute-done.4.refs_1_, ...), custom_call_target="tpu_custom_call", output_to_operand_aliasing={{0}: (6, {}), {1}: (7, {}), {2}: (8, {})} | custom-call | tf_op jit(solution)/shard_map/far1_2/pallas_call | solution.py:494
  34.3 10.9 %all_to_all.9 = f32[32,1,64]{2,1,0:T(1,128)S(1)} all-to-all(f32[32,1,64]{2,1,0:T(1,128)S(1)} %bitcast.4), channel_id=1, replica_groups=mesh['grp'=4,'shard'=8] {'grp','shard'}, dimensions={0} | all-to-all | bytes 16384 | tf_op jit(solution)/shard_map/all_to_all | solution.py:508
  45.2 0.6 %reduce_sum.9 = f32[64]{0:T(128)} reduce(f32[32,1,64]{2,1,0:T(1,128)S(1)} %all_to_all.9, f32[]{:T(128)} %constant.0.clone.1), dimensions={0,1}, to_apply=%region_0.0 | reduce | flops 1984 | bytes 8452 | tf_op jit(solution)/shard_map/reduce_sum | solution.py:509
Async XLA Ops:
  0.0 12.0 %collective-permute-start.3 = (bf16[16,64,768]{2,1,0:T(8,128)(2,1)}, bf16[16,64,768]{2,1,0:T(8,128)(2,1)S(1)}, u32[]{:S(2)}, u32[]{:S(2)}) collective-permute-start(bf16[16,64,768]{2,1,0:T(8,128)(2,1)} %own.1), channel_id=1, source_target_pairs={{0,1},{1,0},{2,3},{3,2},{4,5},{5,4},{6,7},{7,6},{8,9},{9,8},{10,11... | collective-permute-start | bytes 4718600 | tf_op jit(solution)/shard_map/ppermute | solution.py:388
  1.5 22.1 %collective-permute-start.7 = (bf16[4,64,768]{2,1,0:T(8,128)(2,1)S(1)}, bf16[4,64,768]{2,1,0:T(8,128)(2,1)S(1)}, u32[]{:S(2)}, u32[]{:S(2)}) collective-permute-start(bf16[4,64,768]{2,1,0:T(8,128)(2,1)S(1)} %share.1._), channel_id=1, source_target_pairs={{2,0},{3,1},{6,4},{7,5},{0,2},{1,3},{4,6},{5,7},{10,8},{11,9},{14,... | collective-permute-start | bytes 1179656 | tf_op jit(solution)/shard_map/ppermute | solution.py:387
  4.1 20.7 %collective-permute-start.6 = (bf16[4,64,768]{2,1,0:T(8,128)(2,1)S(1)}, bf16[4,64,768]{2,1,0:T(8,128)(2,1)S(1)}, u32[]{:S(2)}, u32[]{:S(2)}) collective-permute-start(bf16[4,64,768]{2,1,0:T(8,128)(2,1)S(1)} %share.1._), channel_id=1, source_target_pairs={{4,0},{5,1},{2,4},{3,5},{6,2},{7,3},{0,6},{1,7},{12,8},{13,9},{10,... | collective-permute-start | bytes 1179656 | tf_op jit(solution)/shard_map/ppermute | solution.py:387
  8.9 10.0 %collective-permute-start.2 = (s32[1,64]{1,0:T(1,128)S(1)}, s32[1,64]{1,0:T(1,128)S(1)}, u32[]{:S(2)}, u32[]{:S(2)}) collective-permute-start(s32[1,64]{1,0:T(1,128)S(1)} %get-tuple-element.21.refs_0_), channel_id=1, source_target_pairs={{24,0},{0,8},{8,16},{16,24},{25,1},{1,9},{9,17},{17,25},{26,2},{2,... | collective-permute-start | bytes 776 | tf_op jit(solution)/shard_map/ppermute | solution.py:404
  10.5 8.4 %collective-permute-start.1 = (s32[1,64]{1,0:T(1,128)S(1)}, s32[1,64]{1,0:T(1,128)S(1)}, u32[]{:S(2)}, u32[]{:S(2)}) collective-permute-start(s32[1,64]{1,0:T(1,128)S(1)} %get-tuple-element.21.refs_0_), channel_id=1, source_target_pairs={{16,0},{24,8},{0,16},{8,24},{17,1},{25,9},{1,17},{9,25},{18,2},{26... | collective-permute-start | bytes 776 | tf_op jit(solution)/shard_map/ppermute | solution.py:404
  12.0 6.9 %collective-permute-start = (s32[1,64]{1,0:T(1,128)S(1)}, s32[1,64]{1,0:T(1,128)S(1)}, u32[]{:S(2)}, u32[]{:S(2)}) collective-permute-start(s32[1,64]{1,0:T(1,128)S(1)} %get-tuple-element.21.refs_0_), channel_id=1, source_target_pairs={{8,0},{16,8},{24,16},{0,24},{9,1},{17,9},{25,17},{1,25},{10,2},{18... | collective-permute-start | bytes 776 | tf_op jit(solution)/shard_map/ppermute | solution.py:404
  19.8 5.0 %collective-permute-start.4 = (s32[4,128]{1,0:T(4,128)S(1)}, s32[4,128]{1,0:T(4,128)S(1)}, u32[]{:S(2)}, u32[]{:S(2)}) collective-permute-start(s32[4,128]{1,0:T(4,128)S(1)} %get-tuple-element.26), channel_id=1, source_target_pairs={{0,1},{1,0},{2,3},{3,2},{4,5},{5,4},{6,7},{7,6},{8,9},{9,8},{10,11... | collective-permute-start | bytes 6152 | tf_op jit(solution)/shard_map/ppermute | solution.py:451
  19.9 10.3 %collective-permute-start.5 = (s32[2,128]{1,0:T(2,128)S(1)}, s32[2,128]{1,0:T(2,128)S(1)}, u32[]{:S(2)}, u32[]{:S(2)}) collective-permute-start(s32[2,128]{1,0:T(2,128)S(1)} %get-tuple-element.27._), channel_id=1, source_target_pairs={{4,0},{5,1},{2,4},{3,5},{6,2},{7,3},{0,6},{1,7},{12,8},{13,9},{10,... | collective-permute-start | bytes 3080 | tf_op jit(solution)/shard_map/ppermute | solution.py:453
